TPU v7x, 512 devices: a whole 4x8x8 slice. The times are simulated.
512 devices in a mesh: seq: 32 (over y, x), mp: 16 (over z, core).
Axes of the slice: x: 4, y: 8, z: 8, core: 2. Of those that a mesh axis runs over, the one named last changes fastest.
Arguments:
- frames: bfloat16 [16384, 1024], P('seq', 'mp'), may hold values from -40 to 40
- cotangent: bfloat16 [16384, 1024], P('seq', 'mp'), may hold values from -6 to 6
- query_weight: bfloat16 [1024, 1024], P('mp'), may hold values from -2 to 2
- key_weight: bfloat16 [1024, 1024], P('mp'), may hold values from -2 to 2
- value_weight: bfloat16 [1024, 1024], P('mp'), may hold values from -0.1875 to 0.1875
- out_weight: bfloat16 [1024, 1024], P('mp'), may hold values from -0.1875 to 0.1875
- turn_blocks: int32 [32, 32, 2], replicated, may hold values from -1 to 127, as said below
Outputs:
- attended: bfloat16 [16384, 1024], P('seq', 'mp')
- grad_frames: bfloat16 [16384, 1024], P('seq', 'mp')
- grad_query: float32 [1024, 1024], P('mp')
- grad_key: float32 [1024, 1024], P('mp')
- grad_value: float32 [1024, 1024], P('mp')
- grad_out: float32 [1024, 1024], P('mp')
Inputs may be any that keep to these rules, and one draw needn't show every extreme that they name: turn_blocks[d, e, c] is -1 or a block of device d (blocks d * 4 to (d + 1) * 4 - 1); slot c of devices d and e joins block turn_blocks[d, e, c] with block turn_blocks[e, d, c], and the two are -1 together; used slots come before unused ones, the blocks of one (d, e) differ, d = e is all -1; some pair of devices uses all 2 slots.
All inputs are finite; a program needn't handle non-finite values.
Results may differ from a plain program's by a relative error of at most 0.025.
The roundings to bfloat16 on the way count: a program that leaves them out, or rounds other values in their place, can miss the bound.
Values may be sent and summed in bfloat16 or wider, within the bound.
A program may use at most 128 MiB of HBM per device.

v0:
```python
import math

import jax
import jax.numpy as jnp
from jax import lax
from jax.sharding import PartitionSpec as P

D = 1024
HEADS = 16
BLK = 128
BAND = 2


def extended_2(cells, sides, width):
    for axis, dim in sides:
        count = lax.axis_size(axis)
        ends = count - 1
        head = lax.slice_in_dim(cells, 0, width, axis=dim)
        tail = lax.slice_in_dim(cells, cells.shape[dim] - width, cells.shape[dim], axis=dim)
        cells = jnp.concatenate(
            [
                lax.ppermute(tail, axis, [(i, (i + 1) % count) for i in range(ends)]),
                cells,
                lax.ppermute(head, axis, [((i + 1) % count, i) for i in range(ends)]),
            ],
            axis=dim,
        )
    return cells


def passed_along(array, axis, by):
    count = lax.axis_size(axis)
    pairs = [(i, i + by) for i in range(count) if 0 <= i + by < count]
    return lax.ppermute(array, axis, pairs)


def heads_view(tensor, head_count):
    return tensor.reshape(tensor.shape[:-1] + (head_count, tensor.shape[-1] // head_count))


def gather_rows(select, values):
    return jnp.einsum("pj,p...->j...", select, values, precision=lax.Precision.HIGHEST)


def tile_grads(probability, slopes, query_rows, grad_rows, score_scale):
    key_part = (
        jnp.einsum("phqk,pqhe->pkhe", slopes, query_rows, preferred_element_type=jnp.float32)
        * score_scale
    )
    value_part = jnp.einsum(
        "phqk,pqhe->pkhe",
        probability.astype(jnp.bfloat16),
        grad_rows,
        preferred_element_type=jnp.float32,
    )
    flat_shape = key_part.shape[:2] + (-1,)
    return jnp.concatenate([key_part.reshape(flat_shape), value_part.reshape(flat_shape)], axis=-1)


def on_device(frames, cotangent, query_weight, key_weight, value_weight, out_weight, turn_blocks):
    highest = lax.Precision.HIGHEST
    row_count = frames.shape[0]
    col_count = query_weight.shape[0]
    head_size = D // HEADS
    head_count = col_count // head_size
    score_scale = 1.0 / math.sqrt(head_size)
    block_count = row_count // BLK
    window = 2 * BAND + 1
    peer_count = lax.axis_size("seq")
    capacity = turn_blocks.shape[2]
    device = lax.axis_index("seq")
    first_block = device * block_count
    whole_frames = lax.all_gather(frames, "mp", axis=1, tiled=True)
    joint_weight = jnp.concatenate([query_weight, key_weight, value_weight], axis=0)
    projected = lax.dot_general(
        whole_frames, joint_weight, (((1,), (1,)), ((), ())), preferred_element_type=jnp.float32
    ).astype(jnp.bfloat16)
    query_rows = projected[:, :col_count]
    keyval = projected[:, col_count:]
    own_list = lax.dynamic_index_in_dim(turn_blocks, device, 0, keepdims=False)
    their_list = lax.dynamic_index_in_dim(turn_blocks, device, 1, keepdims=False)
    slot_used = own_list >= 0
    far_valid = slot_used & (jnp.abs(own_list - their_list) > BAND)
    select = (
        ((own_list - first_block)[:, :, None] == jnp.arange(block_count)[None, None, :])
        & slot_used[:, :, None]
    ).astype(jnp.float32)
    select_flat = select.reshape(peer_count * capacity, block_count).astype(jnp.bfloat16)
    keyval_rows = keyval.reshape(block_count, BLK * 2 * col_count)
    outgoing = jnp.dot(select_flat, keyval_rows, preferred_element_type=jnp.float32).astype(
        jnp.bfloat16
    )
    outgoing = outgoing.reshape(peer_count, capacity, BLK * 2 * col_count)
    incoming = lax.all_to_all(outgoing, "seq", split_axis=0, concat_axis=0, tiled=True).reshape(
        peer_count, capacity, BLK, 2 * col_count
    )
    query_slots = jnp.dot(
        select_flat,
        query_rows.reshape(block_count, BLK * col_count),
        preferred_element_type=jnp.float32,
    ).astype(jnp.bfloat16)
    query_slots = heads_view(query_slots.reshape(peer_count, capacity, BLK, col_count), head_count)
    extended = extended_2(keyval, (("seq", 0),), BAND * BLK)
    ext_blocks = extended.reshape(block_count + 2 * BAND, BLK, 2 * col_count)
    windows = jnp.stack(
        [ext_blocks[offset : offset + block_count] for offset in range(window)], axis=1
    )
    windows = windows.reshape(block_count, window * BLK, 2 * col_count)
    key_window = heads_view(windows[..., :col_count], head_count)
    value_window = heads_view(windows[..., col_count:], head_count)
    placed = first_block + jnp.arange(block_count)[:, None] + jnp.arange(window)[None, :] - BAND
    band_valid = jnp.repeat((placed >= 0) & (placed < block_count * peer_count), BLK, axis=1)
    query_heads = heads_view(query_rows.reshape(block_count, BLK, col_count), head_count)
    band_scores = (
        jnp.einsum("jqhe,jkhe->jhqk", query_heads, key_window, preferred_element_type=jnp.float32)
        * score_scale
    )
    band_scores = jnp.where(band_valid[:, None, None, :], band_scores, -jnp.inf)
    row_top = jnp.max(band_scores, axis=-1)
    far_scores = []
    for column in range(capacity):
        key_far = heads_view(incoming[:, column, :, :col_count], head_count)
        scores = (
            jnp.einsum(
                "pqhe,pkhe->phqk",
                query_slots[:, column],
                key_far,
                preferred_element_type=jnp.float32,
            )
            * score_scale
        )
        scores = jnp.where(far_valid[:, column, None, None, None], scores, -jnp.inf)
        masked = jnp.where(
            select[:, column, :, None, None] > 0, jnp.max(scores, axis=-1)[:, None], -jnp.inf
        )
        row_top = jnp.maximum(row_top, jnp.max(masked, axis=0))
        far_scores.append(scores)
    slot_top = jnp.einsum("pcj,jhq->pchq", select, row_top, precision=highest)
    band_weight = jnp.exp(band_scores - row_top[..., None])
    row_total = jnp.sum(band_weight, axis=-1)
    row_sum = jnp.einsum(
        "jhqk,jkhe->jqhe",
        band_weight.astype(jnp.bfloat16),
        value_window,
        preferred_element_type=jnp.float32,
    )
    far_weight = []
    for column in range(capacity):
        weight_now = jnp.exp(far_scores[column] - slot_top[:, column][..., None])
        far_weight.append(weight_now)
        row_total = row_total + gather_rows(select[:, column], jnp.sum(weight_now, axis=-1))
        value_far = heads_view(incoming[:, column, :, col_count:], head_count)
        part_sum = jnp.einsum(
            "phqk,pkhe->pqhe",
            weight_now.astype(jnp.bfloat16),
            value_far,
            preferred_element_type=jnp.float32,
        )
        row_sum = row_sum + gather_rows(select[:, column], part_sum)
    attended_heads = row_sum / jnp.transpose(row_total, (0, 2, 1))[..., None]
    context = attended_heads.reshape(row_count, col_count).astype(jnp.bfloat16)
    partial_out = jnp.dot(context, out_weight, preferred_element_type=jnp.float32)
    attended = lax.psum_scatter(
        partial_out.astype(jnp.bfloat16), "mp", scatter_dimension=1, tiled=True
    )
    grad_whole = lax.all_gather(cotangent, "mp", axis=1, tiled=True)
    context_grad = lax.dot_general(
        grad_whole, out_weight, (((1,), (1,)), ((), ())), preferred_element_type=jnp.float32
    ).astype(jnp.bfloat16)
    out_grad = lax.dot_general(
        context, grad_whole, (((0,), (0,)), ((), ())), preferred_element_type=jnp.float32
    )
    grad_heads = heads_view(context_grad.reshape(block_count, BLK, col_count), head_count)
    row_drift = jnp.transpose(
        jnp.sum(grad_heads.astype(jnp.float32) * attended_heads, axis=-1), (0, 2, 1)
    )
    band_prob = band_weight / row_total[..., None]
    band_dot = jnp.einsum(
        "jqhe,jkhe->jhqk", grad_heads, value_window, preferred_element_type=jnp.float32
    )
    band_slope = (band_prob * (band_dot - row_drift[..., None])).astype(jnp.bfloat16)
    query_grad = jnp.einsum(
        "jhqk,jkhe->jqhe", band_slope, key_window, preferred_element_type=jnp.float32
    )
    key_window_grad = (
        jnp.einsum("jhqk,jqhe->jkhe", band_slope, query_heads, preferred_element_type=jnp.float32)
        * score_scale
    )
    value_window_grad = jnp.einsum(
        "jhqk,jqhe->jkhe",
        band_prob.astype(jnp.bfloat16),
        grad_heads,
        preferred_element_type=jnp.float32,
    )
    slot_total = jnp.where(
        slot_used[:, :, None, None],
        jnp.einsum("pcj,jhq->pchq", select, row_total, precision=highest),
        1.0,
    )
    slot_drift = jnp.einsum("pcj,jhq->pchq", select, row_drift, precision=highest)
    grad_slots = jnp.dot(
        select_flat,
        context_grad.reshape(block_count, BLK * col_count),
        preferred_element_type=jnp.float32,
    ).astype(jnp.bfloat16)
    grad_slots = heads_view(grad_slots.reshape(peer_count, capacity, BLK, col_count), head_count)
    far_slopes = []
    for column in range(capacity):
        far_prob = far_weight[column] / slot_total[:, column][..., None]
        value_far = heads_view(incoming[:, column, :, col_count:], head_count)
        key_far = heads_view(incoming[:, column, :, :col_count], head_count)
        far_dot = jnp.einsum(
            "pqhe,pkhe->phqk", grad_slots[:, column], value_far, preferred_element_type=jnp.float32
        )
        slope_now = (far_prob * (far_dot - slot_drift[:, column][..., None])).astype(jnp.bfloat16)
        far_slopes.append((far_prob, slope_now))
        query_part = jnp.einsum(
            "phqk,pkhe->pqhe", slope_now, key_far, preferred_element_type=jnp.float32
        )
        query_grad = query_grad + gather_rows(select[:, column], query_part)
    query_grad = query_grad * score_scale
    returned = []
    for column in range(capacity):
        returned.append(
            tile_grads(
                far_slopes[column][0],
                far_slopes[column][1],
                query_slots[:, column],
                grad_slots[:, column],
                score_scale,
            )
        )
    returned_grads = jnp.stack(returned, axis=1).reshape(peer_count, capacity, BLK * 2 * col_count)
    slot_grads = lax.all_to_all(
        returned_grads.astype(jnp.bfloat16), "seq", split_axis=0, concat_axis=0, tiled=True
    ).astype(returned_grads.dtype)
    block_grads = jnp.einsum("pcj,pcx->jx", select, slot_grads, precision=highest).reshape(
        block_count, BLK, 2 * col_count
    )
    window_grad = jnp.concatenate(
        [
            key_window_grad.reshape(block_count, window, BLK, col_count),
            value_window_grad.reshape(block_count, window, BLK, col_count),
        ],
        axis=-1,
    )
    ext_grad = jnp.zeros((block_count + 2 * BAND, BLK, 2 * col_count), jnp.float32)
    for offset in range(window):
        ext_grad = ext_grad.at[offset : offset + block_count].add(window_grad[:, offset])
    lower_rim = ext_grad[:BAND].reshape(BAND * BLK, 2 * col_count)
    upper_rim = ext_grad[BAND + block_count :].reshape(BAND * BLK, 2 * col_count)
    from_above = passed_along(lower_rim.astype(jnp.bfloat16), "seq", -1).astype(lower_rim.dtype)
    from_below = passed_along(upper_rim.astype(jnp.bfloat16), "seq", 1).astype(upper_rim.dtype)
    keyval_grad = (ext_grad[BAND : BAND + block_count] + block_grads).reshape(
        row_count, 2 * col_count
    )
    keyval_grad = keyval_grad.at[: BAND * BLK].add(from_below)
    keyval_grad = keyval_grad.at[row_count - BAND * BLK :].add(from_above)
    joint_grad = jnp.concatenate(
        [query_grad.reshape(row_count, col_count), keyval_grad], axis=1
    ).astype(jnp.bfloat16)
    partial_in = jnp.dot(joint_grad, joint_weight, preferred_element_type=jnp.float32)
    grad_frames = lax.psum_scatter(
        partial_in.astype(jnp.bfloat16), "mp", scatter_dimension=1, tiled=True
    )
    weight_grad = lax.dot_general(
        joint_grad, whole_frames, (((0,), (0,)), ((), ())), preferred_element_type=jnp.float32
    )
    summed = (
        lax.psum(weight_grad.astype(jnp.bfloat16), "seq").astype(jnp.float32),
        lax.psum(out_grad.astype(jnp.bfloat16), "seq").astype(jnp.float32),
    )
    return (
        attended,
        grad_frames,
        summed[0][:col_count],
        summed[0][col_count : 2 * col_count],
        summed[0][2 * col_count :],
        summed[1],
    )


def solution(mesh):
    return jax.shard_map(
        on_device,
        mesh=mesh,
        in_specs=(
            P("seq", "mp"),
            P("seq", "mp"),
            P("mp", None),
            P("mp", None),
            P("mp", None),
            P("mp", None),
            P(),
        ),
        out_specs=(
            P("seq", "mp"),
            P("seq", "mp"),
            P("mp", None),
            P("mp", None),
            P("mp", None),
            P("mp", None),
        ),
        check_vma=False,
    )
```

profile of v0, /device:TPU:1, one launch (start us, length us, event | category | flops | bytes accessed | tf_op | source)
XLA Modules:
  0.0 516.3 jit_solution(8312121588391336749)
XLA Ops:
  12.5 45.5 %all-gather.3.cloned.1.call-done = bf16[512,1024]{0,1:T(8,128)(2,1)} async-done(((bf16[512,64]{0,1:T(8,128)(2,1)}), bf16[512,1024]{0,1:T(8,128)(2,1)}) %all-gather.3.cloned.1.call-update) | async-done | bytes 1048592 | tf_op jit(solution)/shard_map/all_gather | solution.py:73
  58.0 1.6 fusion.17
  60.6 2.7 reshape.638
  63.3 9.5 %all-to-all-start = ((bf16[32,2,16384]{2,1,0:T(2,128)(2,1)}), bf16[32,2,16384]{2,1,0:T(2,128)(2,1)}, u32[]{:S(2)}, u32[]{:S(2)}) async-start(bf16[32,2,16384]{2,1,0:T(2,128)(2,1)} %reshape.638), calls=%async_computation | async-start | bytes 4194304 | tf_op jit(solution)/shard_map/all_to_all | solution.py:94
  75.0 1.3 collective-permute-start.1
  76.3 4.0 collective-permute-start
  81.3 35.0 %all-gather.5.cloned.1.call-done = bf16[512,1024]{0,1:T(8,128)(2,1)} async-done(((bf16[512,64]{0,1:T(8,128)(2,1)}), bf16[512,1024]{0,1:T(8,128)(2,1)}) %all-gather.5.cloned.1.call-update) | async-done | bytes 1048592 | tf_op jit(solution)/shard_map/all_gather | solution.py:166
  116.3 1.5 convolution_convert_fusion.10
  119.7 3.2 reshape_reshape.8
  123.0 3.2 reshape_reshape.9
  128.3 3.5 reshape.674
  131.8 2.2 fusion.3
  140.0 1.0 fusion.40
  142.2 1.4 fusion.70
  145.3 1.2 multiply_convert_fusion
  147.5 1.0 pad_maximum_fusion.2
  148.5 2.3 copy.226
  150.8 2.3 stack.34
  153.2 2.9 fusion.10
  156.3 1.2 multiply_convert_fusion.1
  159.0 1.1 pad_maximum_fusion.1
  160.0 2.3 copy.223
  162.3 2.3 stack.33
  164.6 1.7 pad_maximum_fusion
  166.3 3.5 copy.227
  169.8 9.5 %all-to-all-start.1 = ((bf16[32,2,16384]{2,1,0:T(2,128)(2,1)}), bf16[32,2,16384]{2,1,0:T(2,128)(2,1)}, u32[]{:S(2)}, u32[]{:S(2)}) async-start(bf16[32,2,16384]{2,1,0:T(2,128)(2,1)} %copy.227), calls=%async_computation.2 | async-start | bytes 4194304 | tf_op jit(solution)/shard_map/all_to_all | solution.py:234
  179.4 1.5 copy.200
  181.0 1.9 fusion.6
  183.7 1.1 fusion.9
  184.8 2.2 reshape.654
  187.0 2.2 convolution_bitcast_fusion.4
  189.2 2.3 reshape.655
  191.5 1.2 copy-done.14
  192.8 1.2 fusion.122
  194.5 3.1 collective-permute-start.2
  197.7 1.7 collective-permute-start.3
  199.4 1.7 convolution_bitcast_fusion
  204.3 1.1 convolution_convert_fusion.9
  205.4 22.3 %all-to-all-done.1 = bf16[32,2,16384]{2,1,0:T(2,128)(2,1)} async-done(((bf16[32,2,16384]{2,1,0:T(2,128)(2,1)}), bf16[32,2,16384]{2,1,0:T(2,128)(2,1)}, u32[]{:S(2)}, u32[]{:S(2)}) %all-to-all-start.1) | async-done | bytes 2097184 | tf_op jit(solution)/shard_map/all_to_all | solution.py:234
  227.7 2.8 fusion.14
  231.8 1.4 convolution_convert_fusion.7
  233.3 1.5 convolution_convert_fusion.4
  234.8 1.6 convolution_convert_fusion.3
  236.4 148.1 %all-reduce.4.cloned.1.call-done = (bf16[192,1024]{1,0:T(8,128)(2,1)}, bf16[64,1024]{1,0:T(8,128)(2,1)}) async-done(((bf16[192,1024]{1,0:T(8,128)(2,1)}, bf16[64,1024]{1,0:T(8,128)(2,1)}), (bf16[192,1024]{1,0:T(8,128)(2,1)}, bf16[64,1024]{1,0:T(8,128)(2,1)})) %all-reduce.4.cloned.1.call-update) | async-done | bytes 524304 | tf_op jit(solution)/shard_map/psum | solution.py:270
  384.5 1.6 convert_element_type.149
  386.1 1.9 fusion.123
  388.0 59.8 %reduce-scatter.3.cloned.1.call-done = bf16[512,64]{0,1:T(8,128)(2,1)} async-done(((bf16[512,1024]{0,1:T(8,128)(2,1)}), bf16[512,64]{0,1:T(8,128)(2,1)}) %reduce-scatter.3.cloned.1.call-update) | async-done | bytes 65552 | tf_op jit(solution)/shard_map/reduce_scatter | solution.py:163
  447.8 61.9 %reduce-scatter.5.cloned.1.call-done = bf16[512,64]{0,1:T(8,128)(2,1)} async-done(((bf16[512,1024]{0,1:T(8,128)(2,1)}), bf16[512,64]{0,1:T(8,128)(2,1)}) %reduce-scatter.5.cloned.1.call-update) | async-done | bytes 65552 | tf_op jit(solution)/shard_map/reduce_scatter | solution.py:263
  (197 shorter events, 30.4 us)
Async XLA Ops:
  7.2 109.1 %copy-start = (bf16[64,1024]{1,0:T(8,128)(2,1)S(1)}, bf16[64,1024]{1,0:T(8,128)(2,1)}, u32[]{:S(2)}) copy-start(bf16[64,1024]{1,0:T(8,128)(2,1)} %param.26) | copy-start | bytes 393220
  7.2 50.8 %all-gather.3.cloned.1.call-start = ((), (), s32[]{:S(2)}) async-start(), calls=%async_computation.4 | async-start | bytes 1114112 | tf_op jit(solution)/shard_map/all_gather | solution.py:73
  12.5 47.3 %copy-start.17 = (bf16[192,1024]{1,0:T(8,128)(2,1)}, bf16[192,1024]{1,0:T(8,128)(2,1)S(1)}, u32[]{:S(2)}) copy-start(bf16[192,1024]{1,0:T(8,128)(2,1)S(1)} %constant_dynamic-update-slice_fusion) | copy-start | bytes 1179652
  63.3 10.5 %copy-start.29 = (s32[32,32,2]{1,2,0:T(2,128)S(1)}, s32[32,32,2]{1,2,0:T(2,128)}, u32[]{:S(2)}) copy-start(s32[32,32,2]{1,2,0:T(2,128)} %param.27) | copy-start | bytes 24580
  63.3 65.0 %all-to-all-start = ((bf16[32,2,16384]{2,1,0:T(2,128)(2,1)}), bf16[32,2,16384]{2,1,0:T(2,128)(2,1)}, u32[]{:S(2)}, u32[]{:S(2)}) async-start(bf16[32,2,16384]{2,1,0:T(2,128)(2,1)} %reshape.638), calls=%async_computation | async-start | bytes 4194304 | tf_op jit(solution)/shard_map/all_to_all | solution.py:94
  72.8 43.5 %all-gather.5.cloned.1.call-start = ((), (), s32[]{:S(2)}) async-start(), calls=%async_computation.6 | async-start | bytes 1114112 | tf_op jit(solution)/shard_map/all_gather | solution.py:166
  73.9 43.9 %copy-start.45 = (pred[32,2]{0,1:T(4,128)(4,1)}, pred[32,2]{0,1:T(4,128)(4,1)S(1)}, u32[]{:S(2)}) copy-start(pred[32,2]{0,1:T(4,128)(4,1)S(1)} %get-tuple-element.122) | copy-start | bytes 196
  74.5 59.6 %copy-start.38 = (pred[32]{0:T(512)(128)(4,1)}, pred[32]{0:T(512)(128)(4,1)S(1)}, u32[]{:S(2)}) copy-start(pred[32]{0:T(512)(128)(4,1)S(1)} %get-tuple-element.126) | copy-start | bytes 100
  74.5 60.7 %copy-start.26 = (pred[32,2,4]{0,2,1:T(4,128)(4,1)}, pred[32,2,4]{0,2,1:T(4,128)(4,1)S(1)}, u32[]{:S(2)}) copy-start(pred[32,2,4]{0,2,1:T(4,128)(4,1)S(1)} %get-tuple-element.95) | copy-start | bytes 772
  75.0 51.2 %collective-permute-start.1 = (bf16[256,128]{0,1:T(8,128)(2,1)S(1)}, bf16[256,128]{0,1:T(8,128)(2,1)S(1)}, u32[]{:S(2)}, u32[]{:S(2)}) collective-permute-start(bf16[256,128]{0,1:T(8,128)(2,1)S(1)} %get-tuple-element.108), channel_id=1, source_target_pairs={{16,0},{32,16},{48,32},{64,48},{80,64},{96,80},{112,96},{128,112},... | collective-permute-start | bytes 196616 | tf_op jit(solution)/shard_map/ppermute | solution.py:24
  76.3 49.9 %collective-permute-start = (bf16[256,128]{0,1:T(8,128)(2,1)S(1)}, bf16[256,128]{0,1:T(8,128)(2,1)S(1)}, u32[]{:S(2)}, u32[]{:S(2)}) collective-permute-start(bf16[256,128]{0,1:T(8,128)(2,1)S(1)} %get-tuple-element.109), channel_id=1, source_target_pairs={{0,16},{16,32},{32,48},{48,64},{64,80},{80,96},{96,112},{112,128},... | collective-permute-start | bytes 196616 | tf_op jit(solution)/shard_map/ppermute | solution.py:22
  117.8 5.2 %copy-start.21 = (bf16[512,64]{0,1:T(8,128)(2,1)}, bf16[512,64]{0,1:T(8,128)(2,1)S(1)}, u32[]{:S(2)}) copy-start(bf16[512,64]{0,1:T(8,128)(2,1)S(1)} %convolution_convert_fusion.10) | copy-start | bytes 196612
  126.2 1.6 copy-start.23
  128.3 3.5 copy-start.41
  131.8 2.3 copy-start.1
  135.0 2.5 copy-start.3
  135.2 7.0 %copy-start.30 = (f32[4,128]{1,0:T(4,128)}, f32[4,128]{1,0:T(4,128)S(1)}, u32[]{:S(2)}) copy-start(f32[4,128]{1,0:T(4,128)S(1)} %maximum_maximum_fusion) | copy-start | bytes 6148
  137.5 1.4 copy-start.27
  138.6 2.8 copy-start.46
  138.6 3.6 copy-start.6
  138.6 3.6 copy-start.25
  140.0 4.4 copy-start.19
  141.3 3.1 copy-start.36
  143.6 1.7 copy-start.34
  153.1 3.0 copy-start.4
  153.1 3.2 copy-start.20
  153.1 3.2 copy-start.32
  153.1 3.2 copy-start.33
  153.2 3.2 copy-start.40
  156.3 1.6 copy-start.2
  169.8 11.1 %copy-start.31 = (f32[4,128]{1,0:T(4,128)S(1)}, f32[4,128]{1,0:T(4,128)}, u32[]{:S(2)}) copy-start(f32[4,128]{1,0:T(4,128)} %copy-done.30) | copy-start | bytes 6148
  169.8 11.1 %copy-start.35 = (f32[4,128]{1,0:T(4,128)S(1)}, f32[4,128]{1,0:T(4,128)}, u32[]{:S(2)}) copy-start(f32[4,128]{1,0:T(4,128)} %copy-done.34) | copy-start | bytes 6148
  169.8 11.1 %copy-start.37 = (f32[4,128]{1,0:T(4,128)S(1)}, f32[4,128]{1,0:T(4,128)}, u32[]{:S(2)}) copy-start(f32[4,128]{1,0:T(4,128)} %copy-done.36) | copy-start | bytes 6148
  169.8 57.9 %all-to-all-start.1 = ((bf16[32,2,16384]{2,1,0:T(2,128)(2,1)}), bf16[32,2,16384]{2,1,0:T(2,128)(2,1)}, u32[]{:S(2)}, u32[]{:S(2)}) async-start(bf16[32,2,16384]{2,1,0:T(2,128)(2,1)} %copy.227), calls=%async_computation.2 | async-start | bytes 4194304 | tf_op jit(solution)/shard_map/all_to_all | solution.py:234
  179.4 205.1 %all-reduce.4.cloned.1.call-start = ((), (), s32[]{:S(2)}) async-start(), calls=%async_computation.8 | async-start | bytes 1048576 | tf_op jit(solution)/shard_map/psum | solution.py:270
  181.0 2.7 copy-start.24
  189.2 2.3 copy-start.13
  194.2 6.9 %copy-start.28 = (pred[32,2,4]{0,2,1:T(4,128)(4,1)S(1)}, pred[32,2,4]{0,2,1:T(4,128)(4,1)}, u32[]{:S(2)}) copy-start(pred[32,2,4]{0,2,1:T(4,128)(4,1)} %copy-done.26) | copy-start | bytes 772
  194.5 36.5 %collective-permute-start.2 = (bf16[256,128]{1,0:T(8,128)(2,1)S(1)}, bf16[256,128]{1,0:T(8,128)(2,1)S(1)}, u32[]{:S(2)}, u32[]{:S(2)}) collective-permute-start(bf16[256,128]{1,0:T(8,128)(2,1)S(1)} %bitcast.326), channel_id=1, source_target_pairs={{0,16},{16,32},{32,48},{48,64},{64,80},{80,96},{96,112},{112,128},... | collective-permute-start | bytes 196616 | tf_op jit(solution)/shard_map/ppermute | solution.py:34
  197.7 4.4 copy-start.10
  197.7 33.3 %collective-permute-start.3 = (bf16[256,128]{1,0:T(8,128)(2,1)S(1)}, bf16[256,128]{1,0:T(8,128)(2,1)S(1)}, u32[]{:S(2)}, u32[]{:S(2)}) collective-permute-start(bf16[256,128]{1,0:T(8,128)(2,1)S(1)} %bitcast.327), channel_id=1, source_target_pairs={{16,0},{32,16},{48,32},{64,48},{80,64},{96,80},{112,96},{128,112},... | collective-permute-start | bytes 196616 | tf_op jit(solution)/shard_map/ppermute | solution.py:34
  202.2 1.5 copy-start.7
  202.2 1.5 copy-start.16
  202.6 1.6 copy-start.11
  202.6 1.6 copy-start.22
  231.8 3.0 copy-start.18
  233.2 214.6 %reduce-scatter.3.cloned.1.call-start = ((), (), s32[]{:S(2)}) async-start(), calls=%async_computation.5 | async-start | bytes 1114112 | tf_op jit(solution)/shard_map/reduce_scatter | solution.py:163
  234.8 275.0 %reduce-scatter.5.cloned.1.call-start = ((), (), s32[]{:S(2)}) async-start(), calls=%async_computation.7 | async-start | bytes 1114112 | tf_op jit(solution)/shard_map/reduce_scatter | solution.py:263
  (10 other events, 10.4 us)
Sparse Core Ops, SparseCore 0:
  10.1 47.8 all-gather.2
  75.8 40.4 all-gather.4
  233.3 151.1 all-reduce.3
  388.0 59.8 reduce-scatter.2
  451.0 58.6 reduce-scatter.4
where the time goes:
time: 519 us; the launch traced here: 516 us
  waiting for transfers between devices  374 us (72%)
  local copies, waits for them, and re-layouts  47.8 us (9%)
  matrix products  40.9 us (8%)
  starting transfers between devices  29.3 us (6%)
  between operations  14.8 us (3%)
  other arithmetic  9.43 us (2%)
    psum x1, waiting for transfers between devices, on_device(): lax.psum(weight_grad.astype(jnp.bfloat16), 'seq').astype(jnp.float32)  148 us
    reduce_scatter x1, waiting for transfers between devices, on_device(): lax.psum_scatter(partial_in.astype(jnp.bfloat16), 'mp', scatter_dimension...  61.9 us
    reduce_scatter x1, waiting for transfers between devices, on_device(): lax.psum_scatter(partial_out.astype(jnp.bfloat16), 'mp', scatter_dimensio...  59.8 us
    all_gather x1, waiting for transfers between devices, on_device(): whole_frames = lax.all_gather(frames, 'mp', axis=1, tiled=True)  45.5 us
    all_gather x1, waiting for transfers between devices, on_device(): grad_whole = lax.all_gather(cotangent, 'mp', axis=1, tiled=True)  35 us
    all_to_all x1, waiting for transfers between devices, on_device(): lax.all_to_all(returned_grads.astype(jnp.bfloat16), 'seq', split_axis=0,...  22.3 us
  transfers between devices with their start and end apart: 11, of which 6 were waited for; matrix products, arithmetic and copies ran while one was open for 9% of the time, Pallas kernels for 0%

commit v1 on v0

v1 whole, which is shorter than its diff:
```python
import functools
import math

import jax
import jax.numpy as jnp
from jax import lax
from jax.experimental import pallas as pl
from jax.experimental.pallas import tpu as pltpu
from jax.sharding import PartitionSpec as P

D = 1024
HEADS = 16
BLK = 128
BAND = 2
RING_X = 4
HEAD = D // HEADS
PAIR = 2 * HEAD
UNROLL = 4
SCALE = 1.0 / math.sqrt(HEAD)
EXP2_SCALE = SCALE * math.log2(math.e)
MESH = pl.DeviceIdType.MESH
VMEM = pl.BlockSpec(memory_space=pltpu.VMEM)
SMEM = pl.BlockSpec(memory_space=pltpu.SMEM)
ANY = pl.BlockSpec(memory_space=pl.ANY)
LIMIT = 50 * 1024 * 1024


def wrap(index, count):
    return lax.rem(index + count, count)


def greet(devices):
    barrier = pltpu.get_barrier_semaphore()
    for device in devices:
        pl.semaphore_signal(barrier, inc=1, device_id=device, device_id_type=MESH)
    pl.semaphore_wait(barrier, len(devices))


def remote(source, target, send, recv, device):
    return pltpu.make_async_remote_copy(
        source, target, send, recv, device_id=device, device_id_type=MESH
    )


def take(process, count):
    for _ in range(count):
        next(process, None)


def finish(process):
    for _ in process:
        pass


def fill_weights(refs, whole):
    for index, ref in enumerate(refs):
        whole[index * HEAD : (index + 1) * HEAD] = ref[...]


def places():
    me_mp, me = lax.axis_index("mp"), lax.axis_index("seq")
    chips, count_y = lax.axis_size("mp") // 2, lax.axis_size("seq") // RING_X
    return lax.div(me_mp, 2), lax.rem(me_mp, 2), lax.div(me, RING_X), lax.rem(me, RING_X), chips, count_y


def neighbours(at_y, at_x, count_y):
    return {
        ("x", 1): {"seq": at_y * RING_X + wrap(at_x + 1, RING_X)},
        ("x", -1): {"seq": at_y * RING_X + wrap(at_x - 1, RING_X)},
        ("y", 1): {"seq": wrap(at_y + 1, count_y) * RING_X + at_x},
        ("y", -1): {"seq": wrap(at_y - 1, count_y) * RING_X + at_x},
    }


@functools.cache
def ring_plan(count_y, count_x):
    sizes = {"x": count_x, "y": count_y}
    timed = []

    def ring(kind, axis, at, begin):
        count = sizes[axis]
        for hop in range(1, count // 2 + 1):
            for way in (1, -1):
                far = -way * (hop - 1)
                spot = (far, at) if axis == "x" else (at, far)
                half = None if hop < count // 2 else (0 if way == 1 else 1)
                timed.append((begin + hop - 1, kind, axis, way, spot[0], spot[1], half))

    def steps(count):
        near = [(sign * hop, hop) for hop in range(1, count // 2) for sign in (-1, 1)]
        return [(0, 0)] + near + [(count // 2, count // 2)]

    ring(0, "x", 0, 0)
    ring(1, "y", 0, 0)
    for dx, begin in steps(count_x):
        ring(0, "y", dx, begin)
    for dy, begin in steps(count_y):
        ring(1, "x", dy, begin)
    timed.sort(key=lambda step: step[0])
    plan = []
    for _, kind, axis, way, dx, dy, half in timed:
        plan.append((kind, axis, way, dx % count_x, dy % count_y, half))
    return tuple(plan)


def ring_gather(own, store, local, send, recv):
    _, _, at_y, at_x, _, count_y = places()
    near = neighbours(at_y, at_x, count_y)
    half_rows = store.shape[1] // 2
    plan = ring_plan(count_y, RING_X)

    def part(ref, kind, half):
        if half is None:
            return ref.at[pl.ds(kind * half_rows, half_rows)]
        quarter = half_rows // 2
        return ref.at[pl.ds(kind * half_rows + half * quarter, quarter)]

    def spot(kind, dx, dy, half):
        slot = wrap(at_y + dy, count_y) * RING_X + wrap(at_x + dx, RING_X)
        return part(store.at[slot], kind, half)

    def copy_of(index, source, target):
        _, axis, way, _, _, _ = plan[index]
        return remote(source, target, send.at[index], recv.at[index], near[axis, way])

    def outgoing(index):
        kind, _, _, dx, dy, half = plan[index]
        target = spot(kind, dx, dy, half)
        return copy_of(index, target if dx or dy else part(own, kind, half), target)

    def tile_in(index):
        kind, axis, way, dx, dy, _ = plan[index]
        if axis == "x":
            return kind, (dx - way) % RING_X, dy
        return kind, dx, (dy - way) % count_y

    def incoming(index):
        target = spot(*tile_in(index), plan[index][-1])
        return copy_of(index, target, target)

    arrivals = {}
    for index in range(len(plan)):
        arrivals.setdefault(tile_in(index), []).append(index)
    keep = pltpu.make_async_copy(own, store.at[at_y * RING_X + at_x], local)
    waited = set()
    for index, (kind, _, _, dx, dy, _) in enumerate(plan):
        if dx or dy:
            for before in arrivals[kind, dx, dy]:
                if before not in waited:
                    waited.add(before)
                    incoming(before).wait_recv()
        outgoing(index).start()
        if index == 0:
            keep.start()
        yield
    for index in range(len(plan)):
        if index not in waited:
            incoming(index).wait_recv()
    yield
    for index in range(len(plan)):
        outgoing(index).wait_send()
    keep.wait()


def ring_sems():
    steps = len(ring_plan(lax.axis_size("seq") // RING_X, RING_X))
    return [
        pltpu.SemaphoreType.DMA,
        pltpu.SemaphoreType.DMA((steps,)),
        pltpu.SemaphoreType.DMA((steps,)),
    ]


def sum_over_mp(partial, out_ref, mine, gift, theirs, chip_sum, tiles, done, pair_send, pair_recv, z_send, z_recv, swap_send, swap_recv):
    chip, core, _, _, chips, _ = places()
    sibling = {"mp": 2 * chip + 1 - core}
    half = mine.shape[1]

    def give(step):
        return remote(gift.at[step], theirs.at[step], pair_send.at[step], pair_recv.at[step], sibling)

    def post(step):
        target = {"mp": 2 * lax.rem(chip + step, chips) + core}
        return remote(chip_sum.at[step], tiles.at[step], z_send.at[step - 1], z_recv.at[step - 1], target)

    order = sorted(range(1, chips), key=lambda step: -min(step, chips - step)) + [0]
    for step in order:
        tile = lax.rem(chip + step, chips)
        gift[step] = partial(tile, 1 - core).astype(jnp.bfloat16)
        give(step).start()
        mine[step] = partial(tile, core)
        yield
    for step in order:
        give(step).wait_recv()
        mine[step] += theirs[step].astype(jnp.float32)
        if step:
            chip_sum[step] = mine[step].astype(jnp.bfloat16)
            post(step).start()
        yield
    total = mine[0]
    for step in reversed(order[:-1]):
        post(step).wait_recv()
        total += tiles[step].astype(jnp.float32)
    done[...] = jnp.transpose(total).astype(jnp.bfloat16)
    columns = pl.ds(pl.multiple_of(core * half, half), half)
    other_columns = pl.ds(pl.multiple_of((1 - core) * half, half), half)
    own_rows = pl.ds(pl.multiple_of(core * HEAD, HEAD), HEAD)
    swap = remote(
        done.at[pl.ds(pl.multiple_of((1 - core) * HEAD, HEAD), HEAD)],
        out_ref.at[:, columns],
        swap_send,
        swap_recv,
        sibling,
    )
    swap.start()
    out_ref[:, columns] = done[own_rows]
    yield
    remote(done.at[own_rows], out_ref.at[:, other_columns], swap_send, swap_recv, sibling).wait_recv()
    swap.wait_send()
    for step in order:
        give(step).wait_send()
        if step:
            post(step).wait_send()


def sum_scratch(rows):
    chips = lax.axis_size("mp") // 2
    half = rows // 2
    dma = pltpu.SemaphoreType.DMA
    some = pltpu.VMEM((chips, half, PAIR), jnp.bfloat16)
    return [
        pltpu.VMEM((chips, half, PAIR), jnp.float32),
        some,
        some,
        some,
        some,
        pltpu.VMEM((PAIR, half), jnp.bfloat16),
        dma((chips,)),
        dma((chips,)),
        dma((chips - 1,)),
        dma((chips - 1,)),
        dma,
        dma,
    ]


def mp_partners(chip, core, chips):
    return [{"mp": 2 * chip + 1 - core}] + [
        {"mp": 2 * lax.rem(chip + step, chips) + core} for step in range(1, chips)
    ]


def seq_partners(at_y, at_x, count_y):
    along_x = [{"seq": at_y * RING_X + lax.rem(at_x + step, RING_X)} for step in range(1, RING_X)]
    along_y = [{"seq": lax.rem(at_y + step, count_y) * RING_X + at_x} for step in range(1, count_y)]
    return along_x, along_y


def half_rows_of(ref, half):
    rows = ref.shape[0] // 2
    return ref[pl.ds(pl.multiple_of(half * rows, rows), rows)]


def project_kernel(
    frames_ref,
    grad_ref,
    key_w,
    value_w,
    query_w,
    out_w,
    features,
    own,
    kv_ref,
    weights,
    mine,
    other,
    pair_send,
    pair_recv,
    z_send,
    z_recv,
    share_send,
    share_recv,
    *ring,
):
    chip, core, at_y, at_x, chips, count_y = places()
    hops = chips // 2
    rows = features.shape[0]
    half, width = rows // 2, chips * PAIR
    sibling = {"mp": 2 * chip + 1 - core}
    right = {"mp": 2 * wrap(chip + 1, chips) + core}
    left = {"mp": 2 * wrap(chip - 1, chips) + core}
    greet([sibling, right, left] + list(neighbours(at_y, at_x, count_y).values()))

    mine[:HEAD] = frames_ref[...]
    mine[HEAD:] = grad_ref[...]
    swap = remote(mine, other, pair_send, pair_recv, sibling)
    swap.start()
    fill_weights((key_w, value_w, query_w, out_w), weights)
    swap.wait()
    column = pl.multiple_of(chip * PAIR, PAIR)
    here, there = mine[...].astype(jnp.float32), other[...].astype(jnp.float32)
    even = jnp.where(core == 0, here, there)
    odd = jnp.where(core == 0, there, here)
    for kind in (0, 1):
        side = slice(kind * HEAD, (kind + 1) * HEAD)
        tile = jnp.transpose(jnp.concatenate([even[side], odd[side]], axis=0))
        features[:, pl.ds(kind * width + column, PAIR)] = tile.astype(jnp.bfloat16)

    def place(kind, tile, whose, way, hop):
        start = pl.multiple_of(kind * width + wrap(tile, chips) * PAIR, PAIR)
        count = half if hop < hops else half // 2
        first = whose * half + (0 if hop < hops else way * count)
        return features.at[pl.ds(pl.multiple_of(first, count), count), pl.ds(start, PAIR)]

    def sent(kind, way, hop):
        spot = place(kind, chip + (1 - hop if way == 0 else hop - 1), core, way, hop)
        at = (kind, way, hop - 1)
        return remote(spot, spot, z_send.at[at], z_recv.at[at], right if way == 0 else left)

    def landed(kind, way, hop):
        spot = place(kind, chip + (-hop if way == 0 else hop), core, way, hop)
        at = (kind, way, hop - 1)
        return remote(spot, spot, z_send.at[at], z_recv.at[at], right if way == 0 else left)

    def shared(kind, way, hop, whose):
        spot = place(kind, chip + (-hop if way == 0 else hop), whose, way, hop)
        at = (kind, way, hop - 1)
        return remote(spot, spot, share_send.at[at], share_recv.at[at], sibling)

    def advance(kind, hop):
        for way in (0, 1):
            landed(kind, way, hop).wait_recv()
            if hop < hops:
                sent(kind, way, hop + 1).start()
            shared(kind, way, hop, core).start()

    for kind in (0, 1):
        for way in (0, 1):
            sent(kind, way, 1).start()
    advance(0, 1)
    for hop in range(2, hops + 1):
        advance(0, hop)
        advance(1, hop - 1)
    steps = [(way, hop) for hop in range(1, hops + 1) for way in (0, 1)]
    for way, hop in steps:
        shared(0, way, hop, 1 - core).wait_recv()

    lane = lax.broadcasted_iota(jnp.int32, (BLK, PAIR), 1)
    blocks = [slice(start, start + BLK) for start in range(0, rows, BLK)]
    against = (((1,), (1,)), ((), ()))
    for block in blocks:
        product = lax.dot_general(
            features[block, :width], weights[...], against, preferred_element_type=jnp.float32
        )
        own[block, :PAIR] = product[:, :PAIR].astype(jnp.bfloat16)
        own[block, PAIR:] = product[:, PAIR:].astype(jnp.bfloat16)
    gather = ring_gather(own.at[:, pl.ds(0, PAIR)], kv_ref, *ring)
    take(gather, 8)
    advance(1, hops)
    for way, hop in steps:
        shared(1, way, hop, 1 - core).wait_recv()
    for block in blocks:
        product = lax.dot_general(
            features[block, width:], weights[PAIR:], against, preferred_element_type=jnp.float32
        )
        own[block, PAIR:] = jnp.where(lane < HEAD, own[block, PAIR:], product.astype(jnp.bfloat16))
        take(gather, 4)
    finish(gather)
    for kind in (0, 1):
        for way, hop in steps:
            sent(kind, way, hop).wait_send()
            shared(kind, way, hop, core).wait_send()


def project(frames, cotangent, weights):
    cores, peers = lax.axis_size("mp"), lax.axis_size("seq")
    rows = frames.shape[0]
    dma = pltpu.SemaphoreType.DMA
    sems = dma((2, 2, cores // 4))
    return pl.pallas_call(
        project_kernel,
        out_shape=(
            jax.ShapeDtypeStruct((rows, cores * PAIR), jnp.bfloat16),
            jax.ShapeDtypeStruct((rows, 2 * PAIR), jnp.bfloat16),
            jax.ShapeDtypeStruct((peers, rows, PAIR), jnp.bfloat16),
        ),
        in_specs=[VMEM] * 6,
        out_specs=(VMEM, VMEM, ANY),
        scratch_shapes=[
            pltpu.VMEM((4 * HEAD, D), jnp.bfloat16),
            pltpu.VMEM((PAIR, rows), jnp.bfloat16),
            pltpu.VMEM((PAIR, rows), jnp.bfloat16),
            dma,
            dma,
            sems,
            sems,
            sems,
            sems,
        ]
        + ring_sems(),
        compiler_params=pltpu.CompilerParams(
            collective_id=0, has_side_effects=True, vmem_limit_bytes=LIMIT
        ),
        name="project",
    )(frames.T, cotangent.T, *weights)


def exchange_stats(own_ref, all_ref, x_send, x_recv, y_send, y_recv):
    _, _, at_y, at_x, _, count_y = places()
    along_x, along_y = seq_partners(at_y, at_x, count_y)

    def over_x(step, slot):
        return remote(own_ref, all_ref.at[slot], x_send.at[step], x_recv.at[step], along_x[step])

    def over_y(step, row):
        part = all_ref.at[pl.ds(row * RING_X, RING_X)]
        return remote(part, part, y_send.at[step], y_recv.at[step], along_y[step])

    for step in range(len(along_x)):
        over_x(step, at_y * RING_X + at_x).start()
    all_ref[at_y * RING_X + at_x] = own_ref[...]
    yield
    for step in range(len(along_x)):
        over_x(step, at_y * RING_X + wrap(at_x - step - 1, RING_X)).wait_recv()
    for step in range(len(along_y)):
        over_y(step, at_y).start()
    yield
    for step in range(len(along_y)):
        over_y(step, wrap(at_y - step - 1, count_y)).wait_recv()
    for step in range(len(along_x)):
        over_x(step, at_y * RING_X + at_x).wait_send()
    for step in range(len(along_y)):
        over_y(step, at_y).wait_send()


def share_kernel(
    own,
    stats,
    query_side,
    key_w,
    value_w,
    query_w,
    out_w,
    qg_ref,
    all_stats,
    attended,
    lhs,
    weights,
    local,
    send,
    recv,
    x_send,
    x_recv,
    y_send,
    y_recv,
    *sum_refs,
):
    chip, core, at_y, at_x, chips, count_y = places()
    along_x, along_y = seq_partners(at_y, at_x, count_y)
    greet(along_x + along_y + mp_partners(chip, core, chips))
    table = exchange_stats(stats, all_stats, x_send, x_recv, y_send, y_recv)
    take(table, 1)
    gather = ring_gather(own.at[:, pl.ds(PAIR, PAIR)], qg_ref, local, send, recv)
    take(gather, 8)
    weights[:HEAD] = query_w[...]
    weights[HEAD:] = out_w[...]
    lane = lax.broadcasted_iota(jnp.int32, lhs.shape, 1)
    lhs[...] = jnp.where(lane < HEAD, jnp.zeros_like(lhs[...]), query_side[...])

    def partial(tile, half):
        columns = pl.ds(pl.multiple_of(tile * PAIR, PAIR), PAIR)
        return jnp.dot(half_rows_of(lhs, half), weights[:, columns], preferred_element_type=jnp.float32)

    total = sum_over_mp(partial, attended, *sum_refs)
    take(total, 4)
    take(table, 1)
    for _ in range(2 * chips):
        take(total, 1)
        take(gather, 3)
    finish(gather)
    finish(total)
    finish(table)


def share(own, stats, query_side, weights):
    peers = lax.axis_size("seq")
    rows = own.shape[0]
    dma = pltpu.SemaphoreType.DMA
    x_sems, y_sems = dma((RING_X - 1,)), dma((peers // RING_X - 1,))
    return pl.pallas_call(
        share_kernel,
        out_shape=(
            jax.ShapeDtypeStruct((peers, rows, PAIR), jnp.bfloat16),
            jax.ShapeDtypeStruct((peers,) + stats.shape, jnp.float32),
            jax.ShapeDtypeStruct((HEAD, rows), jnp.bfloat16),
        ),
        in_specs=[ANY] + [VMEM] * 6,
        out_specs=(ANY, VMEM, VMEM),
        scratch_shapes=[
            pltpu.VMEM((rows, PAIR), jnp.bfloat16),
            pltpu.VMEM((2 * HEAD, D), jnp.bfloat16),
        ]
        + ring_sems()
        + [x_sems, x_sems, y_sems, y_sems]
        + sum_scratch(rows),
        compiler_params=pltpu.CompilerParams(
            collective_id=1, has_side_effects=True, vmem_limit_bytes=LIMIT
        ),
        name="share",
    )(own, stats, query_side, *weights)


def list_pairs(peers, blocks, device, turn_ref, own_ref, far_ref):
    first = device * blocks
    total = blocks * peers
    count = jnp.int32(0)
    for block in range(blocks):
        for offset in range(-BAND, BAND + 1):
            key = first + block + offset
            own_ref[count] = block
            far_ref[count] = jnp.clip(key, 0, total - 1)
            count += ((key >= 0) & (key < total)).astype(jnp.int32)
    slots = turn_ref.shape[1]

    def visit(peer, count):
        for slot in range(slots):
            own = turn_ref[device, slot, peer]
            far = turn_ref[peer, slot, device]
            own_ref[count] = jnp.clip(own - first, 0, blocks - 1)
            far_ref[count] = jnp.clip(far, 0, total - 1)
            count += ((own >= 0) & (jnp.abs(own - far) > BAND)).astype(jnp.int32)
        return count

    count = lax.fori_loop(0, peers, visit, count)
    for pad in range(UNROLL):
        own_ref[count + pad] = 0
        far_ref[count + pad] = first
    return count


def most_pairs(peers, blocks, slots):
    return blocks * (2 * BAND + 1) + slots * peers + UNROLL


def query_kernel(
    peers,
    turn_ref,
    own_ref,
    kv_ref,
    out_ref,
    stats_ref,
    own_list,
    far_list,
    rhs,
    score,
    slope,
    top,
    total,
    mixed,
    query,
):
    blocks = own_ref.shape[0] // BLK
    count = list_pairs(peers, blocks, lax.axis_index("seq"), turn_ref, own_list, far_list)
    rounds = lax.div(count + UNROLL - 1, UNROLL)
    lane = lax.broadcasted_iota(jnp.int32, (BLK, PAIR), 1)
    zero = jnp.zeros((BLK, PAIR), jnp.bfloat16)
    for block in range(blocks):
        pair = own_ref[block * BLK : (block + 1) * BLK, PAIR:]
        rhs[block, :BLK] = jnp.where(lane < HEAD, pair, zero)
        rhs[block, BLK:] = jnp.where(lane < HEAD, zero, pair)
    top[...] = jnp.full_like(top, -jnp.inf)
    total[...] = jnp.zeros_like(total)
    mixed[...] = jnp.zeros_like(mixed)
    query[...] = jnp.zeros_like(query)

    def tiles(step):
        return [(step * UNROLL + u, own_list[step * UNROLL + u], far_list[step * UNROLL + u]) for u in range(UNROLL)]

    def score_step(step, carry):
        now = tiles(step)
        both = [
            lax.dot_general(
                rhs[own], kv_ref[far], (((1,), (1,)), ((), ())), preferred_element_type=jnp.float32
            )
            for _, own, far in now
        ]
        scaled = []
        for (tile, _, _), product in zip(now, both):
            masked = product[:BLK] * EXP2_SCALE + jnp.where(tile < count, 0.0, -jnp.inf)
            score[tile] = masked
            slope[tile] = product[BLK:]
            scaled.append(masked)
        for (_, own, _), masked in zip(now, scaled):
            top[own] = jnp.maximum(top[own], masked)
        return carry

    lax.fori_loop(0, rounds, score_step, 0)
    for block in range(blocks):
        top[block] = jnp.broadcast_to(jnp.max(top[block], axis=1, keepdims=True), (BLK, PAIR))

    def weight_step(step, carry):
        now = tiles(step)
        weights = []
        for tile, own, _ in now:
            weight = jnp.exp2(score[tile] - top[own])
            weights.append(weight)
        sums = [
            jnp.dot(weight.astype(jnp.bfloat16), kv_ref[far], preferred_element_type=jnp.float32)
            for weight, (_, _, far) in zip(weights, now)
        ]
        for (tile, own, _), weight, part in zip(now, weights, sums):
            score[tile] = weight
            total[own] += weight
            mixed[own] += part
        return carry

    lax.fori_loop(0, rounds, weight_step, 0)
    column = jnp.zeros((BLK, PAIR), jnp.float32)
    for block in range(blocks):
        inverse = 1.0 / jnp.sum(total[block], axis=1, keepdims=True)
        output = mixed[block] * inverse
        mixed[block] = output
        pair = own_ref[block * BLK : (block + 1) * BLK, PAIR:].astype(jnp.float32)
        drift = jnp.sum(jnp.where(lane < HEAD, 0.0, pair * output), axis=1, keepdims=True)
        column = jnp.where(lane == block, top[block], column)
        column = jnp.where(lane == blocks + block, inverse, column)
        column = jnp.where(lane == 2 * blocks + block, drift, column)
        total[block] = jnp.broadcast_to(inverse, (BLK, PAIR))
        top[block] = jnp.broadcast_to(drift, (BLK, PAIR))
    stats_ref[...] = jnp.transpose(column)[: stats_ref.shape[0]]

    def slope_step(step, carry):
        now = tiles(step)
        slopes = []
        for tile, own, _ in now:
            prob = score[tile] * total[own]
            slopes.append((prob * (slope[tile] - top[own])).astype(jnp.bfloat16))
        parts = [
            jnp.dot(value, kv_ref[far], preferred_element_type=jnp.float32)
            for value, (_, _, far) in zip(slopes, now)
        ]
        for (_, own, _), part in zip(now, parts):
            query[own] += part
        return carry

    lax.fori_loop(0, rounds, slope_step, 0)
    for block in range(blocks):
        out_ref[block * BLK : (block + 1) * BLK] = jnp.where(
            lane < HEAD, query[block] * SCALE, mixed[block]
        ).astype(jnp.bfloat16)


def attend_queries(turns, projected, kv):
    peers = lax.axis_size("seq")
    rows = projected.shape[0]
    blocks = rows // BLK
    most = most_pairs(peers, blocks, turns.shape[1])
    square = pltpu.VMEM((blocks, BLK, PAIR), jnp.float32)
    flops = most * 4 * 2 * 2 * BLK * BLK * PAIR // 2
    return pl.pallas_call(
        functools.partial(query_kernel, peers),
        out_shape=(
            jax.ShapeDtypeStruct((rows, PAIR), jnp.bfloat16),
            jax.ShapeDtypeStruct((4 * blocks, BLK), jnp.float32),
        ),
        in_specs=[SMEM, VMEM, VMEM],
        out_specs=(VMEM, VMEM),
        scratch_shapes=[
            pltpu.SMEM((most,), jnp.int32),
            pltpu.SMEM((most,), jnp.int32),
            pltpu.VMEM((blocks, 2 * BLK, PAIR), jnp.bfloat16),
            pltpu.VMEM((most, BLK, BLK), jnp.float32),
            pltpu.VMEM((most, BLK, BLK), jnp.float32),
            square,
            square,
            square,
            square,
        ],
        compiler_params=pltpu.CompilerParams(vmem_limit_bytes=LIMIT),
        cost_estimate=pl.CostEstimate(flops=flops, bytes_accessed=kv.size * 2, transcendentals=most * BLK * BLK),
        name="attend_queries",
    )(turns, projected, kv.reshape(-1, BLK, PAIR))


def key_kernel(peers, turn_ref, own_ref, qg_ref, stats_ref, out_ref, own_list, far_list, lhs, grads):
    blocks = own_ref.shape[0] // BLK
    count = list_pairs(peers, blocks, lax.axis_index("seq"), turn_ref, own_list, far_list)
    rounds = lax.div(count + UNROLL - 1, UNROLL)
    lane = lax.broadcasted_iota(jnp.int32, (BLK, PAIR), 1)
    zero = jnp.zeros((BLK, PAIR), jnp.bfloat16)
    for block in range(blocks):
        pair = own_ref[block * BLK : (block + 1) * BLK, :PAIR]
        lhs[block, :BLK] = jnp.where(lane < HEAD, pair, zero)
        lhs[block, BLK:] = jnp.where(lane < HEAD, zero, pair)
    grads[...] = jnp.zeros_like(grads)

    def step_of(step, carry):
        now = []
        for u in range(UNROLL):
            tile = step * UNROLL + u
            now.append((tile, own_list[tile], far_list[tile]))
        both = [
            lax.dot_general(
                lhs[own], qg_ref[far], (((1,), (1,)), ((), ())), preferred_element_type=jnp.float32
            )
            for _, own, far in now
        ]
        factors = []
        for (tile, _, far), product in zip(now, both):
            peer, block = lax.div(far, blocks), lax.rem(far, blocks)
            top, inverse, drift = (
                stats_ref[peer, pl.ds(kind * blocks + block, 1), :] for kind in range(3)
            )
            masked = product[:BLK] * EXP2_SCALE + jnp.where(tile < count, 0.0, -jnp.inf)
            prob = jnp.exp2(masked - top) * inverse
            factors.append(
                jnp.concatenate([prob * (product[BLK:] - drift), prob], axis=0).astype(jnp.bfloat16)
            )
        parts = [
            jnp.dot(factor, qg_ref[far], preferred_element_type=jnp.float32)
            for factor, (_, _, far) in zip(factors, now)
        ]
        for (_, own, _), part in zip(now, parts):
            grads[own] += part
        return carry

    lax.fori_loop(0, rounds, step_of, 0)
    for block in range(blocks):
        out_ref[block * BLK : (block + 1) * BLK] = jnp.where(
            lane < HEAD, grads[block, :BLK] * SCALE, grads[block, BLK:]
        ).astype(jnp.bfloat16)


def attend_keys(turns, projected, qg, stats):
    peers = lax.axis_size("seq")
    rows = projected.shape[0]
    blocks = rows // BLK
    most = most_pairs(peers, blocks, turns.shape[1])
    flops = most * 4 * 2 * 2 * BLK * BLK * PAIR // 2
    return pl.pallas_call(
        functools.partial(key_kernel, peers),
        out_shape=jax.ShapeDtypeStruct((rows, PAIR), jnp.bfloat16),
        in_specs=[SMEM, VMEM, VMEM, VMEM],
        out_specs=VMEM,
        scratch_shapes=[
            pltpu.SMEM((most,), jnp.int32),
            pltpu.SMEM((most,), jnp.int32),
            pltpu.VMEM((blocks, 2 * BLK, PAIR), jnp.bfloat16),
            pltpu.VMEM((blocks, 2 * BLK, PAIR), jnp.float32),
        ],
        compiler_params=pltpu.CompilerParams(vmem_limit_bytes=LIMIT),
        cost_estimate=pl.CostEstimate(flops=flops, bytes_accessed=qg.size * 2, transcendentals=most * BLK * BLK),
        name="attend_keys",
    )(turns, projected, qg.reshape(-1, BLK, PAIR), stats)


def sum_over_seq(grads, sums_ref, from_x, x_sum, from_y, piece, totals, sems):
    _, _, at_y, at_x, _, count_y = places()
    along_x, along_y = seq_partners(at_y, at_x, count_y)
    width = totals.shape[1]
    xs, ys = range(len(along_x)), range(len(along_y))

    def weight(index):
        column = pl.multiple_of(jnp.where(index == RING_X - 1, width, 0), PAIR)
        return grads.at[pl.ds(pl.multiple_of(index * HEAD, HEAD), HEAD), pl.ds(column, width)]

    def columns(index):
        return pl.ds(pl.multiple_of(index * PAIR, PAIR), PAIR)

    def rows(index):
        return pl.ds(pl.multiple_of(index * HEAD, HEAD), HEAD)

    def in_x(step):
        source = weight(lax.rem(at_x + step + 1, RING_X))
        return remote(source, from_x.at[step], sems[0].at[step], sems[1].at[step], along_x[step])

    def in_y(step):
        source = x_sum.at[:, columns(lax.rem(at_y + step + 1, count_y))]
        return remote(source, from_y.at[step], sems[2].at[step], sems[3].at[step], along_y[step])

    def out_y(step, owner):
        target = totals.at[rows(at_x), columns(owner)]
        return remote(piece, target, sems[4].at[step], sems[5].at[step], along_y[step])

    def out_x(step, owner):
        part = totals.at[rows(owner)]
        return remote(part, part, sems[6].at[step], sems[7].at[step], along_x[step])

    for step in xs:
        in_x(step).start()
    yield
    total = weight(at_x)[...].astype(jnp.float32)
    for step in xs:
        in_x(step).wait_recv()
        total += from_x[step].astype(jnp.float32)
    x_sum[...] = total.astype(jnp.bfloat16)
    for step in ys:
        in_y(step).start()
    yield
    total = x_sum[:, columns(at_y)].astype(jnp.float32)
    for step in ys:
        in_y(step).wait_recv()
        total += from_y[step].astype(jnp.float32)
    piece[...] = total.astype(jnp.bfloat16)
    for step in ys:
        out_y(step, at_y).start()
    totals[rows(at_x), columns(at_y)] = piece[...]
    yield
    for step in ys:
        out_y(step, wrap(at_y - step - 1, count_y)).wait_recv()
    for step in xs:
        out_x(step, at_x).start()
    yield
    for step in xs:
        out_x(step, wrap(at_x - step - 1, RING_X)).wait_recv()
    sums_ref[...] = totals[...].astype(jnp.float32)
    for step in xs:
        in_x(step).wait_send()
        out_x(step, at_x).wait_send()
    for step in ys:
        in_y(step).wait_send()
        out_y(step, at_y).wait_send()


def finish_kernel(
    key_side,
    query_side,
    grads,
    key_w,
    value_w,
    query_w,
    out_w,
    grad_frames,
    sums_ref,
    lhs,
    weights,
    from_x,
    x_sum,
    from_y,
    piece,
    totals,
    *refs,
):
    chip, core, at_y, at_x, chips, count_y = places()
    along_x, along_y = seq_partners(at_y, at_x, count_y)
    greet(along_x + along_y + mp_partners(chip, core, chips))
    over_seq = sum_over_seq(grads, sums_ref, from_x, x_sum, from_y, piece, totals, refs[:8])
    take(over_seq, 1)
    fill_weights((key_w, value_w, query_w, out_w), weights)
    lane = lax.broadcasted_iota(jnp.int32, query_side.shape, 1)
    lhs[:, :PAIR] = key_side[...]
    lhs[:, PAIR:] = jnp.where(lane < HEAD, query_side[...], jnp.zeros_like(query_side[...]))

    def partial(tile, half):
        columns = pl.ds(pl.multiple_of(tile * PAIR, PAIR), PAIR)
        return jnp.dot(half_rows_of(lhs, half), weights[:, columns], preferred_element_type=jnp.float32)

    over_mp = sum_over_mp(partial, grad_frames, *refs[8:])
    take(over_mp, 2 * chips)
    take(over_seq, 2)
    take(over_mp, 1)
    finish(over_seq)
    finish(over_mp)


def finish_sums(key_side, query_side, grads, weights):
    peers = lax.axis_size("seq")
    rows = key_side.shape[0]
    height, width = 4 * HEAD, D
    dma = pltpu.SemaphoreType.DMA
    x_sems, y_sems = dma((RING_X - 1,)), dma((peers // RING_X - 1,))
    return pl.pallas_call(
        finish_kernel,
        out_shape=(
            jax.ShapeDtypeStruct((HEAD, rows), jnp.bfloat16),
            jax.ShapeDtypeStruct((height, width), jnp.float32),
        ),
        in_specs=[VMEM] * 7,
        out_specs=(VMEM, VMEM),
        scratch_shapes=[
            pltpu.VMEM((rows, 2 * PAIR), jnp.bfloat16),
            pltpu.VMEM((height, width), jnp.bfloat16),
            pltpu.VMEM((RING_X - 1, HEAD, width), jnp.bfloat16),
            pltpu.VMEM((HEAD, width), jnp.bfloat16),
            pltpu.VMEM((peers // RING_X - 1, HEAD, PAIR), jnp.bfloat16),
            pltpu.VMEM((HEAD, PAIR), jnp.bfloat16),
            pltpu.VMEM((height, width), jnp.bfloat16),
            x_sems,
            x_sems,
            y_sems,
            y_sems,
            y_sems,
            y_sems,
            x_sems,
            x_sems,
        ]
        + sum_scratch(rows),
        compiler_params=pltpu.CompilerParams(
            collective_id=2, has_side_effects=True, vmem_limit_bytes=LIMIT
        ),
        name="finish_sums",
    )(key_side, query_side, grads, *weights)


def on_device(frames, cotangent, query_weight, key_weight, value_weight, out_weight, turn_blocks):
    turns = jnp.transpose(turn_blocks, (0, 2, 1))
    weights = (key_weight, value_weight, query_weight, out_weight)
    features, projected, kv = project(frames, cotangent, weights)
    query_side, stats = attend_queries(turns, projected, kv)
    qg, all_stats, attended = share(projected, stats, query_side, weights)
    key_side = attend_keys(turns, projected, qg, all_stats)
    joint = jnp.concatenate([key_side, query_side], axis=1)
    products = lax.dot_general(
        joint, features, (((0,), (0,)), ((), ())), preferred_element_type=jnp.float32
    )
    grad_frames, sums = finish_sums(key_side, query_side, products.astype(jnp.bfloat16), weights)
    grad_key, grad_value, grad_query, grad_out = (
        sums[index * HEAD : (index + 1) * HEAD] for index in range(4)
    )
    return attended.T, grad_frames.T, grad_query, grad_key, grad_value, grad_out


def solution(mesh):
    return jax.shard_map(
        on_device,
        mesh=mesh,
        in_specs=(
            P("seq", "mp"),
            P("seq", "mp"),
            P("mp", None),
            P("mp", None),
            P("mp", None),
            P("mp", None),
            P(),
        ),
        out_specs=(
            P("seq", "mp"),
            P("seq", "mp"),
            P("mp", None),
            P("mp", None),
            P("mp", None),
            P("mp", None),
        ),
        check_vma=False,
    )
```

time: 519 us -> 173 us (0.33)
  waiting for transfers between devices: 374 us -> 0 us
  Pallas kernels: 0 us -> 162 us
  matrix products: 40.9 us -> 0.73 us
  local copies, waits for them, and re-layouts: 47.8 us -> 8.3 us
  starting transfers between devices: 29.3 us -> 0 us
  between operations: 14.8 us -> 0.74 us
  other arithmetic: 9.43 us -> 0 us
    pallas_call x0 -> x5, Pallas kernels: none -> 162 us  [the longest x1 64.8 us: project(): pl.pallas_call(project_kernel, out_shape=(jax.ShapeDtypeStruct((rows, cor...]
    psum x1 -> x0, waiting for transfers between devices: 148 us -> none  [on_device(): lax.psum(weight_grad.astype(jnp.bfloat16), 'seq').astype(jnp.float32)]
    reduce_scatter x2 -> x0, waiting for transfers between devices: 122 us -> none  [the longest x1 61.9 us: on_device(): lax.psum_scatter(partial_in.astype(jnp.bfloat16), 'mp', scatter_dimension...]
    all_gather x2 -> x0, waiting for transfers between devices: 80.6 us -> none  [the longest x1 45.5 us: on_device(): whole_frames = lax.all_gather(frames, 'mp', axis=1, tiled=True)]
    dot_general x37 -> x1, matrix products: 40.9 us -> 0.73 us  [on_device(): lax.dot_general(joint, features, (((0,), (0,)), ((), ())), preferred_elem...]
    all_to_all x2 -> x0, waiting for transfers between devices: 22.3 us -> none  [the longest x1 22.3 us: on_device(): lax.all_to_all(returned_grads.astype(jnp.bfloat16), 'seq', split_axis=0,...]
    all_to_all x2 -> x0, starting transfers between devices: 19 us -> none  [the longest x1 9.53 us: on_device(): lax.all_to_all(returned_grads.astype(jnp.bfloat16), 'seq', split_axis=0,...]
    another operation x13 -> x0, local copies, waits for them, and re-layouts: 15.3 us -> none  [the longest x3 8.11 us: on_device(): jnp.stack(returned, axis=1)]
  transfers between devices with their start and end apart: 11 -> 0, of which waited for: 6 -> 0; matrix products, arithmetic and copies ran while one was open for 9% -> 0% of each run, Pallas kernels for 0% -> 0%
where the time goes in v1:
time: 173 us; the launch traced here: 172 us
  Pallas kernels  162 us (94%)
  local copies, waits for them, and re-layouts  8.3 us (5%)
    pallas_call x1, Pallas kernels, project(): pl.pallas_call(project_kernel, out_shape=(jax.ShapeDtypeStruct((rows, cor...  64.8 us
    pallas_call x1, Pallas kernels, share(): pl.pallas_call(share_kernel, out_shape=(jax.ShapeDtypeStruct((peers, rows...  47.4 us
    pallas_call x1, Pallas kernels, finish_sums(): pl.pallas_call(finish_kernel, out_shape=(jax.ShapeDtypeStruct((HEAD, rows...  30.7 us
    pallas_call x1, Pallas kernels, attend_queries(): pl.pallas_call(functools.partial(query_kernel, peers), out_shape=(jax.Sha...  11 us
    pallas_call x1, Pallas kernels, attend_keys(): pl.pallas_call(functools.partial(key_kernel, peers), out_shape=jax.ShapeD...  7.97 us
    unnamed x24, local copies, waits for them, and re-layouts  7.31 us

profile of v1, /device:TPU:1, one launch (start us, length us, event | category | flops | bytes accessed | tf_op | source)
XLA Modules:
  0.0 171.6 jit_solution(5432138562005895518)
XLA Ops:
  0.6 0.0 copy-start
  0.6 0.9 copy-done
  1.5 0.0 copy-start.2
  1.5 0.9 copy-done.2
  2.4 0.0 copy-start.4
  2.4 0.9 copy-done.4
  3.3 0.0 copy-start.6
  3.4 0.9 copy-done.6
  4.3 0.0 copy-start.8
  4.3 0.8 copy-done.8
  5.1 0.0 copy-start.9
  5.1 0.8 copy-done.9
  5.9 64.8 %project.1 = (bf16[512,2048]{1,0:T(8,128)(2,1)S(1)}, bf16[512,256]{1,0:T(8,128)(2,1)S(1)}, bf16[32,512,128]{2,1,0:T(8,128)(2,1)}) custom-call(bf16[64,512]{1,0:T(8,128)(2,1)S(1)} %bitcast.8, bf16[64,512]{1,0:T(8,128)(2,1)S(1)} %bitcast.9, bf16[64,1024]{1,0:T(8,128)(2,1)S(1)} %copy-done, bf16[64,1024]{1,0:T(8,128)(2,1)S(1)} %copy-done.2, ...), custom_call_target="tpu_custom_call" | custom-call | tf_op jit(solution)/shard_map/project/pallas_call | solution.py:380
  70.8 0.0 copy-start.10
  70.8 0.7 copy-done.10
  71.5 0.0 copy-start.1
  71.5 0.0 copy-start.3
  71.5 0.0 copy-start.5
  71.5 0.0 copy-start.7
  71.5 11.0 %attend_queries.1 = (bf16[512,128]{1,0:T(8,128)(2,1)S(1)}, f32[16,128]{1,0:T(8,128)S(1)}) custom-call(s32[32,2,32]{2,1,0:T(2,128)S(1)} %bitcast.12, bf16[512,256]{1,0:T(8,128)(2,1)S(1)} %get-tuple-element.16.own_ref.own, bf16[128,128,128]{2,1,0:T(8,128)(2,1)} %bitcast.14), custom_call_target="tpu_custom_call" | custom-call | flops 1476395008 | bytes 4194304 | tf_op jit(solution)/shard_map/attend_queries/pallas_call | solution.py:660
  82.5 0.0 copy-done.1
  82.5 0.0 copy-done.3
  82.5 0.0 copy-done.5
  82.6 0.0 copy-done.7
  82.6 47.4 %share.1 = (bf16[32,512,128]{2,1,0:T(8,128)(2,1)}, f32[32,16,128]{2,1,0:T(8,128)S(1)}, bf16[64,512]{1,0:T(8,128)(2,1)S(1)}) custom-call(bf16[512,256]{1,0:T(8,128)(2,1)S(1)} %get-tuple-element.16.own_ref.own, f32[16,128]{1,0:T(8,128)S(1)} %get-tuple-element.18.stats, bf16[512,128]{1,0:T(8,128)(2,1)S(1)} %get-tuple-element.19.query_side, ...), custom_call_target="tpu_custom_call" | custom-call | tf_op jit(solution)/shard_map/share/pallas_call | solution.py:490
  130.0 8.0 %attend_keys.1.key_side = bf16[512,128]{1,0:T(8,128)(2,1)S(1)} custom-call(s32[32,2,32]{2,1,0:T(2,128)S(1)} %bitcast.13, bf16[512,256]{1,0:T(8,128)(2,1)S(1)} %get-tuple-element.16.own_ref.own, bf16[128,128,128]{2,1,0:T(8,128)(2,1)} %bitcast.15, f32[32,16,128]{2,1,0:T(8,128)S(1)} %get-tuple-element.22.stats_ref), custom_call_target="tpu_custom_call" | custom-call | flops 1476395008 | bytes 4194304 | tf_op jit(solution)/shard_map/attend_keys/pallas_call | solution.py:740
  137.9 0.7 convolution_convert_fusion.grads
  138.7 30.7 %finish_sums.1 = (bf16[64,512]{1,0:T(8,128)(2,1)S(1)}, f32[256,1024]{1,0:T(8,128)S(1)}) custom-call(bf16[512,128]{1,0:T(8,128)(2,1)S(1)} %attend_keys.1.key_side, bf16[512,128]{1,0:T(8,128)(2,1)S(1)} %get-tuple-element.19.query_side, bf16[256,2048]{1,0:T(8,128)(2,1)S(1)} %convolution_convert_fusion.grads, bf16[64,1024]{1,0:T(8,128)(2,1)S(1)} %copy-done.1, ...), custom_call_target="tpu_custom_call" | custom-call | tf_op jit(solution)/shard_map/finish_sums/pallas_call | solution.py:872
  169.3 1.0 fusion.4
  170.3 0.6 copy.15
  171.0 0.6 copy.16
Async XLA Ops:
  0.6 0.9 copy-start
  1.5 0.9 copy-start.2
  2.4 0.9 copy-start.4
  3.3 0.9 copy-start.6
  4.3 0.8 copy-start.8
  5.1 0.8 copy-start.9
  70.8 0.8 copy-start.10
  71.5 11.0 %copy-start.1 = (bf16[64,1024]{1,0:T(8,128)(2,1)S(1)}, bf16[64,1024]{1,0:T(8,128)(2,1)}, u32[]{:S(2)}) copy-start(bf16[64,1024]{1,0:T(8,128)(2,1)} %key_w.5) | copy-start | bytes 393220
  71.5 11.0 %copy-start.3 = (bf16[64,1024]{1,0:T(8,128)(2,1)S(1)}, bf16[64,1024]{1,0:T(8,128)(2,1)}, u32[]{:S(2)}) copy-start(bf16[64,1024]{1,0:T(8,128)(2,1)} %value_w.5) | copy-start | bytes 393220
  71.5 11.0 %copy-start.5 = (bf16[64,1024]{1,0:T(8,128)(2,1)S(1)}, bf16[64,1024]{1,0:T(8,128)(2,1)}, u32[]{:S(2)}) copy-start(bf16[64,1024]{1,0:T(8,128)(2,1)} %query_w.5) | copy-start | bytes 393220
  71.5 11.0 %copy-start.7 = (bf16[64,1024]{1,0:T(8,128)(2,1)S(1)}, bf16[64,1024]{1,0:T(8,128)(2,1)}, u32[]{:S(2)}) copy-start(bf16[64,1024]{1,0:T(8,128)(2,1)} %out_w.5) | copy-start | bytes 393220

commit v2 on v1

--- a/solution.py
+++ b/solution.py
@@ -22,7 +22,7 @@
 VMEM = pl.BlockSpec(memory_space=pltpu.VMEM)
 SMEM = pl.BlockSpec(memory_space=pltpu.SMEM)
 ANY = pl.BlockSpec(memory_space=pl.ANY)
-LIMIT = 50 * 1024 * 1024
+LIMIT = 60 * 1024 * 1024
 
 
 def wrap(index, count):
@@ -52,9 +52,12 @@
         pass
 
 
-def fill_weights(refs, whole):
+def stack_rows(refs, whole, sems):
+    copies = []
     for index, ref in enumerate(refs):
-        whole[index * HEAD : (index + 1) * HEAD] = ref[...]
+        target = whole.at[pl.ds(index * HEAD, HEAD)]
+        copies.append(pltpu.make_async_copy(ref, target, sems.at[index]))
+    return copies
 
 
 def places():
@@ -73,97 +76,97 @@
 
 
 @functools.cache
-def ring_plan(count_y, count_x):
-    sizes = {"x": count_x, "y": count_y}
-    timed = []
-
-    def ring(kind, axis, at, begin):
-        count = sizes[axis]
+def ring_messages(count_y, count_x):
+    messages = []
+    for phase, count, split in (("x", count_x, False), ("y", count_y, False), ("row", count_y, True), ("col", count_x, True)):
         for hop in range(1, count // 2 + 1):
-            for way in (1, -1):
-                far = -way * (hop - 1)
-                spot = (far, at) if axis == "x" else (at, far)
-                half = None if hop < count // 2 else (0 if way == 1 else 1)
-                timed.append((begin + hop - 1, kind, axis, way, spot[0], spot[1], half))
-
-    def steps(count):
-        near = [(sign * hop, hop) for hop in range(1, count // 2) for sign in (-1, 1)]
-        return [(0, 0)] + near + [(count // 2, count // 2)]
-
-    ring(0, "x", 0, 0)
-    ring(1, "y", 0, 0)
-    for dx, begin in steps(count_x):
-        ring(0, "y", dx, begin)
-    for dy, begin in steps(count_y):
-        ring(1, "x", dy, begin)
-    timed.sort(key=lambda step: step[0])
-    plan = []
-    for _, kind, axis, way, dx, dy, half in timed:
-        plan.append((kind, axis, way, dx % count_x, dy % count_y, half))
-    return tuple(plan)
+            for way in (0, 1):
+                if hop == count // 2:
+                    messages.append((phase, way, hop, way))
+                elif split:
+                    messages += [(phase, way, hop, 0), (phase, way, hop, 1)]
+                else:
+                    messages.append((phase, way, hop, None))
+    return tuple(messages)
 
 
 def ring_gather(own, store, local, send, recv):
     _, _, at_y, at_x, _, count_y = places()
     near = neighbours(at_y, at_x, count_y)
-    half_rows = store.shape[1] // 2
-    plan = ring_plan(count_y, RING_X)
-
-    def part(ref, kind, half):
-        if half is None:
-            return ref.at[pl.ds(kind * half_rows, half_rows)]
-        quarter = half_rows // 2
-        return ref.at[pl.ds(kind * half_rows + half * quarter, quarter)]
-
-    def spot(kind, dx, dy, half):
-        slot = wrap(at_y + dy, count_y) * RING_X + wrap(at_x + dx, RING_X)
-        return part(store.at[slot], kind, half)
-
-    def copy_of(index, source, target):
-        _, axis, way, _, _, _ = plan[index]
-        return remote(source, target, send.at[index], recv.at[index], near[axis, way])
-
-    def outgoing(index):
-        kind, _, _, dx, dy, half = plan[index]
-        target = spot(kind, dx, dy, half)
-        return copy_of(index, target if dx or dy else part(own, kind, half), target)
-
-    def tile_in(index):
-        kind, axis, way, dx, dy, _ = plan[index]
-        if axis == "x":
-            return kind, (dx - way) % RING_X, dy
-        return kind, dx, (dy - way) % count_y
-
-    def incoming(index):
-        target = spot(*tile_in(index), plan[index][-1])
-        return copy_of(index, target, target)
-
-    arrivals = {}
-    for index in range(len(plan)):
-        arrivals.setdefault(tile_in(index), []).append(index)
-    keep = pltpu.make_async_copy(own, store.at[at_y * RING_X + at_x], local)
-    waited = set()
-    for index, (kind, _, _, dx, dy, _) in enumerate(plan):
-        if dx or dy:
-            for before in arrivals[kind, dx, dy]:
-                if before not in waited:
-                    waited.add(before)
-                    incoming(before).wait_recv()
-        outgoing(index).start()
-        if index == 0:
-            keep.start()
-        yield
-    for index in range(len(plan)):
-        if index not in waited:
-            incoming(index).wait_recv()
+    half_rows = store.shape[2] // 2
+    quarter = half_rows // 2
+    messages = ring_messages(count_y, RING_X)
+
+    def rows(phase, part):
+        base = 0 if phase in ("x", "row") else half_rows
+        return pl.ds(base, half_rows) if part is None else pl.ds(base + part * quarter, quarter)
+
+    def region(phase, offset, part):
+        if phase in ("x", "col"):
+            column = wrap(at_x + offset, RING_X)
+            return store.at[at_y if phase == "x" else slice(None), column, rows(phase, part)]
+        row = wrap(at_y + offset, count_y)
+        return store.at[row, at_x if phase == "y" else slice(None), rows(phase, part)]
+
+    def copy_of(message, arriving):
+        phase, way, hop, part = message
+        sign = -1 if way == 0 else 1
+        target = region(phase, sign * (hop if arriving else hop - 1), part)
+        source = target
+        if hop == 1 and phase in ("x", "y") and not arriving:
+            source = own.at[rows(phase, part)]
+        index = messages.index(message)
+        axis = "x" if phase in ("x", "col") else "y"
+        return remote(source, target, send.at[index], recv.at[index], near[axis, 1 if way == 0 else -1])
+
+    def of(phase, hop):
+        found = [message for message in messages if message[0] == phase and message[2] == hop]
+        return sorted(found, key=lambda message: (message[3] or 0, message[1]))
+
+    waited = []
+
+    def await_all(arrived):
+        for message in arrived:
+            if message not in waited:
+                waited.append(message)
+                copy_of(message, True).wait_recv()
+
+    def start_hop(phase, hop):
+        for message in of(phase, hop):
+            _, way, _, part = message
+            if hop > 1:
+                await_all([m for m in of(phase, hop - 1) if m[1] == way and m[3] in (None, part)])
+            copy_of(message, False).start()
+            yield
+
+    keep = pltpu.make_async_copy(own, store.at[at_y, at_x], local)
+    yield from start_hop("x", 1)
+    yield from start_hop("y", 1)
+    keep.start()
+    yield from start_hop("x", 2)
+    yield from start_hop("y", 2)
+    keep.wait()
+    for hop in range(1, RING_X // 2 + 1):
+        await_all(of("x", hop))
+    yield from start_hop("row", 1)
+    for hop in range(3, count_y // 2 + 1):
+        yield from start_hop("y", hop)
+    yield from start_hop("row", 2)
+    for hop in range(1, count_y // 2 + 1):
+        await_all(of("y", hop))
+    yield from start_hop("col", 1)
+    yield from start_hop("row", 3)
+    yield from start_hop("col", 2)
+    for hop in range(4, count_y // 2 + 1):
+        yield from start_hop("row", hop)
+    await_all(messages)
     yield
-    for index in range(len(plan)):
-        outgoing(index).wait_send()
-    keep.wait()
+    for message in messages:
+        copy_of(message, False).wait_send()
 
 
 def ring_sems():
-    steps = len(ring_plan(lax.axis_size("seq") // RING_X, RING_X))
+    steps = len(ring_messages(lax.axis_size("seq") // RING_X, RING_X))
     return [
         pltpu.SemaphoreType.DMA,
         pltpu.SemaphoreType.DMA((steps,)),
@@ -274,6 +277,8 @@
     weights,
     mine,
     other,
+    loaded,
+    filled,
     pair_send,
     pair_recv,
     z_send,
@@ -289,50 +294,57 @@
     sibling = {"mp": 2 * chip + 1 - core}
     right = {"mp": 2 * wrap(chip + 1, chips) + core}
     left = {"mp": 2 * wrap(chip - 1, chips) + core}
+    inputs = stack_rows((frames_ref, grad_ref), mine, loaded)
+    fill = stack_rows((key_w, value_w, query_w, out_w), weights, filled)
+    for copy in inputs + fill:
+        copy.start()
     greet([sibling, right, left] + list(neighbours(at_y, at_x, count_y).values()))
-
-    mine[:HEAD] = frames_ref[...]
-    mine[HEAD:] = grad_ref[...]
-    swap = remote(mine, other, pair_send, pair_recv, sibling)
+    for copy in inputs:
+        copy.wait()
+
+    def side(whose):
+        return pl.ds(pl.multiple_of(whose * half, half), half)
+
+    swap = remote(mine.at[:, side(1 - core)], other, pair_send, pair_recv, sibling)
     swap.start()
-    fill_weights((key_w, value_w, query_w, out_w), weights)
-    swap.wait()
-    column = pl.multiple_of(chip * PAIR, PAIR)
-    here, there = mine[...].astype(jnp.float32), other[...].astype(jnp.float32)
+    swap.wait_recv()
+    here, there = mine[:, side(core)].astype(jnp.float32), other[...].astype(jnp.float32)
     even = jnp.where(core == 0, here, there)
     odd = jnp.where(core == 0, there, here)
     for kind in (0, 1):
-        side = slice(kind * HEAD, (kind + 1) * HEAD)
-        tile = jnp.transpose(jnp.concatenate([even[side], odd[side]], axis=0))
-        features[:, pl.ds(kind * width + column, PAIR)] = tile.astype(jnp.bfloat16)
-
-    def place(kind, tile, whose, way, hop):
+        part = slice(kind * HEAD, (kind + 1) * HEAD)
+        tile = jnp.transpose(jnp.concatenate([even[part], odd[part]], axis=0))
+        column = pl.multiple_of(kind * width + chip * PAIR, PAIR)
+        features[side(core), pl.ds(column, PAIR)] = tile.astype(jnp.bfloat16)
+
+    def place(kind, tile, way, hop):
         start = pl.multiple_of(kind * width + wrap(tile, chips) * PAIR, PAIR)
         count = half if hop < hops else half // 2
-        first = whose * half + (0 if hop < hops else way * count)
+        first = core * half + (0 if hop < hops else way * count)
         return features.at[pl.ds(pl.multiple_of(first, count), count), pl.ds(start, PAIR)]
 
-    def sent(kind, way, hop):
-        spot = place(kind, chip + (1 - hop if way == 0 else hop - 1), core, way, hop)
+    def along_z(kind, way, hop, moved):
+        spot = place(kind, chip + (-moved if way == 0 else moved), way, hop)
         at = (kind, way, hop - 1)
         return remote(spot, spot, z_send.at[at], z_recv.at[at], right if way == 0 else left)
 
+    def sent(kind, way, hop):
+        return along_z(kind, way, hop, hop - 1)
+
     def landed(kind, way, hop):
-        spot = place(kind, chip + (-hop if way == 0 else hop), core, way, hop)
-        at = (kind, way, hop - 1)
-        return remote(spot, spot, z_send.at[at], z_recv.at[at], right if way == 0 else left)
-
-    def shared(kind, way, hop, whose):
-        spot = place(kind, chip + (-hop if way == 0 else hop), whose, way, hop)
-        at = (kind, way, hop - 1)
-        return remote(spot, spot, share_send.at[at], share_recv.at[at], sibling)
+        return along_z(kind, way, hop, hop)
+
+    def shared(kind, whose):
+        spot = features.at[side(whose), pl.ds(kind * width, width)]
+        return remote(spot, spot, share_send.at[kind], share_recv.at[kind], sibling)
 
     def advance(kind, hop):
         for way in (0, 1):
             landed(kind, way, hop).wait_recv()
             if hop < hops:
                 sent(kind, way, hop + 1).start()
-            shared(kind, way, hop, core).start()
+        if hop == hops:
+            shared(kind, core).start()
 
     for kind in (0, 1):
         for way in (0, 1):
@@ -341,9 +353,9 @@
     for hop in range(2, hops + 1):
         advance(0, hop)
         advance(1, hop - 1)
-    steps = [(way, hop) for hop in range(1, hops + 1) for way in (0, 1)]
-    for way, hop in steps:
-        shared(0, way, hop, 1 - core).wait_recv()
+    for copy in fill:
+        copy.wait()
+    shared(0, 1 - core).wait_recv()
 
     lane = lax.broadcasted_iota(jnp.int32, (BLK, PAIR), 1)
     blocks = [slice(start, start + BLK) for start in range(0, rows, BLK)]
@@ -355,10 +367,9 @@
         own[block, :PAIR] = product[:, :PAIR].astype(jnp.bfloat16)
         own[block, PAIR:] = product[:, PAIR:].astype(jnp.bfloat16)
     gather = ring_gather(own.at[:, pl.ds(0, PAIR)], kv_ref, *ring)
-    take(gather, 8)
+    take(gather, 4)
     advance(1, hops)
-    for way, hop in steps:
-        shared(1, way, hop, 1 - core).wait_recv()
+    shared(1, 1 - core).wait_recv()
     for block in blocks:
         product = lax.dot_general(
             features[block, width:], weights[PAIR:], against, preferred_element_type=jnp.float32
@@ -366,10 +377,12 @@
         own[block, PAIR:] = jnp.where(lane < HEAD, own[block, PAIR:], product.astype(jnp.bfloat16))
         take(gather, 4)
     finish(gather)
+    swap.wait_send()
     for kind in (0, 1):
-        for way, hop in steps:
-            sent(kind, way, hop).wait_send()
-            shared(kind, way, hop, core).wait_send()
+        shared(kind, core).wait_send()
+        for hop in range(1, hops + 1):
+            for way in (0, 1):
+                sent(kind, way, hop).wait_send()
 
 
 def project(frames, cotangent, weights):
@@ -382,20 +395,22 @@
         out_shape=(
             jax.ShapeDtypeStruct((rows, cores * PAIR), jnp.bfloat16),
             jax.ShapeDtypeStruct((rows, 2 * PAIR), jnp.bfloat16),
-            jax.ShapeDtypeStruct((peers, rows, PAIR), jnp.bfloat16),
+            jax.ShapeDtypeStruct((peers // RING_X, RING_X, rows, PAIR), jnp.bfloat16),
         ),
-        in_specs=[VMEM] * 6,
+        in_specs=[ANY] * 6,
         out_specs=(VMEM, VMEM, ANY),
         scratch_shapes=[
             pltpu.VMEM((4 * HEAD, D), jnp.bfloat16),
             pltpu.VMEM((PAIR, rows), jnp.bfloat16),
-            pltpu.VMEM((PAIR, rows), jnp.bfloat16),
+            pltpu.VMEM((PAIR, rows // 2), jnp.bfloat16),
+            dma((2,)),
+            dma((4,)),
             dma,
             dma,
             sems,
             sems,
-            sems,
-            sems,
+            dma((2,)),
+            dma((2,)),
         ]
         + ring_sems(),
         compiler_params=pltpu.CompilerParams(
@@ -437,8 +452,6 @@
     own,
     stats,
     query_side,
-    key_w,
-    value_w,
     query_w,
     out_w,
     qg_ref,
@@ -446,6 +459,7 @@
     attended,
     lhs,
     weights,
+    filled,
     local,
     send,
     recv,
@@ -457,13 +471,16 @@
 ):
     chip, core, at_y, at_x, chips, count_y = places()
     along_x, along_y = seq_partners(at_y, at_x, count_y)
+    fill = stack_rows((query_w, out_w), weights, filled)
+    for copy in fill:
+        copy.start()
     greet(along_x + along_y + mp_partners(chip, core, chips))
     table = exchange_stats(stats, all_stats, x_send, x_recv, y_send, y_recv)
     take(table, 1)
     gather = ring_gather(own.at[:, pl.ds(PAIR, PAIR)], qg_ref, local, send, recv)
-    take(gather, 8)
-    weights[:HEAD] = query_w[...]
-    weights[HEAD:] = out_w[...]
+    take(gather, 4)
+    for copy in fill:
+        copy.wait()
     lane = lax.broadcasted_iota(jnp.int32, lhs.shape, 1)
     lhs[...] = jnp.where(lane < HEAD, jnp.zeros_like(lhs[...]), query_side[...])
 
@@ -476,7 +493,7 @@
     take(table, 1)
     for _ in range(2 * chips):
         take(total, 1)
-        take(gather, 3)
+        take(gather, 2)
     finish(gather)
     finish(total)
     finish(table)
@@ -490,15 +507,16 @@
     return pl.pallas_call(
         share_kernel,
         out_shape=(
-            jax.ShapeDtypeStruct((peers, rows, PAIR), jnp.bfloat16),
+            jax.ShapeDtypeStruct((peers // RING_X, RING_X, rows, PAIR), jnp.bfloat16),
             jax.ShapeDtypeStruct((peers,) + stats.shape, jnp.float32),
             jax.ShapeDtypeStruct((HEAD, rows), jnp.bfloat16),
         ),
-        in_specs=[ANY] + [VMEM] * 6,
+        in_specs=[ANY, VMEM, VMEM, ANY, ANY],
         out_specs=(ANY, VMEM, VMEM),
         scratch_shapes=[
             pltpu.VMEM((rows, PAIR), jnp.bfloat16),
             pltpu.VMEM((2 * HEAD, D), jnp.bfloat16),
+            dma((2,)),
         ]
         + ring_sems()
         + [x_sems, x_sems, y_sems, y_sems]
@@ -507,7 +525,7 @@
             collective_id=1, has_side_effects=True, vmem_limit_bytes=LIMIT
         ),
         name="share",
-    )(own, stats, query_side, *weights)
+    )(own, stats, query_side, *weights[2:])
 
 
 def list_pairs(peers, blocks, device, turn_ref, own_ref, far_ref):
@@ -834,6 +852,7 @@
     sums_ref,
     lhs,
     weights,
+    filled,
     from_x,
     x_sum,
     from_y,
@@ -843,10 +862,14 @@
 ):
     chip, core, at_y, at_x, chips, count_y = places()
     along_x, along_y = seq_partners(at_y, at_x, count_y)
+    fill = stack_rows((key_w, value_w, query_w, out_w), weights, filled)
+    for copy in fill:
+        copy.start()
     greet(along_x + along_y + mp_partners(chip, core, chips))
     over_seq = sum_over_seq(grads, sums_ref, from_x, x_sum, from_y, piece, totals, refs[:8])
     take(over_seq, 1)
-    fill_weights((key_w, value_w, query_w, out_w), weights)
+    for copy in fill:
+        copy.wait()
     lane = lax.broadcasted_iota(jnp.int32, query_side.shape, 1)
     lhs[:, :PAIR] = key_side[...]
     lhs[:, PAIR:] = jnp.where(lane < HEAD, query_side[...], jnp.zeros_like(query_side[...]))
@@ -875,11 +898,12 @@
             jax.ShapeDtypeStruct((HEAD, rows), jnp.bfloat16),
             jax.ShapeDtypeStruct((height, width), jnp.float32),
         ),
-        in_specs=[VMEM] * 7,
+        in_specs=[VMEM] * 3 + [ANY] * 4,
         out_specs=(VMEM, VMEM),
         scratch_shapes=[
             pltpu.VMEM((rows, 2 * PAIR), jnp.bfloat16),
             pltpu.VMEM((height, width), jnp.bfloat16),
+            dma((4,)),
             pltpu.VMEM((RING_X - 1, HEAD, width), jnp.bfloat16),
             pltpu.VMEM((HEAD, width), jnp.bfloat16),
             pltpu.VMEM((peers // RING_X - 1, HEAD, PAIR), jnp.bfloat16),

time: 173 us -> 182 us (1.052)
  Pallas kernels: 162 us -> 174 us
  local copies, waits for them, and re-layouts: 8.3 us -> 3.48 us
  matrix products: 0.73 us -> 2.6 us
    unnamed x24 -> x10, local copies, waits for them, and re-layouts: 7.31 us -> 1.28 us
    pallas_call x1, Pallas kernels: 64.8 us -> 70.7 us  [project(): pl.pallas_call(project_kernel, out_shape=(jax.ShapeDtypeStruct((rows, cor...]
    pallas_call x1, Pallas kernels: 30.7 us -> 36.4 us  [finish_sums(): pl.pallas_call(finish_kernel, out_shape=(jax.ShapeDtypeStruct((HEAD, rows...]
    dot_general x1, matrix products: 0.73 us -> 2.6 us  [on_device(): lax.dot_general(joint, features, (((0,), (0,)), ((), ())), preferred_elem...]
where the time goes in v2:
time: 182 us; the launch traced here: 181 us
  Pallas kernels  174 us (96%)
  local copies, waits for them, and re-layouts  3.48 us (2%)
  matrix products  2.6 us (1%)
    pallas_call x1, Pallas kernels, project(): pl.pallas_call(project_kernel, out_shape=(jax.ShapeDtypeStruct((rows, cor...  70.7 us
    pallas_call x1, Pallas kernels, share(): pl.pallas_call(share_kernel, out_shape=(jax.ShapeDtypeStruct((peers // RI...  46.5 us
    pallas_call x1, Pallas kernels, finish_sums(): pl.pallas_call(finish_kernel, out_shape=(jax.ShapeDtypeStruct((HEAD, rows...  36.4 us
    pallas_call x1, Pallas kernels, attend_queries(): pl.pallas_call(functools.partial(query_kernel, peers), out_shape=(jax.Sha...  11.7 us
    pallas_call x1, Pallas kernels, attend_keys(): pl.pallas_call(functools.partial(key_kernel, peers), out_shape=jax.ShapeD...  8.88 us

profile of v2, /device:TPU:1, one launch (start us, length us, event | category | flops | bytes accessed | tf_op | source)
XLA Modules:
  0.0 180.9 jit_solution(8225764886063709501)
XLA Ops:
  0.6 70.7 %project.1 = (bf16[512,2048]{1,0:T(8,128)(2,1)}, bf16[512,256]{1,0:T(8,128)(2,1)}, bf16[8,4,512,128]{3,2,1,0:T(8,128)(2,1)}) custom-call(bf16[64,512]{1,0:T(8,128)(2,1)} %bitcast.8, bf16[64,512]{1,0:T(8,128)(2,1)} %bitcast.9, bf16[64,1024]{1,0:T(8,128)(2,1)} %key_w.3, bf16[64,1024]{1,0:T(8,128)(2,1)} %value_w.3, bf16[64,1024]{1,0:T(8,128)(2,1)} %query_w.5, ...), custom_call_target="tpu_custom_call" | custom-call | tf_op jit(solution)/shard_map/project/pallas_call | solution.py:393
  71.3 11.7 %attend_queries.1 = (bf16[512,128]{1,0:T(8,128)(2,1)}, f32[16,128]{1,0:T(8,128)}) custom-call(s32[32,2,32]{2,1,0:T(2,128)} %bitcast.14, bf16[512,256]{1,0:T(8,128)(2,1)} %get-tuple-element.16.own_ref.own, bf16[128,128,128]{2,1,0:T(8,128)(2,1)} %bitcast.12), custom_call_target="tpu_custom_call" | custom-call | flops 1476395008 | bytes 4194304 | tf_op jit(solution)/shard_map/attend_queries/pallas_call | solution.py:678
  83.0 46.5 %share.1 = (bf16[8,4,512,128]{3,2,1,0:T(8,128)(2,1)}, f32[32,16,128]{2,1,0:T(8,128)}, bf16[64,512]{1,0:T(8,128)(2,1)}) custom-call(bf16[512,256]{1,0:T(8,128)(2,1)} %get-tuple-element.16.own_ref.own, f32[16,128]{1,0:T(8,128)} %get-tuple-element.18.stats, bf16[512,128]{1,0:T(8,128)(2,1)} %get-tuple-element.19.query_side, bf16[64,1024]{1,0:T(8,128)(2,1)} %query_w.5, ...), custom_call_target="tpu_custom_call" | custom-call | tf_op jit(solution)/shard_map/share/pallas_call | solution.py:507
  129.5 0.0 copy-start
  129.5 0.0 copy-start.1
  129.5 8.9 %attend_keys.1.key_side = bf16[512,128]{1,0:T(8,128)(2,1)} custom-call(s32[32,2,32]{2,1,0:T(2,128)} %bitcast.15, bf16[512,256]{1,0:T(8,128)(2,1)} %get-tuple-element.16.own_ref.own, bf16[128,128,128]{2,1,0:T(8,128)(2,1)} %bitcast.13, f32[32,16,128]{2,1,0:T(8,128)} %get-tuple-element.22.stats_ref), custom_call_target="tpu_custom_call" | custom-call | flops 1476395008 | bytes 4194304 | tf_op jit(solution)/shard_map/attend_keys/pallas_call | solution.py:758
  138.4 0.0 copy-done
  138.4 0.0 copy-done.1
  138.4 2.6 %convolution_convert_fusion.grads = bf16[256,2048]{1,0:T(8,128)(2,1)} fusion(bf16[512,2048]{1,0:T(8,128)(2,1)S(1)} %copy-done, bf16[512,128]{1,0:T(8,128)(2,1)S(1)} %copy-done.1, bf16[512,128]{1,0:T(8,128)(2,1)} %attend_keys.1.key_side), kind=kOutput, calls=%fused_computation | convolution fusion | flops 537919488 | bytes 3407872 | tf_op jit(solution)/shard_map/dot_general | solution.py:937
  141.0 0.0 copy-start.2
  141.0 36.4 %finish_sums.1 = (bf16[64,512]{1,0:T(8,128)(2,1)}, f32[256,1024]{1,0:T(8,128)}) custom-call(bf16[512,128]{1,0:T(8,128)(2,1)} %attend_keys.1.key_side, bf16[512,128]{1,0:T(8,128)(2,1)} %get-tuple-element.19.query_side, bf16[256,2048]{1,0:T(8,128)(2,1)} %convolution_convert_fusion.grads, bf16[64,1024]{1,0:T(8,128)(2,1)} %key_w.3, bf16[64,1024]{1,0:T(8,128)(2,1)} %value_w.3, ...), custom_call_target="tpu_custom_call" | custom-call | tf_op jit(solution)/shard_map/finish_sums/pallas_call | solution.py:895
  177.4 0.0 copy-start.3
  177.5 2.2 %fusion.4 = (f32[64,1024]{1,0:T(8,128)}, f32[64,1024]{1,0:T(8,128)}, f32[64,1024]{1,0:T(8,128)}, f32[64,1024]{1,0:T(8,128)}) fusion(f32[256,1024]{1,0:T(8,128)} %get-tuple-element.25), kind=kLoop, calls=%fused_computation.5 | loop fusion | bytes 2097152 | tf_op jit(solution)/shard_map/slice | solution.py:942
  179.7 0.0 copy-done.2
  179.7 0.6 copy.15
  180.3 0.0 copy-done.3
  180.3 0.6 copy.16
Async XLA Ops:
  129.5 8.9 %copy-start = (bf16[512,2048]{1,0:T(8,128)(2,1)S(1)}, bf16[512,2048]{1,0:T(8,128)(2,1)}, u32[]{:S(2)}) copy-start(bf16[512,2048]{1,0:T(8,128)(2,1)} %get-tuple-element.23) | copy-start | bytes 6291460
  129.5 8.9 %copy-start.1 = (bf16[512,128]{1,0:T(8,128)(2,1)S(1)}, bf16[512,128]{1,0:T(8,128)(2,1)}, u32[]{:S(2)}) copy-start(bf16[512,128]{1,0:T(8,128)(2,1)} %get-tuple-element.19.query_side) | copy-start | bytes 393220
  141.0 38.7 %copy-start.2 = (bf16[64,512]{1,0:T(8,128)(2,1)S(1)}, bf16[64,512]{1,0:T(8,128)(2,1)}, u32[]{:S(2)}) copy-start(bf16[64,512]{1,0:T(8,128)(2,1)} %get-tuple-element.20) | copy-start | bytes 196612
  177.4 2.8 %copy-start.3 = (bf16[64,512]{1,0:T(8,128)(2,1)S(1)}, bf16[64,512]{1,0:T(8,128)(2,1)}, u32[]{:S(2)}) copy-start(bf16[64,512]{1,0:T(8,128)(2,1)} %get-tuple-element.24) | copy-start | bytes 196612

commit v3 on v2

v3 whole, which is shorter than its diff:
```python
import functools
import math

import jax
import jax.numpy as jnp
from jax import lax
from jax.experimental import pallas as pl
from jax.experimental.pallas import tpu as pltpu
from jax.sharding import PartitionSpec as P

D = 1024
HEADS = 16
BLK = 128
BAND = 2
RING_X = 4
ROWS = 4
LEAST = -3e38
HEAD = D // HEADS
PAIR = 2 * HEAD
UNROLL = 4
SCALE = 1.0 / math.sqrt(HEAD)
EXP2_SCALE = SCALE * math.log2(math.e)
MESH = pl.DeviceIdType.MESH
VMEM = pl.BlockSpec(memory_space=pltpu.VMEM)
SMEM = pl.BlockSpec(memory_space=pltpu.SMEM)
ANY = pl.BlockSpec(memory_space=pl.ANY)
LIMIT = 48 * 1024 * 1024


def wrap(index, count):
    return lax.rem(index + count, count)


def greet(devices):
    barrier = pltpu.get_barrier_semaphore()
    for device in devices:
        pl.semaphore_signal(barrier, inc=1, device_id=device, device_id_type=MESH)
    pl.semaphore_wait(barrier, len(devices))


def remote(source, target, send, recv, device):
    return pltpu.make_async_remote_copy(
        source, target, send, recv, device_id=device, device_id_type=MESH
    )


def take(process, count):
    for _ in range(count):
        next(process, None)


def finish(process):
    for _ in process:
        pass


def stack_rows(refs, whole, sems):
    copies = []
    for index, ref in enumerate(refs):
        target = whole.at[pl.ds(index * HEAD, HEAD)]
        copies.append(pltpu.make_async_copy(ref, target, sems.at[index]))
    return copies


def places():
    me_mp, me = lax.axis_index("mp"), lax.axis_index("seq")
    chips, count_y = lax.axis_size("mp") // 2, lax.axis_size("seq") // RING_X
    return lax.div(me_mp, 2), lax.rem(me_mp, 2), lax.div(me, RING_X), lax.rem(me, RING_X), chips, count_y


def neighbours(at_y, at_x, count_y):
    return {
        ("x", 1): {"seq": at_y * RING_X + wrap(at_x + 1, RING_X)},
        ("x", -1): {"seq": at_y * RING_X + wrap(at_x - 1, RING_X)},
        ("y", 1): {"seq": wrap(at_y + 1, count_y) * RING_X + at_x},
        ("y", -1): {"seq": wrap(at_y - 1, count_y) * RING_X + at_x},
    }


def ring_gather(store, at, count, devices, send, recv):
    half_rows = store.shape[1] // 2
    last = count // 2

    def copy_of(hop, way, part, arriving):
        moved = hop if arriving else hop - 1
        slot = wrap(at + (-moved if way == 0 else moved), count)
        spot = store.at[slot, pl.ds(part * half_rows, half_rows)]
        index = (hop - 1, way, part)
        return remote(spot, spot, send.at[index], recv.at[index], devices[way])

    messages = [
        (hop, way, part)
        for hop in range(1, last + 1)
        for part in (0, 1)
        for way in (0, 1)
        if hop < last or part == way
    ]
    for hop, way, part in messages:
        if hop > 1:
            copy_of(hop - 1, way, part, True).wait_recv()
        copy_of(hop, way, part, False).start()
        yield
    for hop, way, part in messages:
        if (hop + 1, way, part) not in messages:
            copy_of(hop, way, part, True).wait_recv()
    yield
    for hop, way, part in messages:
        copy_of(hop, way, part, False).wait_send()


def ring_sum(parts, out, arrived, leaving, at, count, devices, send, recv):
    half_rows = parts.shape[1] // 2
    last = count // 2

    def rows(part):
        return pl.ds(part * half_rows, half_rows)

    def copy_of(hop, way, part):
        index = (hop - 1, way, part)
        if hop == 1:
            source = parts.at[wrap(at + last, count), rows(part)]
        else:
            source = leaving.at[hop - 2, way, rows(part)]
        target = arrived.at[hop - 1, way, rows(part)]
        return remote(source, target, send.at[index], recv.at[index], devices[way])

    def summed(hop, way, part):
        slot = wrap(at + (last + 1 - hop if way == 0 else hop - 1 - last), count)
        value = parts[slot, rows(part)].astype(jnp.float32)
        if hop > 2 or part == way:
            copy_of(hop - 1, way, part).wait_recv()
            value += arrived[hop - 2, way, rows(part)].astype(jnp.float32)
        return value

    messages = [(1, way, way) for way in (0, 1)] + [
        (hop, way, part) for hop in range(2, last + 1) for part in (0, 1) for way in (0, 1)
    ]
    for hop, way, part in messages:
        if hop > 1:
            leaving[hop - 2, way, rows(part)] = summed(hop, way, part).astype(jnp.bfloat16)
        copy_of(hop, way, part).start()
        yield
    for part in (0, 1):
        value = parts[at, rows(part)].astype(jnp.float32)
        for way in (0, 1):
            copy_of(last, way, part).wait_recv()
            value += arrived[last - 1, way, rows(part)].astype(jnp.float32)
        out[rows(part)] = value.astype(jnp.bfloat16)
    yield
    for message in messages:
        copy_of(*message).wait_send()


def sum_over_mp(partial, out_ref, mine, gift, theirs, chip_sum, tiles, done, pair_send, pair_recv, z_send, z_recv, swap_send, swap_recv):
    chip, core, _, _, chips, _ = places()
    sibling = {"mp": 2 * chip + 1 - core}
    half = mine.shape[1]

    def give(step):
        return remote(gift.at[step], theirs.at[step], pair_send.at[step], pair_recv.at[step], sibling)

    def post(step):
        target = {"mp": 2 * lax.rem(chip + step, chips) + core}
        return remote(chip_sum.at[step], tiles.at[step], z_send.at[step - 1], z_recv.at[step - 1], target)

    order = sorted(range(1, chips), key=lambda step: -min(step, chips - step)) + [0]
    for step in order:
        tile = lax.rem(chip + step, chips)
        gift[step] = partial(tile, 1 - core).astype(jnp.bfloat16)
        give(step).start()
        mine[step] = partial(tile, core)
        yield
    for step in order:
        give(step).wait_recv()
        mine[step] += theirs[step].astype(jnp.float32)
        if step:
            chip_sum[step] = mine[step].astype(jnp.bfloat16)
            post(step).start()
        yield
    total = mine[0]
    for step in reversed(order[:-1]):
        post(step).wait_recv()
        total += tiles[step].astype(jnp.float32)
    done[...] = jnp.transpose(total).astype(jnp.bfloat16)
    columns = pl.ds(pl.multiple_of(core * half, half), half)
    other_columns = pl.ds(pl.multiple_of((1 - core) * half, half), half)
    own_rows = pl.ds(pl.multiple_of(core * HEAD, HEAD), HEAD)
    swap = remote(
        done.at[pl.ds(pl.multiple_of((1 - core) * HEAD, HEAD), HEAD)],
        out_ref.at[:, columns],
        swap_send,
        swap_recv,
        sibling,
    )
    swap.start()
    out_ref[:, columns] = done[own_rows]
    yield
    remote(done.at[own_rows], out_ref.at[:, other_columns], swap_send, swap_recv, sibling).wait_recv()
    swap.wait_send()
    for step in order:
        give(step).wait_send()
        if step:
            post(step).wait_send()


def sum_scratch(rows):
    chips = lax.axis_size("mp") // 2
    half = rows // 2
    dma = pltpu.SemaphoreType.DMA
    some = pltpu.VMEM((chips, half, PAIR), jnp.bfloat16)
    return [
        pltpu.VMEM((chips, half, PAIR), jnp.float32),
        some,
        some,
        some,
        some,
        pltpu.VMEM((PAIR, half), jnp.bfloat16),
        dma((chips,)),
        dma((chips,)),
        dma((chips - 1,)),
        dma((chips - 1,)),
        dma,
        dma,
    ]


def mp_partners(chip, core, chips):
    return [{"mp": 2 * chip + 1 - core}] + [
        {"mp": 2 * lax.rem(chip + step, chips) + core} for step in range(1, chips)
    ]


def seq_partners(at_y, at_x, count_y):
    along_x = [{"seq": at_y * RING_X + lax.rem(at_x + step, RING_X)} for step in range(1, RING_X)]
    along_y = [{"seq": lax.rem(at_y + step, count_y) * RING_X + at_x} for step in range(1, count_y)]
    return along_x, along_y


def half_rows_of(ref, half):
    rows = ref.shape[0] // 2
    return ref[pl.ds(pl.multiple_of(half * rows, rows), rows)]


def project_kernel(
    frames_ref,
    grad_ref,
    key_w,
    value_w,
    query_w,
    out_w,
    features,
    kv_ref,
    qg_ref,
    weights,
    mine,
    other,
    loaded,
    filled,
    pair_send,
    pair_recv,
    z_send,
    z_recv,
    share_send,
    share_recv,
    y_send,
    y_recv,
    x_send,
    x_recv,
):
    chip, core, at_y, at_x, chips, count_y = places()
    hops = chips // 2
    rows = features.shape[0]
    half, width = rows // 2, chips * PAIR
    sibling = {"mp": 2 * chip + 1 - core}
    right = {"mp": 2 * wrap(chip + 1, chips) + core}
    left = {"mp": 2 * wrap(chip - 1, chips) + core}
    inputs = stack_rows((frames_ref, grad_ref), mine, loaded)
    fill = stack_rows((key_w, value_w, query_w, out_w), weights, filled)
    for copy in inputs + fill:
        copy.start()
    greet([sibling, right, left] + list(neighbours(at_y, at_x, count_y).values()))
    for copy in inputs:
        copy.wait()

    def side(whose):
        return pl.ds(pl.multiple_of(whose * half, half), half)

    swap = remote(mine.at[:, side(1 - core)], other, pair_send, pair_recv, sibling)
    swap.start()
    swap.wait_recv()
    here, there = mine[:, side(core)].astype(jnp.float32), other[...].astype(jnp.float32)
    even = jnp.where(core == 0, here, there)
    odd = jnp.where(core == 0, there, here)
    for kind in (0, 1):
        part = slice(kind * HEAD, (kind + 1) * HEAD)
        tile = jnp.transpose(jnp.concatenate([even[part], odd[part]], axis=0))
        column = pl.multiple_of(kind * width + chip * PAIR, PAIR)
        features[side(core), pl.ds(column, PAIR)] = tile.astype(jnp.bfloat16)

    def place(kind, tile, way, hop):
        start = pl.multiple_of(kind * width + wrap(tile, chips) * PAIR, PAIR)
        count = half if hop < hops else half // 2
        first = core * half + (0 if hop < hops else way * count)
        return features.at[pl.ds(pl.multiple_of(first, count), count), pl.ds(start, PAIR)]

    def along_z(kind, way, hop, moved):
        spot = place(kind, chip + (-moved if way == 0 else moved), way, hop)
        at = (kind, way, hop - 1)
        return remote(spot, spot, z_send.at[at], z_recv.at[at], right if way == 0 else left)

    def sent(kind, way, hop):
        return along_z(kind, way, hop, hop - 1)

    def landed(kind, way, hop):
        return along_z(kind, way, hop, hop)

    def shared(kind, whose):
        spot = features.at[side(whose), pl.ds(kind * width, width)]
        return remote(spot, spot, share_send.at[kind], share_recv.at[kind], sibling)

    def advance(kind, hop):
        for way in (0, 1):
            landed(kind, way, hop).wait_recv()
            if hop < hops:
                sent(kind, way, hop + 1).start()
        if hop == hops:
            shared(kind, core).start()

    def begin(kind):
        for way in (0, 1):
            sent(kind, way, 1).start()

    begin(0)
    for hop in range(1, hops + 1):
        advance(0, hop)
        if hop == hops - 2:
            begin(1)
        if hop > hops - 2:
            advance(1, hop - hops + 2)
    for copy in fill:
        copy.wait()
    shared(0, 1 - core).wait_recv()

    lane = lax.broadcasted_iota(jnp.int32, (BLK, PAIR), 1)
    blocks = [slice(start, start + BLK) for start in range(0, rows, BLK)]
    against = (((1,), (1,)), ((), ()))
    for block in blocks:
        product = lax.dot_general(
            features[block, :width], weights[...], against, preferred_element_type=jnp.float32
        )
        kv_ref[at_y, block] = product[:, :PAIR].astype(jnp.bfloat16)
        qg_ref[at_x, block] = product[:, PAIR:].astype(jnp.bfloat16)
    near = neighbours(at_y, at_x, count_y)
    over_y = ring_gather(kv_ref, at_y, count_y, (near["y", 1], near["y", -1]), y_send, y_recv)
    take(over_y, 4)
    for hop in range(3, hops + 1):
        advance(1, hop)
    shared(1, 1 - core).wait_recv()
    for block in blocks:
        product = lax.dot_general(
            features[block, width:], weights[PAIR:], against, preferred_element_type=jnp.float32
        )
        pair = jnp.where(lane < HEAD, qg_ref[at_x, block], product.astype(jnp.bfloat16))
        qg_ref[at_x, block] = pair
    over_x = ring_gather(qg_ref, at_x, RING_X, (near["x", 1], near["x", -1]), x_send, x_recv)
    take(over_x, 4)
    take(over_y, 4)
    take(over_x, 2)
    finish(over_y)
    finish(over_x)
    swap.wait_send()
    for kind in (0, 1):
        shared(kind, core).wait_send()
        for hop in range(1, hops + 1):
            for way in (0, 1):
                sent(kind, way, hop).wait_send()


def project(frames, cotangent, weights):
    cores, peers = lax.axis_size("mp"), lax.axis_size("seq")
    rows = frames.shape[0]
    dma = pltpu.SemaphoreType.DMA
    sems = dma((2, 2, cores // 4))
    x_sems, y_sems = dma((RING_X // 2, 2, 2)), dma((peers // RING_X // 2, 2, 2))
    return pl.pallas_call(
        project_kernel,
        out_shape=(
            jax.ShapeDtypeStruct((rows, cores * PAIR), jnp.bfloat16),
            jax.ShapeDtypeStruct((peers // RING_X, rows, PAIR), jnp.bfloat16),
            jax.ShapeDtypeStruct((RING_X, rows, PAIR), jnp.bfloat16),
        ),
        in_specs=[ANY] * 6,
        out_specs=(VMEM, VMEM, VMEM),
        scratch_shapes=[
            pltpu.VMEM((4 * HEAD, D), jnp.bfloat16),
            pltpu.VMEM((PAIR, rows), jnp.bfloat16),
            pltpu.VMEM((PAIR, rows // 2), jnp.bfloat16),
            dma((2,)),
            dma((4,)),
            dma,
            dma,
            sems,
            sems,
            dma((2,)),
            dma((2,)),
            y_sems,
            y_sems,
            x_sems,
            x_sems,
        ],
        compiler_params=pltpu.CompilerParams(
            collective_id=0, has_side_effects=True, vmem_limit_bytes=60 * 1024 * 1024
        ),
        name="project",
    )(frames.T, cotangent.T, *weights)


def list_pairs(turn_ref, own_ref, far_ref):
    _, _, at_y, at_x, _, count_y = places()
    count = jnp.int32(0)
    spread = RING_X * ROWS

    def add(count, own, far, ok):
        own_ref[count] = jnp.clip(own, 0, spread - 1)
        far_ref[count] = jnp.clip(far, 0, count_y * ROWS - 1)
        return count + ok.astype(jnp.int32)

    for block in range(ROWS):
        for offset in range(-BAND, BAND + 1):
            own = at_x * ROWS + block + offset
            count = add(count, own, at_y * ROWS + block, (own >= 0) & (own < spread))
    first, final = at_x == 0, at_x == RING_X - 1
    crosses = (first & (at_y + 1 < count_y)) | (final & (at_y > 0))
    for ahead in range(BAND):
        for back in range(BAND - ahead):
            own = jnp.where(first, spread - 1 - back, back)
            far = jnp.where(first, (at_y + 1) * ROWS + ahead, at_y * ROWS - 1 - ahead)
            count = add(count, own, far, crosses)

    def visit(index, count):
        row, column = lax.div(index, RING_X), lax.rem(index, RING_X)
        holder, partner = at_y * RING_X + column, row * RING_X + at_x
        for slot in range(turn_ref.shape[1]):
            own = turn_ref[holder, slot, partner]
            far = turn_ref[partner, slot, holder]
            ok = (own >= 0) & (jnp.abs(own - far) > BAND)
            count = add(count, own - at_y * spread, far + (row - partner) * ROWS, ok)
        return count

    count = lax.fori_loop(0, count_y * RING_X, visit, count)
    for pad in range(UNROLL):
        own_ref[count + pad] = 0
        far_ref[count + pad] = 0
    return count


def most_pairs(turns):
    return ROWS * (2 * BAND + 1) + BAND * (BAND + 1) // 2 + turns.shape[0] * turns.shape[1] + UNROLL


def forward_kernel(turn_ref, qg_ref, kv_ref, out_ref, own_list, far_list, lhs, score, top, total, mixed):
    count = list_pairs(turn_ref, own_list, far_list)
    rounds = lax.div(count + UNROLL - 1, UNROLL)
    lane = lax.broadcasted_iota(jnp.int32, (BLK, PAIR), 1)
    blocks = qg_ref.shape[0]
    zero = jnp.zeros((BLK, PAIR), jnp.bfloat16)
    for block in range(blocks):
        lhs[block] = jnp.where(lane < HEAD, qg_ref[block], zero)
    top[...] = jnp.full_like(top, LEAST)
    total[...] = jnp.zeros_like(total)
    mixed[...] = jnp.zeros_like(mixed)

    def tiles(step):
        at = [step * UNROLL + u for u in range(UNROLL)]
        return [(tile, own_list[tile], far_list[tile]) for tile in at]

    def score_step(step, carry):
        now = tiles(step)
        products = [
            lax.dot_general(
                lhs[own], kv_ref[far], (((1,), (1,)), ((), ())), preferred_element_type=jnp.float32
            )
            for _, own, far in now
        ]
        scaled = []
        for (tile, _, _), product in zip(now, products):
            masked = product * EXP2_SCALE + jnp.where(tile < count, 0.0, -jnp.inf)
            score[tile] = masked
            scaled.append(masked)
        for (_, own, _), masked in zip(now, scaled):
            top[own] = jnp.maximum(top[own], masked)
        return carry

    lax.fori_loop(0, rounds, score_step, 0)
    for block in range(blocks):
        top[block] = jnp.broadcast_to(jnp.max(top[block], axis=1, keepdims=True), (BLK, PAIR))

    def weight_step(step, carry):
        now = tiles(step)
        weights = [jnp.exp2(score[tile] - top[own]) for tile, own, _ in now]
        sums = [
            jnp.dot(weight.astype(jnp.bfloat16), kv_ref[far], preferred_element_type=jnp.float32)
            for weight, (_, _, far) in zip(weights, now)
        ]
        for (_, own, _), weight, part in zip(now, weights, sums):
            total[own] += weight
            mixed[own] += part
        return carry

    lax.fori_loop(0, rounds, weight_step, 0)
    for device in range(RING_X):
        column = jnp.zeros((BLK, PAIR), jnp.float32)
        for block in range(ROWS):
            at = device * ROWS + block
            column = jnp.where(lane == block, top[at], column)
            column = jnp.where(lane == ROWS + block, jnp.sum(total[at], axis=1, keepdims=True), column)
        for pair in range(ROWS // 2):
            even, odd = mixed[device * ROWS + 2 * pair], mixed[device * ROWS + 2 * pair + 1]
            out_ref[device, pair * BLK : (pair + 1) * BLK] = jnp.where(
                lane < HEAD, pltpu.roll(even, HEAD, 1), odd
            )
        out_ref[device, ROWS // 2 * BLK :] = jnp.transpose(column)[: 2 * ROWS]


def attend_forward(turns, qg, kv):
    most = most_pairs(turns)
    blocks = RING_X * ROWS
    square = pltpu.VMEM((blocks, BLK, PAIR), jnp.float32)
    return pl.pallas_call(
        forward_kernel,
        out_shape=jax.ShapeDtypeStruct((RING_X, ROWS // 2 * BLK + 2 * ROWS, PAIR), jnp.float32),
        in_specs=[SMEM, VMEM, VMEM],
        out_specs=VMEM,
        scratch_shapes=[
            pltpu.SMEM((most,), jnp.int32),
            pltpu.SMEM((most,), jnp.int32),
            pltpu.VMEM((blocks, BLK, PAIR), jnp.bfloat16),
            pltpu.VMEM((most, BLK, BLK), jnp.float32),
            square,
            square,
            square,
        ],
        compiler_params=pltpu.CompilerParams(vmem_limit_bytes=LIMIT),
        cost_estimate=pl.CostEstimate(
            flops=most * 4 * BLK * BLK * PAIR, bytes_accessed=kv.size * 4, transcendentals=most * BLK * BLK
        ),
        name="attend_forward",
    )(turns, qg.reshape(-1, BLK, PAIR), kv.reshape(-1, BLK, PAIR))


def backward_kernel(
    turn_ref, qg_ref, kv_ref, stats_ref, query_ref, key_ref, own_list, far_list, rhs, query, key
):
    count = list_pairs(turn_ref, own_list, far_list)
    rounds = lax.div(count + UNROLL - 1, UNROLL)
    lane = lax.broadcasted_iota(jnp.int32, (BLK, PAIR), 1)
    zero = jnp.zeros((BLK, PAIR), jnp.bfloat16)
    for block in range(qg_ref.shape[0]):
        pair = qg_ref[block]
        rhs[block, :BLK] = jnp.where(lane < HEAD, pair, zero)
        rhs[block, BLK:] = jnp.where(lane < HEAD, zero, pair)
    query[...] = jnp.zeros_like(query)
    key[...] = jnp.zeros_like(key)

    def step_of(step, carry):
        now = []
        for u in range(UNROLL):
            tile = step * UNROLL + u
            now.append((tile, own_list[tile], far_list[tile]))
        both = [
            lax.dot_general(
                kv_ref[far], rhs[own], (((1,), (1,)), ((), ())), preferred_element_type=jnp.float32
            )
            for _, own, far in now
        ]
        factors = []
        for (tile, own, _), product in zip(now, both):
            device, block = lax.div(own, ROWS), lax.rem(own, ROWS)
            top, inverse, drift = (
                stats_ref[device, pl.ds(kind * ROWS + block, 1), :] for kind in range(3)
            )
            masked = product[:, :BLK] * EXP2_SCALE + jnp.where(tile < count, 0.0, -jnp.inf)
            prob = jnp.exp2(masked - top) * inverse
            slope = prob * (product[:, BLK:] - drift)
            factors.append((slope.astype(jnp.bfloat16), prob.astype(jnp.bfloat16)))
        to_keys = [
            jnp.dot(jnp.concatenate(factor, axis=1), rhs[own], preferred_element_type=jnp.float32)
            for factor, (_, own, _) in zip(factors, now)
        ]
        to_queries = [
            lax.dot_general(
                slope, kv_ref[far], (((0,), (0,)), ((), ())), preferred_element_type=jnp.float32
            )
            for (slope, _), (_, _, far) in zip(factors, now)
        ]
        for (_, own, far), to_key, to_query in zip(now, to_keys, to_queries):
            key[far] += to_key
            query[own] += to_query
        return carry

    lax.fori_loop(0, rounds, step_of, 0)
    for block in range(key.shape[0]):
        key_ref[block] = jnp.where(lane < HEAD, key[block] * SCALE, key[block]).astype(jnp.bfloat16)
    for device in range(RING_X):
        for pair in range(ROWS // 2):
            even, odd = query[device * ROWS + 2 * pair], query[device * ROWS + 2 * pair + 1]
            query_ref[device, pair * BLK : (pair + 1) * BLK] = (
                jnp.where(lane < HEAD, even, pltpu.roll(odd, HEAD, 1)) * SCALE
            )


def attend_backward(turns, qg, kv, stats):
    most = most_pairs(turns)
    blocks, keys = RING_X * ROWS, kv.shape[0] * ROWS
    return pl.pallas_call(
        backward_kernel,
        out_shape=(
            jax.ShapeDtypeStruct((RING_X, ROWS // 2 * BLK, PAIR), jnp.float32),
            jax.ShapeDtypeStruct((keys, BLK, PAIR), jnp.bfloat16),
        ),
        in_specs=[SMEM, VMEM, VMEM, VMEM],
        out_specs=(VMEM, VMEM),
        scratch_shapes=[
            pltpu.SMEM((most,), jnp.int32),
            pltpu.SMEM((most,), jnp.int32),
            pltpu.VMEM((blocks, 2 * BLK, PAIR), jnp.bfloat16),
            pltpu.VMEM((blocks, BLK, PAIR), jnp.float32),
            pltpu.VMEM((keys, BLK, PAIR), jnp.float32),
        ],
        compiler_params=pltpu.CompilerParams(vmem_limit_bytes=LIMIT),
        cost_estimate=pl.CostEstimate(
            flops=most * 10 * BLK * BLK * PAIR, bytes_accessed=kv.size * 4, transcendentals=most * BLK * BLK
        ),
        name="attend_backward",
    )(turns, qg.reshape(-1, BLK, PAIR), kv.reshape(-1, BLK, PAIR), stats)


def combine_kernel(parts, qg_ref, context, stats_ref, got, send, recv, s_send, s_recv):
    _, _, at_y, at_x, _, count_y = places()
    along_x, _ = seq_partners(at_y, at_x, count_y)
    greet(along_x)
    steps = range(len(along_x))

    def give(step):
        target = lax.rem(at_x + step + 1, RING_X)
        return remote(parts.at[target], got.at[step], send.at[step], recv.at[step], along_x[step])

    def tell(step, slot):
        part = stats_ref.at[slot]
        return remote(part, part, s_send.at[step], s_recv.at[step], along_x[step])

    for step in steps:
        give(step).start()
    for step in steps:
        give(step).wait_recv()
    packed = ROWS // 2 * BLK
    lane = lax.broadcasted_iota(jnp.int32, (BLK, PAIR), 1)

    def values(start, count):
        rows = slice(start, start + count)
        return [parts[at_x, rows]] + [got[step, rows] for step in steps]

    tops, totals = values(packed, ROWS), values(packed + ROWS, ROWS)
    top = functools.reduce(jnp.maximum, tops)
    factors = [jnp.exp2(part - top) for part in tops]
    inverse = 1.0 / sum(factor * part for factor, part in zip(factors, totals))
    shares = [factor * inverse for factor in factors]
    blank = jnp.zeros((BLK - ROWS * RING_X, PAIR), jnp.float32)
    columns = jnp.transpose(jnp.concatenate(shares + [blank], axis=0))
    drifts = jnp.zeros((BLK, PAIR), jnp.float32)
    for block in range(ROWS):
        output = jnp.zeros((BLK, PAIR), jnp.float32)
        for index, part in enumerate(values(block // 2 * BLK, BLK)):
            at = index * ROWS + block
            output += (part if block % 2 else pltpu.roll(part, HEAD, 1)) * columns[:, at : at + 1]
        output = jnp.where(lane < HEAD, 0.0, output)
        rows = slice(block * BLK, (block + 1) * BLK)
        context[rows] = output.astype(jnp.bfloat16)
        drift = jnp.sum(qg_ref[at_x, rows].astype(jnp.float32) * output, axis=1, keepdims=True)
        drifts = jnp.where(lane == block, drift, drifts)
    drift_rows = jnp.transpose(drifts)[: 2 * ROWS]
    stats_ref[at_x] = jnp.concatenate([top, inverse, drift_rows], axis=0)
    for step in steps:
        tell(step, at_x).start()
    for step in steps:
        tell(step, wrap(at_x - step - 1, RING_X)).wait_recv()
    for step in steps:
        give(step).wait_send()
        tell(step, at_x).wait_send()


def combine(parts, qg):
    sems = pltpu.SemaphoreType.DMA((RING_X - 1,))
    return pl.pallas_call(
        combine_kernel,
        out_shape=(
            jax.ShapeDtypeStruct((ROWS * BLK, PAIR), jnp.bfloat16),
            jax.ShapeDtypeStruct((RING_X, 4 * ROWS, PAIR), jnp.float32),
        ),
        in_specs=[VMEM, VMEM],
        out_specs=(VMEM, VMEM),
        scratch_shapes=[pltpu.VMEM((RING_X - 1,) + parts.shape[1:], jnp.float32), sems, sems, sems, sems],
        compiler_params=pltpu.CompilerParams(
            collective_id=1, has_side_effects=True, vmem_limit_bytes=LIMIT
        ),
        name="combine",
    )(parts, qg)


def sum_over_seq(parts, sums_ref, x_sum, arrived, leaving, from_y, piece, totals, sems):
    _, _, at_y, at_x, _, count_y = places()
    near = neighbours(at_y, at_x, count_y)
    around = (near["x", 1], near["x", -1])
    _, along_y = seq_partners(at_y, at_x, count_y)
    ys = range(len(along_y))

    def columns(index):
        return pl.ds(pl.multiple_of(index * PAIR, PAIR), PAIR)

    def in_y(step):
        source = x_sum.at[:, columns(lax.rem(at_y + step + 1, count_y))]
        return remote(source, from_y.at[step], sems[2].at[step], sems[3].at[step], along_y[step])

    def out_y(step, owner):
        target = totals.at[at_x, :, columns(owner)]
        return remote(piece, target, sems[4].at[step], sems[5].at[step], along_y[step])

    over_x = ring_sum(parts, x_sum, arrived, leaving, at_x, RING_X, around, sems[0], sems[1])
    take(over_x, 2)
    yield
    take(over_x, 4)
    yield
    take(over_x, 1)
    for step in ys:
        in_y(step).start()
    yield
    total = x_sum[:, columns(at_y)].astype(jnp.float32)
    for step in ys:
        in_y(step).wait_recv()
        total += from_y[step].astype(jnp.float32)
    piece[...] = total.astype(jnp.bfloat16)
    for step in ys:
        out_y(step, at_y).start()
    totals[at_x, :, columns(at_y)] = piece[...]
    yield
    for step in ys:
        out_y(step, wrap(at_y - step - 1, count_y)).wait_recv()
    back = ring_gather(totals, at_x, RING_X, around, sems[6], sems[7])
    take(back, 4)
    yield
    finish(back)
    for index in range(RING_X):
        sums_ref[index * HEAD : (index + 1) * HEAD] = totals[index].astype(jnp.float32)
    finish(over_x)
    for step in ys:
        in_y(step).wait_send()
        out_y(step, at_y).wait_send()


def gradient_kernel(
    query_parts,
    key_parts,
    context,
    features_ref,
    key_w,
    value_w,
    query_w,
    out_w,
    attended,
    grad_frames,
    sums_ref,
    features,
    weights,
    filled,
    loaded,
    joint,
    lhs,
    got,
    key_sum,
    arrived,
    leaving,
    x_send,
    x_recv,
    y_send,
    y_recv,
    products,
    x_sum,
    w_arrived,
    w_leaving,
    from_y,
    piece,
    totals,
    *refs,
):
    chip, core, at_y, at_x, chips, count_y = places()
    along_x, along_y = seq_partners(at_y, at_x, count_y)
    near = neighbours(at_y, at_x, count_y)
    fill = stack_rows((key_w, value_w, query_w, out_w), weights, filled)
    load = pltpu.make_async_copy(features_ref, features, loaded)
    for copy in fill + [load]:
        copy.start()
    greet(along_x + along_y + mp_partners(chip, core, chips))
    steps = range(len(along_x))

    def give(step):
        target = lax.rem(at_x + step + 1, RING_X)
        return remote(query_parts.at[target], got.at[step], x_send.at[step], x_recv.at[step], along_x[step])

    over_y = ring_sum(
        key_parts, key_sum, arrived, leaving, at_y, count_y, (near["y", 1], near["y", -1]), y_send, y_recv
    )
    take(over_y, 4)
    for step in steps:
        give(step).start()
    for copy in fill:
        copy.wait()

    def columns(tile):
        return pl.ds(pl.multiple_of(tile * PAIR, PAIR), PAIR)

    def output_part(tile, half):
        return jnp.dot(
            half_rows_of(context, half), weights[PAIR:, columns(tile)], preferred_element_type=jnp.float32
        )

    def input_part(tile, half):
        return jnp.dot(half_rows_of(lhs, half), weights[:, columns(tile)], preferred_element_type=jnp.float32)

    half_refs = len(refs[8:]) // 2
    outputs = sum_over_mp(output_part, attended, *refs[8 : 8 + half_refs])
    inputs = sum_over_mp(input_part, grad_frames, *refs[8 + half_refs :])
    for _ in range(chips):
        take(outputs, 2)
        take(over_y, 1)
    lane = lax.broadcasted_iota(jnp.int32, (BLK, PAIR), 1)
    for step in steps:
        give(step).wait_recv()
    for pair in range(ROWS // 2):
        part = slice(pair * BLK, (pair + 1) * BLK)
        total = query_parts[at_x, part]
        for step in steps:
            total += got[step, part]
        for block, value in ((2 * pair, total), (2 * pair + 1, pltpu.roll(total, HEAD, 1))):
            rows = slice(block * BLK, (block + 1) * BLK)
            value = value.astype(jnp.bfloat16)
            joint[rows] = jnp.where(lane < HEAD, value, context[rows])
            lhs[rows, PAIR:] = jnp.where(lane < HEAD, value, jnp.zeros_like(value))
    load.wait()
    width = products.shape[2]
    along_rows = (((0,), (0,)), ((), ()))
    for index, at in ((2, 0), (3, 1)):
        product = lax.dot_general(
            joint[...],
            features[:, at * width : (at + 1) * width],
            along_rows,
            preferred_element_type=jnp.float32,
        )
        products[index] = product[at * HEAD : (at + 1) * HEAD].astype(jnp.bfloat16)
    take(over_y, 3)
    lhs[:, :PAIR] = key_sum[...]
    product = lax.dot_general(
        key_sum[...], features[:, :width], along_rows, preferred_element_type=jnp.float32
    )
    products[0] = product[:HEAD].astype(jnp.bfloat16)
    products[1] = product[HEAD:].astype(jnp.bfloat16)
    over_seq = sum_over_seq(products, sums_ref, x_sum, w_arrived, w_leaving, from_y, piece, totals, refs[:8])
    take(over_seq, 1)
    take(inputs, chips)
    take(over_seq, 1)
    take(inputs, chips)
    take(over_seq, 1)
    take(outputs, 1)
    take(over_seq, 2)
    take(inputs, 1)
    finish(over_seq)
    finish(outputs)
    finish(inputs)
    finish(over_y)
    for step in steps:
        give(step).wait_send()


def sum_gradients(query_parts, key_parts, context, features, weights):
    peers = lax.axis_size("seq")
    rows = context.shape[0]
    count_y = peers // RING_X
    dma = pltpu.SemaphoreType.DMA
    x_sems, y_sems = dma((RING_X - 1,)), dma((count_y - 1,))
    x_ring, y_ring = dma((RING_X // 2, 2, 2)), dma((count_y // 2, 2, 2))
    out = jax.ShapeDtypeStruct((HEAD, rows), jnp.bfloat16)
    stack = (RING_X, HEAD, D)

    def rounded(*shape):
        return pltpu.VMEM(shape, jnp.bfloat16)

    return pl.pallas_call(
        gradient_kernel,
        out_shape=(out, out, jax.ShapeDtypeStruct((RING_X * HEAD, D), jnp.float32)),
        in_specs=[VMEM] * 3 + [ANY] * 5,
        out_specs=(VMEM, VMEM, VMEM),
        scratch_shapes=[
            rounded(*features.shape),
            rounded(RING_X * HEAD, D),
            dma((4,)),
            dma,
            rounded(rows, PAIR),
            rounded(rows, 2 * PAIR),
            pltpu.VMEM((RING_X - 1,) + query_parts.shape[1:], jnp.float32),
            rounded(rows, PAIR),
            rounded(count_y // 2, 2, rows, PAIR),
            rounded(count_y // 2 - 1, 2, rows, PAIR),
            x_sems,
            x_sems,
            y_ring,
            y_ring,
            rounded(*stack),
            rounded(HEAD, D),
            rounded(RING_X // 2, 2, HEAD, D),
            rounded(RING_X // 2 - 1, 2, HEAD, D),
            rounded(count_y - 1, HEAD, PAIR),
            rounded(HEAD, PAIR),
            rounded(*stack),
            x_ring,
            x_ring,
            y_sems,
            y_sems,
            y_sems,
            y_sems,
            x_ring,
            x_ring,
        ]
        + sum_scratch(rows)
        + sum_scratch(rows),
        compiler_params=pltpu.CompilerParams(
            collective_id=2, has_side_effects=True, vmem_limit_bytes=LIMIT
        ),
        name="sum_gradients",
    )(query_parts, key_parts.reshape(count_y, rows, PAIR), context, features, *weights)


def on_device(frames, cotangent, query_weight, key_weight, value_weight, out_weight, turn_blocks):
    turns = jnp.transpose(turn_blocks, (0, 2, 1))
    weights = (key_weight, value_weight, query_weight, out_weight)
    features, kv, qg = project(frames, cotangent, weights)
    context, stats = combine(attend_forward(turns, qg, kv), qg)
    query_parts, key_parts = attend_backward(turns, qg, kv, stats)
    attended, grad_frames, sums = sum_gradients(query_parts, key_parts, context, features, weights)
    grad_key, grad_value, grad_query, grad_out = (
        sums[index * HEAD : (index + 1) * HEAD] for index in range(4)
    )
    return attended.T, grad_frames.T, grad_query, grad_key, grad_value, grad_out


def solution(mesh):
    return jax.shard_map(
        on_device,
        mesh=mesh,
        in_specs=(
            P("seq", "mp"),
            P("seq", "mp"),
            P("mp", None),
            P("mp", None),
            P("mp", None),
            P("mp", None),
            P(),
        ),
        out_specs=(
            P("seq", "mp"),
            P("seq", "mp"),
            P("mp", None),
            P("mp", None),
            P("mp", None),
            P("mp", None),
        ),
        check_vma=False,
    )
```

time: 182 us -> 142 us (0.78)
  the two profiles are of different devices: /device:TPU:1 before, /device:TPU:4 now
where the time goes in v3:
time: 142 us
  Pallas kernels  136 us (96%)
  local copies, waits for them, and re-layouts  5.29 us (4%)
    pallas_call x1, Pallas kernels, sum_gradients(): pl.pallas_call(gradient_kernel, out_shape=(out, out, jax.ShapeDtypeStruct...  54.8 us
    pallas_call x1, Pallas kernels, project(): pl.pallas_call(project_kernel, out_shape=(jax.ShapeDtypeStruct((rows, cor...  49.9 us
    pallas_call x1, Pallas kernels, combine(): pl.pallas_call(combine_kernel, out_shape=(jax.ShapeDtypeStruct((ROWS * BL...  15 us
    pallas_call x1, Pallas kernels, attend_forward(): pl.pallas_call(forward_kernel, out_shape=jax.ShapeDtypeStruct((RING_X, RO...  8.22 us
    pallas_call x1, Pallas kernels, attend_backward(): pl.pallas_call(backward_kernel, out_shape=(jax.ShapeDtypeStruct((RING_X,...  8.05 us
    unnamed x20, local copies, waits for them, and re-layouts  4.31 us

profile of v3, /device:TPU:4, one launch (start us, length us, event | category | flops | bytes accessed | tf_op | source)
XLA Modules:
  0.0 142.0 jit_solution(3376367342444382314)
XLA Ops:
  0.6 49.9 %project.1 = (bf16[512,2048]{1,0:T(8,128)(2,1)}, bf16[8,512,128]{2,1,0:T(8,128)(2,1)}, bf16[4,512,128]{2,1,0:T(8,128)(2,1)}) custom-call(bf16[64,512]{1,0:T(8,128)(2,1)} %bitcast.17, bf16[64,512]{1,0:T(8,128)(2,1)} %bitcast.18, bf16[64,1024]{1,0:T(8,128)(2,1)} %key_w.3, bf16[64,1024]{1,0:T(8,128)(2,1)} %value_w.3, bf16[64,1024]{1,0:T(8,128)(2,1)} %query_w.3, ...), custom_call_target="tpu_custom_call" | custom-call | tf_op jit(solution)/shard_map/project/pallas_call | solution.py:385
  50.5 0.0 copy-start.5
  50.5 1.0 copy-done.5
  51.6 0.0 copy-start.7
  51.6 1.2 copy-done.7
  52.8 0.0 copy-start.8
  52.8 0.8 copy-done.8
  53.5 0.0 copy-start.6
  53.5 8.2 %attend_forward.1.parts = f32[4,264,128]{2,1,0:T(8,128)S(1)} custom-call(s32[32,2,32]{2,1,0:T(2,128)S(1)} %bitcast.15, bf16[16,128,128]{2,1,0:T(8,128)(2,1)S(1)} %bitcast.9, bf16[32,128,128]{2,1,0:T(8,128)(2,1)S(1)} %bitcast.13), custom_call_target="tpu_custom_call" | custom-call | flops 763363328 | bytes 2097152 | tf_op jit(solution)/shard_map/attend_forward/pallas_call | solution.py:529
  61.8 0.0 copy-done.6
  61.8 15.0 %combine.1 = (bf16[512,128]{1,0:T(8,128)(2,1)S(1)}, f32[4,16,128]{2,1,0:T(8,128)S(1)}) custom-call(f32[4,264,128]{2,1,0:T(8,128)S(1)} %attend_forward.1.parts, bf16[4,512,128]{2,1,0:T(8,128)(2,1)S(1)} %copy-done.6), custom_call_target="tpu_custom_call" | custom-call | tf_op jit(solution)/shard_map/combine/pallas_call | solution.py:694
  76.8 0.0 copy-start
  76.8 0.0 copy-start.1
  76.8 0.0 copy-start.2
  76.8 0.0 copy-start.3
  76.8 0.0 copy-start.4
  76.8 8.0 %attend_backward.1 = (f32[4,256,128]{2,1,0:T(8,128)S(1)}, bf16[32,128,128]{2,1,0:T(8,128)(2,1)S(1)}) custom-call(s32[32,2,32]{2,1,0:T(2,128)S(1)} %bitcast.16, bf16[16,128,128]{2,1,0:T(8,128)(2,1)S(1)} %bitcast.10, bf16[32,128,128]{2,1,0:T(8,128)(2,1)S(1)} %bitcast.14, f32[4,16,128]{2,1,0:T(8,128)S(1)} %get-tuple-element.18.stats_ref), custom_call_target="tpu_custom_call" | custom-call | flops 1908408320 | bytes 2097152 | tf_op jit(solution)/shard_map/attend_backward/pallas_call | solution.py:615
  84.9 0.0 copy-done
  84.9 0.0 copy-done.1
  84.9 0.0 copy-done.2
  84.9 0.0 copy-done.3
  84.9 0.0 copy-done.4
  84.9 54.8 %sum_gradients.1 = (bf16[64,512]{1,0:T(8,128)(2,1)S(1)}, bf16[64,512]{1,0:T(8,128)(2,1)S(1)}, f32[256,1024]{1,0:T(8,128)S(1)}) custom-call(f32[4,256,128]{2,1,0:T(8,128)S(1)} %get-tuple-element.19.query_parts, bf16[8,512,128]{2,1,0:T(8,128)(2,1)S(1)} %bitcast.8, bf16[512,128]{1,0:T(8,128)(2,1)S(1)} %get-tuple-element.21.context, ...), custom_call_target="tpu_custom_call" | custom-call | tf_op jit(solution)/shard_map/sum_gradients/pallas_call | solution.py:896
  139.7 1.0 fusion
  140.7 0.6 copy.15
  141.3 0.6 copy.16
Async XLA Ops:
  50.5 1.0 copy-start.5
  51.6 1.2 copy-start.7
  52.8 0.8 copy-start.8
  53.5 8.2 %copy-start.6 = (bf16[4,512,128]{2,1,0:T(8,128)(2,1)S(1)}, bf16[4,512,128]{2,1,0:T(8,128)(2,1)}, u32[]{:S(2)}) copy-start(bf16[4,512,128]{2,1,0:T(8,128)(2,1)} %get-tuple-element.16.qg_ref) | copy-start | bytes 1572868
  76.8 8.1 %copy-start = (bf16[512,2048]{1,0:T(8,128)(2,1)S(1)}, bf16[512,2048]{1,0:T(8,128)(2,1)}, u32[]{:S(2)}) copy-start(bf16[512,2048]{1,0:T(8,128)(2,1)} %get-tuple-element.22.features_ref) | copy-start | bytes 6291460
  76.8 8.1 %copy-start.1 = (bf16[64,1024]{1,0:T(8,128)(2,1)S(1)}, bf16[64,1024]{1,0:T(8,128)(2,1)}, u32[]{:S(2)}) copy-start(bf16[64,1024]{1,0:T(8,128)(2,1)} %key_w.3) | copy-start | bytes 393220
  76.8 8.1 %copy-start.2 = (bf16[64,1024]{1,0:T(8,128)(2,1)S(1)}, bf16[64,1024]{1,0:T(8,128)(2,1)}, u32[]{:S(2)}) copy-start(bf16[64,1024]{1,0:T(8,128)(2,1)} %value_w.3) | copy-start | bytes 393220
  76.8 8.1 %copy-start.3 = (bf16[64,1024]{1,0:T(8,128)(2,1)S(1)}, bf16[64,1024]{1,0:T(8,128)(2,1)}, u32[]{:S(2)}) copy-start(bf16[64,1024]{1,0:T(8,128)(2,1)} %query_w.3) | copy-start | bytes 393220
  76.8 8.1 %copy-start.4 = (bf16[64,1024]{1,0:T(8,128)(2,1)S(1)}, bf16[64,1024]{1,0:T(8,128)(2,1)}, u32[]{:S(2)}) copy-start(bf16[64,1024]{1,0:T(8,128)(2,1)} %out_w.3) | copy-start | bytes 393220

commit v4 on v3

--- a/solution.py
+++ b/solution.py
@@ -17,7 +17,7 @@
 LEAST = -3e38
 HEAD = D // HEADS
 PAIR = 2 * HEAD
-UNROLL = 4
+UNROLL = 8
 SCALE = 1.0 / math.sqrt(HEAD)
 EXP2_SCALE = SCALE * math.log2(math.e)
 MESH = pl.DeviceIdType.MESH
@@ -77,24 +77,28 @@
     }
 
 
+def ring_messages(count, parts):
+    return [
+        (hop, way, part)
+        for hop in range(1, count // 2 + 1)
+        for part in range(parts)
+        for way in (0, 1)
+        if hop < count // 2 or part // (parts // 2) == way
+    ]
+
+
 def ring_gather(store, at, count, devices, send, recv):
-    half_rows = store.shape[1] // 2
-    last = count // 2
+    parts = send.shape[2]
+    part_rows = store.shape[1] // parts
 
     def copy_of(hop, way, part, arriving):
         moved = hop if arriving else hop - 1
         slot = wrap(at + (-moved if way == 0 else moved), count)
-        spot = store.at[slot, pl.ds(part * half_rows, half_rows)]
+        spot = store.at[slot, pl.ds(part * part_rows, part_rows)]
         index = (hop - 1, way, part)
         return remote(spot, spot, send.at[index], recv.at[index], devices[way])
 
-    messages = [
-        (hop, way, part)
-        for hop in range(1, last + 1)
-        for part in (0, 1)
-        for way in (0, 1)
-        if hop < last or part == way
-    ]
+    messages = ring_messages(count, parts)
     for hop, way, part in messages:
         if hop > 1:
             copy_of(hop - 1, way, part, True).wait_recv()
@@ -108,40 +112,46 @@
         copy_of(hop, way, part, False).wait_send()
 
 
-def ring_sum(parts, out, arrived, leaving, at, count, devices, send, recv):
-    half_rows = parts.shape[1] // 2
+def ring_sum(values, out, arrived, leaving, at, count, devices, send, recv):
+    parts = send.shape[2]
+    part_rows = values.shape[1] // parts
     last = count // 2
 
     def rows(part):
-        return pl.ds(part * half_rows, half_rows)
+        return pl.ds(part * part_rows, part_rows)
 
     def copy_of(hop, way, part):
         index = (hop - 1, way, part)
         if hop == 1:
-            source = parts.at[wrap(at + last, count), rows(part)]
+            source = values.at[wrap(at + last, count), rows(part)]
         else:
             source = leaving.at[hop - 2, way, rows(part)]
         target = arrived.at[hop - 1, way, rows(part)]
         return remote(source, target, send.at[index], recv.at[index], devices[way])
 
+    messages = [
+        (hop, way, part)
+        for hop in range(1, last + 1)
+        for part in range(parts)
+        for way in (0, 1)
+        if hop > 1 or part // (parts // 2) == way
+    ]
+
     def summed(hop, way, part):
         slot = wrap(at + (last + 1 - hop if way == 0 else hop - 1 - last), count)
-        value = parts[slot, rows(part)].astype(jnp.float32)
-        if hop > 2 or part == way:
+        value = values[slot, rows(part)].astype(jnp.float32)
+        if (hop - 1, way, part) in messages:
             copy_of(hop - 1, way, part).wait_recv()
             value += arrived[hop - 2, way, rows(part)].astype(jnp.float32)
         return value
 
-    messages = [(1, way, way) for way in (0, 1)] + [
-        (hop, way, part) for hop in range(2, last + 1) for part in (0, 1) for way in (0, 1)
-    ]
     for hop, way, part in messages:
         if hop > 1:
             leaving[hop - 2, way, rows(part)] = summed(hop, way, part).astype(jnp.bfloat16)
         copy_of(hop, way, part).start()
         yield
-    for part in (0, 1):
-        value = parts[at, rows(part)].astype(jnp.float32)
+    for part in range(parts):
+        value = values[at, rows(part)].astype(jnp.float32)
         for way in (0, 1):
             copy_of(last, way, part).wait_recv()
             value += arrived[last - 1, way, rows(part)].astype(jnp.float32)
@@ -297,38 +307,37 @@
         column = pl.multiple_of(kind * width + chip * PAIR, PAIR)
         features[side(core), pl.ds(column, PAIR)] = tile.astype(jnp.bfloat16)
 
-    def place(kind, tile, way, hop):
-        start = pl.multiple_of(kind * width + wrap(tile, chips) * PAIR, PAIR)
-        count = half if hop < hops else half // 2
-        first = core * half + (0 if hop < hops else way * count)
-        return features.at[pl.ds(pl.multiple_of(first, count), count), pl.ds(start, PAIR)]
-
-    def along_z(kind, way, hop, moved):
-        spot = place(kind, chip + (-moved if way == 0 else moved), way, hop)
-        at = (kind, way, hop - 1)
+    def along_z(kind, way, hop, part, moved):
+        tile = wrap(chip + (-moved if way == 0 else moved), chips)
+        start = pl.multiple_of(kind * width + tile * PAIR, PAIR)
+        first = pl.multiple_of(core * half + part * (half // 2), half // 2)
+        spot = features.at[pl.ds(first, half // 2), pl.ds(start, PAIR)]
+        at = (kind, way, hop - 1, part)
         return remote(spot, spot, z_send.at[at], z_recv.at[at], right if way == 0 else left)
 
-    def sent(kind, way, hop):
-        return along_z(kind, way, hop, hop - 1)
-
-    def landed(kind, way, hop):
-        return along_z(kind, way, hop, hop)
+    def sent(kind, way, hop, part):
+        return along_z(kind, way, hop, part, hop - 1)
+
+    def landed(kind, way, hop, part):
+        return along_z(kind, way, hop, part, hop)
 
     def shared(kind, whose):
         spot = features.at[side(whose), pl.ds(kind * width, width)]
         return remote(spot, spot, share_send.at[kind], share_recv.at[kind], sibling)
 
+    z_messages = ring_messages(chips, 2)
+
     def advance(kind, hop):
-        for way in (0, 1):
-            landed(kind, way, hop).wait_recv()
-            if hop < hops:
-                sent(kind, way, hop + 1).start()
+        for _, way, part in [message for message in z_messages if message[0] == hop]:
+            landed(kind, way, hop, part).wait_recv()
+            if (hop + 1, way, part) in z_messages:
+                sent(kind, way, hop + 1, part).start()
         if hop == hops:
             shared(kind, core).start()
 
     def begin(kind):
-        for way in (0, 1):
-            sent(kind, way, 1).start()
+        for _, way, part in [message for message in z_messages if message[0] == 1]:
+            sent(kind, way, 1, part).start()
 
     begin(0)
     for hop in range(1, hops + 1):
@@ -352,9 +361,10 @@
         qg_ref[at_x, block] = product[:, PAIR:].astype(jnp.bfloat16)
     near = neighbours(at_y, at_x, count_y)
     over_y = ring_gather(kv_ref, at_y, count_y, (near["y", 1], near["y", -1]), y_send, y_recv)
-    take(over_y, 4)
+    take(over_y, 8)
     for hop in range(3, hops + 1):
         advance(1, hop)
+        take(over_y, 4)
     shared(1, 1 - core).wait_recv()
     for block in blocks:
         product = lax.dot_general(
@@ -364,24 +374,23 @@
         qg_ref[at_x, block] = pair
     over_x = ring_gather(qg_ref, at_x, RING_X, (near["x", 1], near["x", -1]), x_send, x_recv)
     take(over_x, 4)
-    take(over_y, 4)
+    take(over_y, 6)
     take(over_x, 2)
     finish(over_y)
     finish(over_x)
     swap.wait_send()
     for kind in (0, 1):
         shared(kind, core).wait_send()
-        for hop in range(1, hops + 1):
-            for way in (0, 1):
-                sent(kind, way, hop).wait_send()
+        for hop, way, part in z_messages:
+            sent(kind, way, hop, part).wait_send()
 
 
 def project(frames, cotangent, weights):
     cores, peers = lax.axis_size("mp"), lax.axis_size("seq")
     rows = frames.shape[0]
     dma = pltpu.SemaphoreType.DMA
-    sems = dma((2, 2, cores // 4))
-    x_sems, y_sems = dma((RING_X // 2, 2, 2)), dma((peers // RING_X // 2, 2, 2))
+    sems = dma((2, 2, cores // 4, 2))
+    x_sems, y_sems = dma((RING_X // 2, 2, 2)), dma((peers // RING_X // 2, 2, 4))
     return pl.pallas_call(
         project_kernel,
         out_shape=(
@@ -707,7 +716,7 @@
     )(parts, qg)
 
 
-def sum_over_seq(parts, sums_ref, x_sum, arrived, leaving, from_y, piece, totals, sems):
+def sum_over_seq(parts, sums_refs, x_sum, arrived, leaving, from_y, piece, totals, *sems):
     _, _, at_y, at_x, _, count_y = places()
     near = neighbours(at_y, at_x, count_y)
     around = (near["x", 1], near["x", -1])
@@ -749,8 +758,11 @@
     take(back, 4)
     yield
     finish(back)
+    count = RING_X // len(sums_refs)
     for index in range(RING_X):
-        sums_ref[index * HEAD : (index + 1) * HEAD] = totals[index].astype(jnp.float32)
+        height = totals.shape[1]
+        rows = pl.ds(index % count * height, height)
+        sums_refs[index // count][rows] = totals[index].astype(jnp.float32)
     finish(over_x)
     for step in ys:
         in_y(step).wait_send()
@@ -783,13 +795,6 @@
     x_recv,
     y_send,
     y_recv,
-    products,
-    x_sum,
-    w_arrived,
-    w_leaving,
-    from_y,
-    piece,
-    totals,
     *refs,
 ):
     chip, core, at_y, at_x, chips, count_y = places()
@@ -826,53 +831,66 @@
     def input_part(tile, half):
         return jnp.dot(half_rows_of(lhs, half), weights[:, columns(tile)], preferred_element_type=jnp.float32)
 
-    half_refs = len(refs[8:]) // 2
-    outputs = sum_over_mp(output_part, attended, *refs[8 : 8 + half_refs])
-    inputs = sum_over_mp(input_part, grad_frames, *refs[8 + half_refs :])
-    for _ in range(chips):
+    seq_refs = len(seq_scratch(count_y))
+    mp_refs = (len(refs) - 2 * seq_refs) // 2
+    early, late = refs[:seq_refs], refs[seq_refs : 2 * seq_refs]
+    outputs = sum_over_mp(output_part, attended, *refs[2 * seq_refs : 2 * seq_refs + mp_refs])
+    inputs = sum_over_mp(input_part, grad_frames, *refs[2 * seq_refs + mp_refs :])
+    sums = [sums_ref.at[pl.ds(index * HEAD, HEAD)] for index in range(4)]
+    over_seq = [
+        sum_over_seq(early[0], sums[2:], *early[1:]),
+        sum_over_seq(late[0], sums[:2], *late[1:]),
+    ]
+    width = D
+    along_rows = (((0,), (0,)), ((), ()))
+
+    def store_product(target, first, values, at, lower, upper):
+        product = lax.dot_general(
+            values, features[:, at * width : (at + 1) * width], along_rows, preferred_element_type=jnp.float32
+        )
+        height = target.shape[1]
+        for index in range((upper - lower) // height):
+            start = lower + index * height
+            target[first + index] = product[start : start + height].astype(jnp.bfloat16)
+
+    lane = lax.broadcasted_iota(jnp.int32, (BLK, PAIR), 1)
+    for turn in range(chips):
         take(outputs, 2)
-        take(over_y, 1)
-    lane = lax.broadcasted_iota(jnp.int32, (BLK, PAIR), 1)
-    for step in steps:
-        give(step).wait_recv()
-    for pair in range(ROWS // 2):
-        part = slice(pair * BLK, (pair + 1) * BLK)
-        total = query_parts[at_x, part]
-        for step in steps:
-            total += got[step, part]
-        for block, value in ((2 * pair, total), (2 * pair + 1, pltpu.roll(total, HEAD, 1))):
-            rows = slice(block * BLK, (block + 1) * BLK)
-            value = value.astype(jnp.bfloat16)
-            joint[rows] = jnp.where(lane < HEAD, value, context[rows])
-            lhs[rows, PAIR:] = jnp.where(lane < HEAD, value, jnp.zeros_like(value))
-    load.wait()
-    width = products.shape[2]
-    along_rows = (((0,), (0,)), ((), ()))
-    for index, at in ((2, 0), (3, 1)):
-        product = lax.dot_general(
-            joint[...],
-            features[:, at * width : (at + 1) * width],
-            along_rows,
-            preferred_element_type=jnp.float32,
-        )
-        products[index] = product[at * HEAD : (at + 1) * HEAD].astype(jnp.bfloat16)
-    take(over_y, 3)
+        take(over_y, 3)
+        if turn == chips // 2:
+            for step in steps:
+                give(step).wait_recv()
+            for pair in range(ROWS // 2):
+                part = slice(pair * BLK, (pair + 1) * BLK)
+                total = query_parts[at_x, part]
+                for step in steps:
+                    total += got[step, part]
+                for block, value in ((2 * pair, total), (2 * pair + 1, pltpu.roll(total, HEAD, 1))):
+                    rows = slice(block * BLK, (block + 1) * BLK)
+                    value = value.astype(jnp.bfloat16)
+                    joint[rows] = jnp.where(lane < HEAD, value, context[rows])
+                    lhs[rows, PAIR:] = jnp.where(lane < HEAD, value, jnp.zeros_like(value))
+            load.wait()
+            store_product(early[0], 0, joint[...], 0, 0, HEAD)
+            store_product(early[0], RING_X // 2, joint[...], 1, HEAD, PAIR)
+            take(over_seq[0], 1)
+    take(over_seq[0], 1)
+    take(over_y, 1)
     lhs[:, :PAIR] = key_sum[...]
-    product = lax.dot_general(
-        key_sum[...], features[:, :width], along_rows, preferred_element_type=jnp.float32
-    )
-    products[0] = product[:HEAD].astype(jnp.bfloat16)
-    products[1] = product[HEAD:].astype(jnp.bfloat16)
-    over_seq = sum_over_seq(products, sums_ref, x_sum, w_arrived, w_leaving, from_y, piece, totals, refs[:8])
-    take(over_seq, 1)
+    store_product(late[0], 0, key_sum[...], 0, 0, PAIR)
+    take(over_seq[1], 1)
+    take(over_seq[0], 1)
     take(inputs, chips)
-    take(over_seq, 1)
+    take(over_seq[1], 1)
+    take(over_seq[0], 1)
     take(inputs, chips)
-    take(over_seq, 1)
+    take(over_seq[1], 1)
+    take(over_seq[0], 1)
     take(outputs, 1)
-    take(over_seq, 2)
+    take(over_seq[1], 2)
     take(inputs, 1)
-    finish(over_seq)
+    finish(over_seq[0])
+    finish(over_seq[1])
     finish(outputs)
     finish(inputs)
     finish(over_y)
@@ -880,15 +898,37 @@
         give(step).wait_send()
 
 
+def seq_scratch(count_y):
+    dma = pltpu.SemaphoreType.DMA
+    x_ring, y_sems = dma((RING_X // 2, 2, 2)), dma((count_y - 1,))
+    height = 2 * HEAD // RING_X
+    stack = pltpu.VMEM((RING_X, height, D), jnp.bfloat16)
+    return [
+        stack,
+        pltpu.VMEM((height, D), jnp.bfloat16),
+        pltpu.VMEM((RING_X // 2, 2, height, D), jnp.bfloat16),
+        pltpu.VMEM((RING_X // 2 - 1, 2, height, D), jnp.bfloat16),
+        pltpu.VMEM((count_y - 1, height, PAIR), jnp.bfloat16),
+        pltpu.VMEM((height, PAIR), jnp.bfloat16),
+        stack,
+        x_ring,
+        x_ring,
+        y_sems,
+        y_sems,
+        y_sems,
+        y_sems,
+        x_ring,
+        x_ring,
+    ]
+
+
 def sum_gradients(query_parts, key_parts, context, features, weights):
     peers = lax.axis_size("seq")
     rows = context.shape[0]
     count_y = peers // RING_X
     dma = pltpu.SemaphoreType.DMA
-    x_sems, y_sems = dma((RING_X - 1,)), dma((count_y - 1,))
-    x_ring, y_ring = dma((RING_X // 2, 2, 2)), dma((count_y // 2, 2, 2))
+    x_sems, y_ring = dma((RING_X - 1,)), dma((count_y // 2, 2, 4))
     out = jax.ShapeDtypeStruct((HEAD, rows), jnp.bfloat16)
-    stack = (RING_X, HEAD, D)
 
     def rounded(*shape):
         return pltpu.VMEM(shape, jnp.bfloat16)
@@ -913,22 +953,9 @@
             x_sems,
             y_ring,
             y_ring,
-            rounded(*stack),
-            rounded(HEAD, D),
-            rounded(RING_X // 2, 2, HEAD, D),
-            rounded(RING_X // 2 - 1, 2, HEAD, D),
-            rounded(count_y - 1, HEAD, PAIR),
-            rounded(HEAD, PAIR),
-            rounded(*stack),
-            x_ring,
-            x_ring,
-            y_sems,
-            y_sems,
-            y_sems,
-            y_sems,
-            x_ring,
-            x_ring,
         ]
+        + seq_scratch(count_y)
+        + seq_scratch(count_y)
         + sum_scratch(rows)
         + sum_scratch(rows),
         compiler_params=pltpu.CompilerParams(

time: 142 us -> 133 us (0.937)
  the two profiles are of different devices: /device:TPU:4 before, /device:TPU:2 now
where the time goes in v4:
time: 133 us
  Pallas kernels  127 us (95%)
  local copies, waits for them, and re-layouts  5.29 us (4%)
    pallas_call x1, Pallas kernels, sum_gradients(): pl.pallas_call(gradient_kernel, out_shape=(out, out, jax.ShapeDtypeStruct...  50 us
    pallas_call x1, Pallas kernels, project(): pl.pallas_call(project_kernel, out_shape=(jax.ShapeDtypeStruct((rows, cor...  49.2 us
    pallas_call x1, Pallas kernels, combine(): pl.pallas_call(combine_kernel, out_shape=(jax.ShapeDtypeStruct((ROWS * BL...  14 us
    pallas_call x1, Pallas kernels, attend_forward(): pl.pallas_call(forward_kernel, out_shape=jax.ShapeDtypeStruct((RING_X, RO...  7.22 us
    pallas_call x1, Pallas kernels, attend_backward(): pl.pallas_call(backward_kernel, out_shape=(jax.ShapeDtypeStruct((RING_X,...  6.36 us
    unnamed x20, local copies, waits for them, and re-layouts  4.31 us

profile of v4, /device:TPU:2, one launch (start us, length us, event | category | flops | bytes accessed | tf_op | source)
XLA Modules:
  0.0 132.9 jit_solution(17801279640533994550)
XLA Ops:
  0.6 49.2 %project.1 = (bf16[512,2048]{1,0:T(8,128)(2,1)}, bf16[8,512,128]{2,1,0:T(8,128)(2,1)}, bf16[4,512,128]{2,1,0:T(8,128)(2,1)}) custom-call(bf16[64,512]{1,0:T(8,128)(2,1)} %bitcast.17, bf16[64,512]{1,0:T(8,128)(2,1)} %bitcast.18, bf16[64,1024]{1,0:T(8,128)(2,1)} %key_w.3, bf16[64,1024]{1,0:T(8,128)(2,1)} %value_w.3, bf16[64,1024]{1,0:T(8,128)(2,1)} %query_w.3, ...), custom_call_target="tpu_custom_call" | custom-call | tf_op jit(solution)/shard_map/project/pallas_call | solution.py:394
  49.8 0.0 copy-start.5
  49.8 1.0 copy-done.5
  50.9 0.0 copy-start.7
  50.9 1.2 copy-done.7
  52.1 0.0 copy-start.8
  52.1 0.8 copy-done.8
  52.9 0.0 copy-start.6
  52.9 7.2 %attend_forward.1.parts = f32[4,264,128]{2,1,0:T(8,128)S(1)} custom-call(s32[32,2,32]{2,1,0:T(2,128)S(1)} %bitcast.15, bf16[16,128,128]{2,1,0:T(8,128)(2,1)S(1)} %bitcast.9, bf16[32,128,128]{2,1,0:T(8,128)(2,1)S(1)} %bitcast.13), custom_call_target="tpu_custom_call" | custom-call | flops 796917760 | bytes 2097152 | tf_op jit(solution)/shard_map/attend_forward/pallas_call | solution.py:538
  60.1 0.0 copy-done.6
  60.1 14.0 %combine.1 = (bf16[512,128]{1,0:T(8,128)(2,1)S(1)}, f32[4,16,128]{2,1,0:T(8,128)S(1)}) custom-call(f32[4,264,128]{2,1,0:T(8,128)S(1)} %attend_forward.1.parts, bf16[4,512,128]{2,1,0:T(8,128)(2,1)S(1)} %copy-done.6), custom_call_target="tpu_custom_call" | custom-call | tf_op jit(solution)/shard_map/combine/pallas_call | solution.py:703
  74.1 0.0 copy-start
  74.1 0.0 copy-start.1
  74.2 0.0 copy-start.2
  74.2 0.0 copy-start.3
  74.2 0.0 copy-start.4
  74.2 6.4 %attend_backward.1 = (f32[4,256,128]{2,1,0:T(8,128)S(1)}, bf16[32,128,128]{2,1,0:T(8,128)(2,1)S(1)}) custom-call(s32[32,2,32]{2,1,0:T(2,128)S(1)} %bitcast.16, bf16[16,128,128]{2,1,0:T(8,128)(2,1)S(1)} %bitcast.10, bf16[32,128,128]{2,1,0:T(8,128)(2,1)S(1)} %bitcast.14, f32[4,16,128]{2,1,0:T(8,128)S(1)} %get-tuple-element.18.stats_ref), custom_call_target="tpu_custom_call" | custom-call | flops 1992294400 | bytes 2097152 | tf_op jit(solution)/shard_map/attend_backward/pallas_call | solution.py:624
  80.6 0.0 copy-done
  80.6 0.0 copy-done.1
  80.6 0.0 copy-done.2
  80.6 0.0 copy-done.3
  80.6 0.0 copy-done.4
  80.6 50.0 %sum_gradients.1 = (bf16[64,512]{1,0:T(8,128)(2,1)S(1)}, bf16[64,512]{1,0:T(8,128)(2,1)S(1)}, f32[256,1024]{1,0:T(8,128)S(1)}) custom-call(f32[4,256,128]{2,1,0:T(8,128)S(1)} %get-tuple-element.19.query_parts, bf16[8,512,128]{2,1,0:T(8,128)(2,1)S(1)} %bitcast.8, bf16[512,128]{1,0:T(8,128)(2,1)S(1)} %get-tuple-element.21.context, ...), custom_call_target="tpu_custom_call" | custom-call | tf_op jit(solution)/shard_map/sum_gradients/pallas_call | solution.py:936
  130.6 1.0 fusion
  131.6 0.6 copy.15
  132.3 0.6 copy.16
Async XLA Ops:
  49.8 1.0 copy-start.5
  50.9 1.2 copy-start.7
  52.1 0.8 copy-start.8
  52.9 7.2 %copy-start.6 = (bf16[4,512,128]{2,1,0:T(8,128)(2,1)S(1)}, bf16[4,512,128]{2,1,0:T(8,128)(2,1)}, u32[]{:S(2)}) copy-start(bf16[4,512,128]{2,1,0:T(8,128)(2,1)} %get-tuple-element.16.qg_ref) | copy-start | bytes 1572868
  74.1 6.4 %copy-start = (bf16[512,2048]{1,0:T(8,128)(2,1)S(1)}, bf16[512,2048]{1,0:T(8,128)(2,1)}, u32[]{:S(2)}) copy-start(bf16[512,2048]{1,0:T(8,128)(2,1)} %get-tuple-element.22.features_ref) | copy-start | bytes 6291460
  74.1 6.4 %copy-start.1 = (bf16[64,1024]{1,0:T(8,128)(2,1)S(1)}, bf16[64,1024]{1,0:T(8,128)(2,1)}, u32[]{:S(2)}) copy-start(bf16[64,1024]{1,0:T(8,128)(2,1)} %key_w.3) | copy-start | bytes 393220
  74.2 6.4 %copy-start.2 = (bf16[64,1024]{1,0:T(8,128)(2,1)S(1)}, bf16[64,1024]{1,0:T(8,128)(2,1)}, u32[]{:S(2)}) copy-start(bf16[64,1024]{1,0:T(8,128)(2,1)} %value_w.3) | copy-start | bytes 393220
  74.2 6.4 %copy-start.3 = (bf16[64,1024]{1,0:T(8,128)(2,1)S(1)}, bf16[64,1024]{1,0:T(8,128)(2,1)}, u32[]{:S(2)}) copy-start(bf16[64,1024]{1,0:T(8,128)(2,1)} %query_w.3) | copy-start | bytes 393220
  74.2 6.4 %copy-start.4 = (bf16[64,1024]{1,0:T(8,128)(2,1)S(1)}, bf16[64,1024]{1,0:T(8,128)(2,1)}, u32[]{:S(2)}) copy-start(bf16[64,1024]{1,0:T(8,128)(2,1)} %out_w.3) | copy-start | bytes 393220

commit v5 on v4

--- a/solution.py
+++ b/solution.py
@@ -176,9 +176,10 @@
     order = sorted(range(1, chips), key=lambda step: -min(step, chips - step)) + [0]
     for step in order:
         tile = lax.rem(chip + step, chips)
-        gift[step] = partial(tile, 1 - core).astype(jnp.bfloat16)
+        product = partial(tile)
+        gift[step] = product[:half].astype(jnp.bfloat16)
         give(step).start()
-        mine[step] = partial(tile, core)
+        mine[step] = product[half:]
         yield
     for step in order:
         give(step).wait_recv()
@@ -262,12 +263,8 @@
     kv_ref,
     qg_ref,
     weights,
-    mine,
-    other,
     loaded,
     filled,
-    pair_send,
-    pair_recv,
     z_send,
     z_recv,
     share_send,
@@ -279,12 +276,15 @@
 ):
     chip, core, at_y, at_x, chips, count_y = places()
     hops = chips // 2
-    rows = features.shape[0]
-    half, width = rows // 2, chips * PAIR
+    rows = features.shape[-1]
+    half = rows // 2
     sibling = {"mp": 2 * chip + 1 - core}
     right = {"mp": 2 * wrap(chip + 1, chips) + core}
     left = {"mp": 2 * wrap(chip - 1, chips) + core}
-    inputs = stack_rows((frames_ref, grad_ref), mine, loaded)
+    inputs = [
+        pltpu.make_async_copy(ref, features.at[kind, chip, core], loaded.at[kind])
+        for kind, ref in enumerate((frames_ref, grad_ref))
+    ]
     fill = stack_rows((key_w, value_w, query_w, out_w), weights, filled)
     for copy in inputs + fill:
         copy.start()
@@ -292,26 +292,9 @@
     for copy in inputs:
         copy.wait()
 
-    def side(whose):
-        return pl.ds(pl.multiple_of(whose * half, half), half)
-
-    swap = remote(mine.at[:, side(1 - core)], other, pair_send, pair_recv, sibling)
-    swap.start()
-    swap.wait_recv()
-    here, there = mine[:, side(core)].astype(jnp.float32), other[...].astype(jnp.float32)
-    even = jnp.where(core == 0, here, there)
-    odd = jnp.where(core == 0, there, here)
-    for kind in (0, 1):
-        part = slice(kind * HEAD, (kind + 1) * HEAD)
-        tile = jnp.transpose(jnp.concatenate([even[part], odd[part]], axis=0))
-        column = pl.multiple_of(kind * width + chip * PAIR, PAIR)
-        features[side(core), pl.ds(column, PAIR)] = tile.astype(jnp.bfloat16)
-
     def along_z(kind, way, hop, part, moved):
         tile = wrap(chip + (-moved if way == 0 else moved), chips)
-        start = pl.multiple_of(kind * width + tile * PAIR, PAIR)
-        first = pl.multiple_of(core * half + part * (half // 2), half // 2)
-        spot = features.at[pl.ds(first, half // 2), pl.ds(start, PAIR)]
+        spot = features.at[kind, tile, core, :, pl.ds(part * half, half)]
         at = (kind, way, hop - 1, part)
         return remote(spot, spot, z_send.at[at], z_recv.at[at], right if way == 0 else left)
 
@@ -322,7 +305,7 @@
         return along_z(kind, way, hop, part, hop)
 
     def shared(kind, whose):
-        spot = features.at[side(whose), pl.ds(kind * width, width)]
+        spot = features.at[kind, :, whose]
         return remote(spot, spot, share_send.at[kind], share_recv.at[kind], sibling)
 
     z_messages = ring_messages(chips, 2)
@@ -350,15 +333,14 @@
         copy.wait()
     shared(0, 1 - core).wait_recv()
 
-    lane = lax.broadcasted_iota(jnp.int32, (BLK, PAIR), 1)
-    blocks = [slice(start, start + BLK) for start in range(0, rows, BLK)]
-    against = (((1,), (1,)), ((), ()))
-    for block in blocks:
-        product = lax.dot_general(
-            features[block, :width], weights[...], against, preferred_element_type=jnp.float32
-        )
-        kv_ref[at_y, block] = product[:, :PAIR].astype(jnp.bfloat16)
-        qg_ref[at_x, block] = product[:, PAIR:].astype(jnp.bfloat16)
+    def products(rows_of_weights, kind):
+        whole = features[kind].reshape(chips * PAIR, rows)
+        product = jnp.dot(weights[rows_of_weights], whole, preferred_element_type=jnp.float32)
+        return jnp.transpose(product).astype(jnp.bfloat16)
+
+    joined = products(slice(None), 0)
+    kv_ref[at_y] = joined[:, :PAIR]
+    queries = joined[:, PAIR:]
     near = neighbours(at_y, at_x, count_y)
     over_y = ring_gather(kv_ref, at_y, count_y, (near["y", 1], near["y", -1]), y_send, y_recv)
     take(over_y, 8)
@@ -366,19 +348,14 @@
         advance(1, hop)
         take(over_y, 4)
     shared(1, 1 - core).wait_recv()
-    for block in blocks:
-        product = lax.dot_general(
-            features[block, width:], weights[PAIR:], against, preferred_element_type=jnp.float32
-        )
-        pair = jnp.where(lane < HEAD, qg_ref[at_x, block], product.astype(jnp.bfloat16))
-        qg_ref[at_x, block] = pair
+    lane = lax.broadcasted_iota(jnp.int32, queries.shape, 1)
+    qg_ref[at_x] = jnp.where(lane < HEAD, queries, products(slice(PAIR, None), 1))
     over_x = ring_gather(qg_ref, at_x, RING_X, (near["x", 1], near["x", -1]), x_send, x_recv)
     take(over_x, 4)
     take(over_y, 6)
     take(over_x, 2)
     finish(over_y)
     finish(over_x)
-    swap.wait_send()
     for kind in (0, 1):
         shared(kind, core).wait_send()
         for hop, way, part in z_messages:
@@ -394,7 +371,7 @@
     return pl.pallas_call(
         project_kernel,
         out_shape=(
-            jax.ShapeDtypeStruct((rows, cores * PAIR), jnp.bfloat16),
+            jax.ShapeDtypeStruct((2, cores // 2, 2, HEAD, rows), jnp.bfloat16),
             jax.ShapeDtypeStruct((peers // RING_X, rows, PAIR), jnp.bfloat16),
             jax.ShapeDtypeStruct((RING_X, rows, PAIR), jnp.bfloat16),
         ),
@@ -402,12 +379,8 @@
         out_specs=(VMEM, VMEM, VMEM),
         scratch_shapes=[
             pltpu.VMEM((4 * HEAD, D), jnp.bfloat16),
-            pltpu.VMEM((PAIR, rows), jnp.bfloat16),
-            pltpu.VMEM((PAIR, rows // 2), jnp.bfloat16),
             dma((2,)),
             dma((4,)),
-            dma,
-            dma,
             sems,
             sems,
             dma((2,)),
@@ -467,7 +440,7 @@
     return ROWS * (2 * BAND + 1) + BAND * (BAND + 1) // 2 + turns.shape[0] * turns.shape[1] + UNROLL
 
 
-def forward_kernel(turn_ref, qg_ref, kv_ref, out_ref, own_list, far_list, lhs, score, top, total, mixed):
+def forward_kernel(turn_ref, qg_ref, kv_ref, out_ref, table_ref, own_list, far_list, lhs, score, top, total, mixed):
     count = list_pairs(turn_ref, own_list, far_list)
     rounds = lax.div(count + UNROLL - 1, UNROLL)
     lane = lax.broadcasted_iota(jnp.int32, (BLK, PAIR), 1)
@@ -527,8 +500,8 @@
             even, odd = mixed[device * ROWS + 2 * pair], mixed[device * ROWS + 2 * pair + 1]
             out_ref[device, pair * BLK : (pair + 1) * BLK] = jnp.where(
                 lane < HEAD, pltpu.roll(even, HEAD, 1), odd
-            )
-        out_ref[device, ROWS // 2 * BLK :] = jnp.transpose(column)[: 2 * ROWS]
+            ).astype(jnp.bfloat16)
+        table_ref[device] = jnp.transpose(column)[: 2 * ROWS]
 
 
 def attend_forward(turns, qg, kv):
@@ -537,9 +510,12 @@
     square = pltpu.VMEM((blocks, BLK, PAIR), jnp.float32)
     return pl.pallas_call(
         forward_kernel,
-        out_shape=jax.ShapeDtypeStruct((RING_X, ROWS // 2 * BLK + 2 * ROWS, PAIR), jnp.float32),
+        out_shape=(
+            jax.ShapeDtypeStruct((RING_X, ROWS // 2 * BLK, PAIR), jnp.bfloat16),
+            jax.ShapeDtypeStruct((RING_X, 2 * ROWS, PAIR), jnp.float32),
+        ),
         in_specs=[SMEM, VMEM, VMEM],
-        out_specs=VMEM,
+        out_specs=(VMEM, VMEM),
         scratch_shapes=[
             pltpu.SMEM((most,), jnp.int32),
             pltpu.SMEM((most,), jnp.int32),
@@ -644,7 +620,9 @@
     )(turns, qg.reshape(-1, BLK, PAIR), kv.reshape(-1, BLK, PAIR), stats)
 
 
-def combine_kernel(parts, qg_ref, context, stats_ref, got, send, recv, s_send, s_recv):
+def combine_kernel(
+    parts, tables, qg_ref, context, stats_ref, got, got_tables, send, recv, t_send, t_recv, s_send, s_recv
+):
     _, _, at_y, at_x, _, count_y = places()
     along_x, _ = seq_partners(at_y, at_x, count_y)
     greet(along_x)
@@ -654,22 +632,31 @@
         target = lax.rem(at_x + step + 1, RING_X)
         return remote(parts.at[target], got.at[step], send.at[step], recv.at[step], along_x[step])
 
+    def give_table(step):
+        target = lax.rem(at_x + step + 1, RING_X)
+        return remote(
+            tables.at[target], got_tables.at[step], t_send.at[step], t_recv.at[step], along_x[step]
+        )
+
     def tell(step, slot):
         part = stats_ref.at[slot]
         return remote(part, part, s_send.at[step], s_recv.at[step], along_x[step])
 
     for step in steps:
+        give_table(step).start()
+    for step in steps:
         give(step).start()
     for step in steps:
-        give(step).wait_recv()
-    packed = ROWS // 2 * BLK
+        give_table(step).wait_recv()
     lane = lax.broadcasted_iota(jnp.int32, (BLK, PAIR), 1)
 
-    def values(start, count):
-        rows = slice(start, start + count)
-        return [parts[at_x, rows]] + [got[step, rows] for step in steps]
-
-    tops, totals = values(packed, ROWS), values(packed + ROWS, ROWS)
+    def values(start):
+        rows = slice(start, start + BLK)
+        found = [parts[at_x, rows]] + [got[step, rows] for step in steps]
+        return [part.astype(jnp.float32) for part in found]
+
+    both = [tables[at_x]] + [got_tables[step] for step in steps]
+    tops, totals = [table[:ROWS] for table in both], [table[ROWS:] for table in both]
     top = functools.reduce(jnp.maximum, tops)
     factors = [jnp.exp2(part - top) for part in tops]
     inverse = 1.0 / sum(factor * part for factor, part in zip(factors, totals))
@@ -677,9 +664,11 @@
     blank = jnp.zeros((BLK - ROWS * RING_X, PAIR), jnp.float32)
     columns = jnp.transpose(jnp.concatenate(shares + [blank], axis=0))
     drifts = jnp.zeros((BLK, PAIR), jnp.float32)
+    for step in steps:
+        give(step).wait_recv()
     for block in range(ROWS):
         output = jnp.zeros((BLK, PAIR), jnp.float32)
-        for index, part in enumerate(values(block // 2 * BLK, BLK)):
+        for index, part in enumerate(values(block // 2 * BLK)):
             at = index * ROWS + block
             output += (part if block % 2 else pltpu.roll(part, HEAD, 1)) * columns[:, at : at + 1]
         output = jnp.where(lane < HEAD, 0.0, output)
@@ -695,10 +684,11 @@
         tell(step, wrap(at_x - step - 1, RING_X)).wait_recv()
     for step in steps:
         give(step).wait_send()
+        give_table(step).wait_send()
         tell(step, at_x).wait_send()
 
 
-def combine(parts, qg):
+def combine(parts, tables, qg):
     sems = pltpu.SemaphoreType.DMA((RING_X - 1,))
     return pl.pallas_call(
         combine_kernel,
@@ -706,14 +696,18 @@
             jax.ShapeDtypeStruct((ROWS * BLK, PAIR), jnp.bfloat16),
             jax.ShapeDtypeStruct((RING_X, 4 * ROWS, PAIR), jnp.float32),
         ),
-        in_specs=[VMEM, VMEM],
+        in_specs=[VMEM, VMEM, VMEM],
         out_specs=(VMEM, VMEM),
-        scratch_shapes=[pltpu.VMEM((RING_X - 1,) + parts.shape[1:], jnp.float32), sems, sems, sems, sems],
+        scratch_shapes=[
+            pltpu.VMEM((RING_X - 1,) + parts.shape[1:], jnp.bfloat16),
+            pltpu.VMEM((RING_X - 1,) + tables.shape[1:], jnp.float32),
+        ]
+        + [sems] * 6,
         compiler_params=pltpu.CompilerParams(
             collective_id=1, has_side_effects=True, vmem_limit_bytes=LIMIT
         ),
         name="combine",
-    )(parts, qg)
+    )(parts, tables, qg)
 
 
 def sum_over_seq(parts, sums_refs, x_sum, arrived, leaving, from_y, piece, totals, *sems):
@@ -787,6 +781,7 @@
     loaded,
     joint,
     lhs,
+    turned,
     got,
     key_sum,
     arrived,
@@ -823,14 +818,19 @@
     def columns(tile):
         return pl.ds(pl.multiple_of(tile * PAIR, PAIR), PAIR)
 
-    def output_part(tile, half):
-        return jnp.dot(
-            half_rows_of(context, half), weights[PAIR:, columns(tile)], preferred_element_type=jnp.float32
-        )
-
-    def input_part(tile, half):
-        return jnp.dot(half_rows_of(lhs, half), weights[:, columns(tile)], preferred_element_type=jnp.float32)
-
+    half = context.shape[0] // 2
+
+    def turned_rows(target, source):
+        target[:half] = half_rows_of(source, 1 - core)
+        target[half:] = half_rows_of(source, core)
+
+    def output_part(tile):
+        return jnp.dot(turned[:, :PAIR], weights[PAIR:, columns(tile)], preferred_element_type=jnp.float32)
+
+    def input_part(tile):
+        return jnp.dot(turned[...], weights[:, columns(tile)], preferred_element_type=jnp.float32)
+
+    turned_rows(turned.at[:, pl.ds(0, PAIR)], context)
     seq_refs = len(seq_scratch(count_y))
     mp_refs = (len(refs) - 2 * seq_refs) // 2
     early, late = refs[:seq_refs], refs[seq_refs : 2 * seq_refs]
@@ -842,11 +842,14 @@
         sum_over_seq(late[0], sums[:2], *late[1:]),
     ]
     width = D
-    along_rows = (((0,), (0,)), ((), ()))
 
     def store_product(target, first, values, at, lower, upper):
+        turned = jnp.transpose(values.astype(jnp.float32)).astype(jnp.bfloat16)
         product = lax.dot_general(
-            values, features[:, at * width : (at + 1) * width], along_rows, preferred_element_type=jnp.float32
+            turned,
+            features[at].reshape(width, values.shape[0]),
+            (((1,), (1,)), ((), ())),
+            preferred_element_type=jnp.float32,
         )
         height = target.shape[1]
         for index in range((upper - lower) // height):
@@ -877,6 +880,7 @@
     take(over_seq[0], 1)
     take(over_y, 1)
     lhs[:, :PAIR] = key_sum[...]
+    turned_rows(turned, lhs)
     store_product(late[0], 0, key_sum[...], 0, 0, PAIR)
     take(over_seq[1], 1)
     take(over_seq[0], 1)
@@ -945,6 +949,7 @@
             dma,
             rounded(rows, PAIR),
             rounded(rows, 2 * PAIR),
+            rounded(rows, 2 * PAIR),
             pltpu.VMEM((RING_X - 1,) + query_parts.shape[1:], jnp.float32),
             rounded(rows, PAIR),
             rounded(count_y // 2, 2, rows, PAIR),
@@ -969,7 +974,7 @@
     turns = jnp.transpose(turn_blocks, (0, 2, 1))
     weights = (key_weight, value_weight, query_weight, out_weight)
     features, kv, qg = project(frames, cotangent, weights)
-    context, stats = combine(attend_forward(turns, qg, kv), qg)
+    context, stats = combine(*attend_forward(turns, qg, kv), qg)
     query_parts, key_parts = attend_backward(turns, qg, kv, stats)
     attended, grad_frames, sums = sum_gradients(query_parts, key_parts, context, features, weights)
     grad_key, grad_value, grad_query, grad_out = (

time: 133 us -> 131 us (0.985)
  Pallas kernels: 127 us -> 124 us
    pallas_call x2, Pallas kernels: 56.4 us -> 54.4 us  [the longest x1 47.2 us: project(): pl.pallas_call(project_kernel, out_shape=(jax.ShapeDtypeStruct((2, cores...]
    pallas_call x1, Pallas kernels: 14 us -> 12 us  [combine(): pl.pallas_call(combine_kernel, out_shape=(jax.ShapeDtypeStruct((ROWS * BL...]
    pallas_call x1, Pallas kernels: 50 us -> 51.4 us  [sum_gradients(): pl.pallas_call(gradient_kernel, out_shape=(out, out, jax.ShapeDtypeStruct...]
where the time goes in v5:
time: 131 us; the launch traced here: 130 us
  Pallas kernels  124 us (95%)
  local copies, waits for them, and re-layouts  5.29 us (4%)
    pallas_call x1, Pallas kernels, sum_gradients(): pl.pallas_call(gradient_kernel, out_shape=(out, out, jax.ShapeDtypeStruct...  51.4 us
    pallas_call x1, Pallas kernels, project(): pl.pallas_call(project_kernel, out_shape=(jax.ShapeDtypeStruct((2, cores...  47.2 us
    pallas_call x1, Pallas kernels, combine(): pl.pallas_call(combine_kernel, out_shape=(jax.ShapeDtypeStruct((ROWS * BL...  12 us
    pallas_call x1, Pallas kernels, attend_forward(): pl.pallas_call(forward_kernel, out_shape=(jax.ShapeDtypeStruct((RING_X, R...  7.16 us
    pallas_call x1, Pallas kernels, attend_backward(): pl.pallas_call(backward_kernel, out_shape=(jax.ShapeDtypeStruct((RING_X,...  6.36 us
    unnamed x20, local copies, waits for them, and re-layouts  4.31 us

profile of v5, /device:TPU:2, one launch (start us, length us, event | category | flops | bytes accessed | tf_op | source)
XLA Modules:
  0.0 130.2 jit_solution(3941894413805529857)
XLA Ops:
  0.6 47.2 %project.1 = (bf16[2,8,2,64,512]{4,3,2,1,0:T(8,128)(2,1)}, bf16[8,512,128]{2,1,0:T(8,128)(2,1)}, bf16[4,512,128]{2,1,0:T(8,128)(2,1)}) custom-call(bf16[64,512]{1,0:T(8,128)(2,1)} %bitcast.17, bf16[64,512]{1,0:T(8,128)(2,1)} %bitcast.18, bf16[64,1024]{1,0:T(8,128)(2,1)} %key_w.3, bf16[64,1024]{1,0:T(8,128)(2,1)} %value_w.3, bf16[64,1024]{1,0:T(8,128)(2,1)} %query_w.3, ...), custom_call_target="tpu_custom_call" | custom-call | tf_op jit(solution)/shard_map/project/pallas_call | solution.py:371
  47.9 0.0 copy-start.5
  47.9 1.0 copy-done.5
  48.9 0.0 copy-start.6
  48.9 1.2 copy-done.6
  50.1 0.0 copy-start.8
  50.1 0.8 copy-done.8
  50.9 0.0 copy-start.7
  50.9 7.2 %attend_forward.1 = (bf16[4,256,128]{2,1,0:T(8,128)(2,1)S(1)}, f32[4,8,128]{2,1,0:T(8,128)S(1)}) custom-call(s32[32,2,32]{2,1,0:T(2,128)S(1)} %bitcast.15, bf16[16,128,128]{2,1,0:T(8,128)(2,1)S(1)} %bitcast.9, bf16[32,128,128]{2,1,0:T(8,128)(2,1)S(1)} %bitcast.13), custom_call_target="tpu_custom_call" | custom-call | flops 796917760 | bytes 2097152 | tf_op jit(solution)/shard_map/attend_forward/pallas_call | solution.py:511
  58.1 12.0 %combine.1 = (bf16[512,128]{1,0:T(8,128)(2,1)S(1)}, f32[4,16,128]{2,1,0:T(8,128)S(1)}) custom-call(bf16[4,256,128]{2,1,0:T(8,128)(2,1)S(1)} %get-tuple-element.20.parts, f32[4,8,128]{2,1,0:T(8,128)S(1)} %get-tuple-element.21.tables, bf16[4,512,128]{2,1,0:T(8,128)(2,1)S(1)} %copy-done.5), custom_call_target="tpu_custom_call" | custom-call | tf_op jit(solution)/shard_map/combine/pallas_call | solution.py:693
  70.1 0.0 copy-done.7
  70.1 0.0 copy-start
  70.1 0.0 copy-start.1
  70.1 0.0 copy-start.2
  70.1 0.0 copy-start.3
  70.1 0.0 copy-start.4
  70.2 6.4 %attend_backward.1 = (f32[4,256,128]{2,1,0:T(8,128)S(1)}, bf16[32,128,128]{2,1,0:T(8,128)(2,1)S(1)}) custom-call(s32[32,2,32]{2,1,0:T(2,128)S(1)} %bitcast.16, bf16[16,128,128]{2,1,0:T(8,128)(2,1)S(1)} %bitcast.10, bf16[32,128,128]{2,1,0:T(8,128)(2,1)S(1)} %bitcast.14, f32[4,16,128]{2,1,0:T(8,128)S(1)} %get-tuple-element.22.stats_ref), custom_call_target="tpu_custom_call" | custom-call | flops 1992294400 | bytes 2097152 | tf_op jit(solution)/shard_map/attend_backward/pallas_call | solution.py:600
  76.5 0.0 copy-done
  76.5 0.0 copy-done.1
  76.5 0.0 copy-done.2
  76.5 0.0 copy-done.3
  76.6 0.0 copy-done.4
  76.6 51.4 %sum_gradients.1 = (bf16[64,512]{1,0:T(8,128)(2,1)S(1)}, bf16[64,512]{1,0:T(8,128)(2,1)S(1)}, f32[256,1024]{1,0:T(8,128)S(1)}) custom-call(f32[4,256,128]{2,1,0:T(8,128)S(1)} %get-tuple-element.23.query_parts, bf16[8,512,128]{2,1,0:T(8,128)(2,1)S(1)} %bitcast.8, bf16[512,128]{1,0:T(8,128)(2,1)S(1)} %get-tuple-element.25.context, ...), custom_call_target="tpu_custom_call" | custom-call | tf_op jit(solution)/shard_map/sum_gradients/pallas_call | solution.py:940
  128.0 1.0 fusion
  129.0 0.6 copy.15
  129.6 0.6 copy.16
Async XLA Ops:
  47.9 1.0 copy-start.5
  48.9 1.2 copy-start.6
  50.1 0.8 copy-start.8
  50.9 19.2 %copy-start.7 = (bf16[8,512,128]{2,1,0:T(8,128)(2,1)S(1)}, bf16[8,512,128]{2,1,0:T(8,128)(2,1)}, u32[]{:S(2)}) copy-start(bf16[8,512,128]{2,1,0:T(8,128)(2,1)} %get-tuple-element.19) | copy-start | bytes 3145732
  70.1 6.4 %copy-start = (bf16[2,8,2,64,512]{4,3,2,1,0:T(8,128)(2,1)S(1)}, bf16[2,8,2,64,512]{4,3,2,1,0:T(8,128)(2,1)}, u32[]{:S(2)}) copy-start(bf16[2,8,2,64,512]{4,3,2,1,0:T(8,128)(2,1)} %get-tuple-element.26.features_ref) | copy-start | bytes 6291460
  70.1 6.4 %copy-start.1 = (bf16[64,1024]{1,0:T(8,128)(2,1)S(1)}, bf16[64,1024]{1,0:T(8,128)(2,1)}, u32[]{:S(2)}) copy-start(bf16[64,1024]{1,0:T(8,128)(2,1)} %key_w.3) | copy-start | bytes 393220
  70.1 6.4 %copy-start.2 = (bf16[64,1024]{1,0:T(8,128)(2,1)S(1)}, bf16[64,1024]{1,0:T(8,128)(2,1)}, u32[]{:S(2)}) copy-start(bf16[64,1024]{1,0:T(8,128)(2,1)} %value_w.3) | copy-start | bytes 393220
  70.1 6.4 %copy-start.3 = (bf16[64,1024]{1,0:T(8,128)(2,1)S(1)}, bf16[64,1024]{1,0:T(8,128)(2,1)}, u32[]{:S(2)}) copy-start(bf16[64,1024]{1,0:T(8,128)(2,1)} %query_w.3) | copy-start | bytes 393220
  70.1 6.4 %copy-start.4 = (bf16[64,1024]{1,0:T(8,128)(2,1)S(1)}, bf16[64,1024]{1,0:T(8,128)(2,1)}, u32[]{:S(2)}) copy-start(bf16[64,1024]{1,0:T(8,128)(2,1)} %out_w.3) | copy-start | bytes 393220

commit v6 on v5

--- a/solution.py
+++ b/solution.py
@@ -710,12 +710,18 @@
     )(parts, tables, qg)
 
 
-def sum_over_seq(parts, sums_refs, x_sum, arrived, leaving, from_y, piece, totals, *sems):
+def sum_over_seq(parts, sums_refs, x_sum, arrived, from_y, piece, totals, *sems):
     _, _, at_y, at_x, _, count_y = places()
-    near = neighbours(at_y, at_x, count_y)
-    around = (near["x", 1], near["x", -1])
-    _, along_y = seq_partners(at_y, at_x, count_y)
-    ys = range(len(along_y))
+    along_x, along_y = seq_partners(at_y, at_x, count_y)
+    xs, ys = range(len(along_x)), range(len(along_y))
+
+    def in_x(step):
+        source = parts.at[lax.rem(at_x + step + 1, RING_X)]
+        return remote(source, arrived.at[step], sems[0].at[step], sems[1].at[step], along_x[step])
+
+    def out_x(step, owner):
+        part = totals.at[owner]
+        return remote(part, part, sems[6].at[step], sems[7].at[step], along_x[step])
 
     def columns(index):
         return pl.ds(pl.multiple_of(index * PAIR, PAIR), PAIR)
@@ -728,12 +734,14 @@
         target = totals.at[at_x, :, columns(owner)]
         return remote(piece, target, sems[4].at[step], sems[5].at[step], along_y[step])
 
-    over_x = ring_sum(parts, x_sum, arrived, leaving, at_x, RING_X, around, sems[0], sems[1])
-    take(over_x, 2)
+    for step in xs:
+        in_x(step).start()
     yield
-    take(over_x, 4)
-    yield
-    take(over_x, 1)
+    total = parts[at_x].astype(jnp.float32)
+    for step in xs:
+        in_x(step).wait_recv()
+        total += arrived[step].astype(jnp.float32)
+    x_sum[...] = total.astype(jnp.bfloat16)
     for step in ys:
         in_y(step).start()
     yield
@@ -748,16 +756,19 @@
     yield
     for step in ys:
         out_y(step, wrap(at_y - step - 1, count_y)).wait_recv()
-    back = ring_gather(totals, at_x, RING_X, around, sems[6], sems[7])
-    take(back, 4)
+    for step in xs:
+        out_x(step, at_x).start()
     yield
-    finish(back)
+    for step in xs:
+        out_x(step, wrap(at_x - step - 1, RING_X)).wait_recv()
     count = RING_X // len(sums_refs)
     for index in range(RING_X):
         height = totals.shape[1]
         rows = pl.ds(index % count * height, height)
         sums_refs[index // count][rows] = totals[index].astype(jnp.float32)
-    finish(over_x)
+    for step in xs:
+        in_x(step).wait_send()
+        out_x(step, at_x).wait_send()
     for step in ys:
         in_y(step).wait_send()
         out_y(step, at_y).wait_send()
@@ -877,7 +888,6 @@
             store_product(early[0], 0, joint[...], 0, 0, HEAD)
             store_product(early[0], RING_X // 2, joint[...], 1, HEAD, PAIR)
             take(over_seq[0], 1)
-    take(over_seq[0], 1)
     take(over_y, 1)
     lhs[:, :PAIR] = key_sum[...]
     turned_rows(turned, lhs)
@@ -904,14 +914,13 @@
 
 def seq_scratch(count_y):
     dma = pltpu.SemaphoreType.DMA
-    x_ring, y_sems = dma((RING_X // 2, 2, 2)), dma((count_y - 1,))
+    x_ring, y_sems = dma((RING_X - 1,)), dma((count_y - 1,))
     height = 2 * HEAD // RING_X
     stack = pltpu.VMEM((RING_X, height, D), jnp.bfloat16)
     return [
         stack,
         pltpu.VMEM((height, D), jnp.bfloat16),
-        pltpu.VMEM((RING_X // 2, 2, height, D), jnp.bfloat16),
-        pltpu.VMEM((RING_X // 2 - 1, 2, height, D), jnp.bfloat16),
+        pltpu.VMEM((RING_X - 1, height, D), jnp.bfloat16),
         pltpu.VMEM((count_y - 1, height, PAIR), jnp.bfloat16),
         pltpu.VMEM((height, PAIR), jnp.bfloat16),
         stack,

time: 131 us -> 127 us (0.969)
  the two profiles are of different devices: /device:TPU:2 before, /device:TPU:1 now
where the time goes in v6:
time: 127 us
  Pallas kernels  121 us (95%)
  local copies, waits for them, and re-layouts  5.29 us (4%)
    pallas_call x1, Pallas kernels, project(): pl.pallas_call(project_kernel, out_shape=(jax.ShapeDtypeStruct((2, cores...  48 us
    pallas_call x1, Pallas kernels, sum_gradients(): pl.pallas_call(gradient_kernel, out_shape=(out, out, jax.ShapeDtypeStruct...  47.5 us
    pallas_call x1, Pallas kernels, combine(): pl.pallas_call(combine_kernel, out_shape=(jax.ShapeDtypeStruct((ROWS * BL...  12.8 us
    pallas_call x1, Pallas kernels, attend_forward(): pl.pallas_call(forward_kernel, out_shape=(jax.ShapeDtypeStruct((RING_X, R...  6.6 us
    pallas_call x1, Pallas kernels, attend_backward(): pl.pallas_call(backward_kernel, out_shape=(jax.ShapeDtypeStruct((RING_X,...  5.84 us
    unnamed x20, local copies, waits for them, and re-layouts  4.31 us

profile of v6, /device:TPU:1, one launch (start us, length us, event | category | flops | bytes accessed | tf_op | source)
XLA Modules:
  0.0 126.7 jit_solution(17963597335348105642)
XLA Ops:
  0.6 48.0 %project.1 = (bf16[2,8,2,64,512]{4,3,2,1,0:T(8,128)(2,1)}, bf16[8,512,128]{2,1,0:T(8,128)(2,1)}, bf16[4,512,128]{2,1,0:T(8,128)(2,1)}) custom-call(bf16[64,512]{1,0:T(8,128)(2,1)} %bitcast.17, bf16[64,512]{1,0:T(8,128)(2,1)} %bitcast.18, bf16[64,1024]{1,0:T(8,128)(2,1)} %key_w.3, bf16[64,1024]{1,0:T(8,128)(2,1)} %value_w.3, bf16[64,1024]{1,0:T(8,128)(2,1)} %query_w.3, ...), custom_call_target="tpu_custom_call" | custom-call | tf_op jit(solution)/shard_map/project/pallas_call | solution.py:371
  48.6 0.0 copy-start.5
  48.6 1.0 copy-done.5
  49.6 0.0 copy-start.6
  49.6 1.2 copy-done.6
  50.9 0.0 copy-start.8
  50.9 0.8 copy-done.8
  51.6 0.0 copy-start.7
  51.6 6.6 %attend_forward.1 = (bf16[4,256,128]{2,1,0:T(8,128)(2,1)S(1)}, f32[4,8,128]{2,1,0:T(8,128)S(1)}) custom-call(s32[32,2,32]{2,1,0:T(2,128)S(1)} %bitcast.15, bf16[16,128,128]{2,1,0:T(8,128)(2,1)S(1)} %bitcast.9, bf16[32,128,128]{2,1,0:T(8,128)(2,1)S(1)} %bitcast.13), custom_call_target="tpu_custom_call" | custom-call | flops 796917760 | bytes 2097152 | tf_op jit(solution)/shard_map/attend_forward/pallas_call | solution.py:511
  58.2 12.8 %combine.1 = (bf16[512,128]{1,0:T(8,128)(2,1)S(1)}, f32[4,16,128]{2,1,0:T(8,128)S(1)}) custom-call(bf16[4,256,128]{2,1,0:T(8,128)(2,1)S(1)} %get-tuple-element.20.parts, f32[4,8,128]{2,1,0:T(8,128)S(1)} %get-tuple-element.21.tables, bf16[4,512,128]{2,1,0:T(8,128)(2,1)S(1)} %copy-done.5), custom_call_target="tpu_custom_call" | custom-call | tf_op jit(solution)/shard_map/combine/pallas_call | solution.py:693
  71.0 0.0 copy-done.7
  71.1 0.0 copy-start
  71.1 0.0 copy-start.1
  71.1 0.0 copy-start.2
  71.1 0.0 copy-start.3
  71.1 0.0 copy-start.4
  71.1 5.8 %attend_backward.1 = (f32[4,256,128]{2,1,0:T(8,128)S(1)}, bf16[32,128,128]{2,1,0:T(8,128)(2,1)S(1)}) custom-call(s32[32,2,32]{2,1,0:T(2,128)S(1)} %bitcast.16, bf16[16,128,128]{2,1,0:T(8,128)(2,1)S(1)} %bitcast.10, bf16[32,128,128]{2,1,0:T(8,128)(2,1)S(1)} %bitcast.14, f32[4,16,128]{2,1,0:T(8,128)S(1)} %get-tuple-element.22.stats_ref), custom_call_target="tpu_custom_call" | custom-call | flops 1992294400 | bytes 2097152 | tf_op jit(solution)/shard_map/attend_backward/pallas_call | solution.py:600
  77.0 0.0 copy-done
  77.0 0.0 copy-done.1
  77.0 0.0 copy-done.2
  77.0 0.0 copy-done.3
  77.0 0.0 copy-done.4
  77.0 47.5 %sum_gradients.1 = (bf16[64,512]{1,0:T(8,128)(2,1)S(1)}, bf16[64,512]{1,0:T(8,128)(2,1)S(1)}, f32[256,1024]{1,0:T(8,128)S(1)}) custom-call(f32[4,256,128]{2,1,0:T(8,128)S(1)} %get-tuple-element.23.query_parts, bf16[8,512,128]{2,1,0:T(8,128)(2,1)S(1)} %bitcast.8, bf16[512,128]{1,0:T(8,128)(2,1)S(1)} %get-tuple-element.25.context, ...), custom_call_target="tpu_custom_call" | custom-call | tf_op jit(solution)/shard_map/sum_gradients/pallas_call | solution.py:949
  124.5 1.0 fusion
  125.5 0.6 copy.15
  126.1 0.6 copy.16
Async XLA Ops:
  48.6 1.0 copy-start.5
  49.6 1.2 copy-start.6
  50.9 0.8 copy-start.8
  51.6 19.4 %copy-start.7 = (bf16[8,512,128]{2,1,0:T(8,128)(2,1)S(1)}, bf16[8,512,128]{2,1,0:T(8,128)(2,1)}, u32[]{:S(2)}) copy-start(bf16[8,512,128]{2,1,0:T(8,128)(2,1)} %get-tuple-element.19) | copy-start | bytes 3145732
  71.1 5.9 %copy-start = (bf16[2,8,2,64,512]{4,3,2,1,0:T(8,128)(2,1)S(1)}, bf16[2,8,2,64,512]{4,3,2,1,0:T(8,128)(2,1)}, u32[]{:S(2)}) copy-start(bf16[2,8,2,64,512]{4,3,2,1,0:T(8,128)(2,1)} %get-tuple-element.26.features_ref) | copy-start | bytes 6291460
  71.1 5.9 %copy-start.1 = (bf16[64,1024]{1,0:T(8,128)(2,1)S(1)}, bf16[64,1024]{1,0:T(8,128)(2,1)}, u32[]{:S(2)}) copy-start(bf16[64,1024]{1,0:T(8,128)(2,1)} %key_w.3) | copy-start | bytes 393220
  71.1 5.9 %copy-start.2 = (bf16[64,1024]{1,0:T(8,128)(2,1)S(1)}, bf16[64,1024]{1,0:T(8,128)(2,1)}, u32[]{:S(2)}) copy-start(bf16[64,1024]{1,0:T(8,128)(2,1)} %value_w.3) | copy-start | bytes 393220
  71.1 5.9 %copy-start.3 = (bf16[64,1024]{1,0:T(8,128)(2,1)S(1)}, bf16[64,1024]{1,0:T(8,128)(2,1)}, u32[]{:S(2)}) copy-start(bf16[64,1024]{1,0:T(8,128)(2,1)} %query_w.3) | copy-start | bytes 393220
  71.1 5.9 %copy-start.4 = (bf16[64,1024]{1,0:T(8,128)(2,1)S(1)}, bf16[64,1024]{1,0:T(8,128)(2,1)}, u32[]{:S(2)}) copy-start(bf16[64,1024]{1,0:T(8,128)(2,1)} %out_w.3) | copy-start | bytes 393220
